TPU v7x, 32 devices: a whole 2x2x4 slice. The times are simulated.
32 devices in a mesh: out: 4 (over y, x), blk: 8 (over z, core).
Axes of the slice: x: 2, y: 2, z: 4, core: 2. Of those that a mesh axis runs over, the one named last changes fastest.
Arguments:
- checkpoints: bfloat16 [4, 5, 128, 1024], P('out', None, None, 'blk'), may hold values from -4 to 4
- owner: int32 [4], replicated, may hold values from 0 to 3, each once
- flux_matrix: float32 [5, 5], replicated, may hold values from -2.5 to 2.5
- row_link: int32 [8, 128], P('blk'), may hold values from 0 to 127, each once within a row
- blade_group: int32 [96], replicated, may hold values from 0 to 7
- forcing: float32 [5, 128, 1024], P(None, None, 'blk'), may hold values from -6 to 6
Outputs:
- adjoint: float32 [8, 4, 5, 128, 1024], P('out', None, None, None, 'blk')
- sensitivity: float32 [8, 4], P('out')
Inputs may be any that keep to these rules, and one draw needn't show every extreme that they name: Each tile's row_link is a permutation of its rows.
All inputs are finite; a program needn't handle non-finite values.
Results may differ from a plain program's by a relative error of at most 0.0003.
Values may be sent and summed in bfloat16 or wider, within the bound.
No kernel may reach another device: no remote copies, remote signals or barrier semaphores. Data moves between devices by JAX's collectives and lax.ppermute only.
A program may use at most 128 MiB of HBM per device.

v0:
```python
import functools
import math

import jax
import jax.numpy as jnp
import numpy as np
from jax import lax
from jax.experimental import pallas as pl
from jax.experimental.pallas import tpu as pltpu
from jax.sharding import PartitionSpec as P

FIELDS = 5
BLADES = 96
AMP = 4
GRP_DEV = 2
STEPS = 3
PAIRS = GRP_DEV * AMP

time_step = 0.25
second_diff = 0.1
fourth_diff = 0.02
link_weight = 0.5
two_pi = 2.0 * math.pi

C0 = 1.0 - time_step * (2.0 * second_diff + 6.0 * fourth_diff + link_weight)
C1 = time_step * (second_diff + 4.0 * fourth_diff)
C2 = -time_step * fourth_diff
CP = time_step * link_weight
CM = 0.5 * time_step
CU = 0.25 * time_step

FW = 6
QW = 4
PARTS = 3
SLOT = 32
QROW = PARTS * FW
LINK_ROW = QROW + STEPS * QW
QS_ROWS = 48
SEG = 16
HALF = SEG // 2

VMEM = pl.BlockSpec(memory_space=pltpu.VMEM)
SMEM = pl.BlockSpec(memory_space=pltpu.SMEM)
HBM = pl.BlockSpec(memory_space=pl.ANY)
F32 = jnp.float32
BF16 = jnp.bfloat16
NT = (((1,), (1,)), ((), ()))
TN = (((0,), (0,)), ((), ()))
NN = (((1,), (0,)), ((), ()))


def mm(a, b, dims=NN):
    return lax.dot_general(a, b, dims, preferred_element_type=F32)


def split3(x):
    hi = x.astype(BF16)
    rest = x - hi.astype(F32)
    mid = rest.astype(BF16)
    return hi, mid, (rest - mid.astype(F32)).astype(BF16)


def exact_mm(a, x):
    hi, mid, lo = split3(x)
    return mm(a, hi) + mm(a, mid) + mm(a, lo)


def q_select(width):
    out = np.zeros((FIELDS, QS_ROWS, width), np.float32)
    for f in range(FIELDS):
        for j in range(QW):
            out[f, f * 8 + j, j] = 1.0
            out[f, f * 8 + QW + j, width - QW + j] = 1.0
    return out.astype(jnp.bfloat16)


def q_edges_kernel(ck_ref, sel_ref, out_ref):
    total = None
    for f in range(FIELDS):
        part = mm(sel_ref[f], ck_ref[f], NT)
        total = part if total is None else total + part
    out_ref[...] = total.astype(BF16)


def strip_selects(width):
    forcing_sel = np.zeros((PARTS, 2 * SLOT, width), np.float32)
    for part in range(PARTS):
        for j in range(FW):
            forcing_sel[part, part * FW + j, j] = 1.0
            forcing_sel[part, SLOT + part * FW + j, width - FW + j] = 1.0
    place = np.zeros((FIELDS, 2 * SLOT, STEPS * QS_ROWS), np.float32)
    for f in range(FIELDS):
        for n in range(STEPS):
            for j in range(QW):
                place[f, QROW + n * QW + j, n * QS_ROWS + f * 8 + j] = 1.0
                place[f, SLOT + QROW + n * QW + j, n * QS_ROWS + f * 8 + QW + j] = 1.0
    return forcing_sel.astype(jnp.bfloat16), place.astype(jnp.bfloat16)


def pick(values, index):
    out = values[0]
    for k in range(1, len(values)):
        out = jnp.where(index == k, values[k], out)
    return out


def strips_kernel(n_out, *refs):
    pos, owner, *qs = refs[: 2 + n_out]
    forcing, link, fsel, place, send_a, send_b = refs[2 + n_out :]
    me = pos[0]
    even = pos[1] % 2 == 0
    edges = [q[...].astype(F32) for q in qs]
    chosen = jnp.concatenate(
        [pick(edges, (me - owner[n] + n_out) % n_out) for n in range(STEPS)], axis=0
    ).astype(BF16)
    row = lax.broadcasted_iota(jnp.int32, (2 * SLOT, link.shape[1]), 0)
    links = jnp.broadcast_to(link[...].astype(F32), row.shape)
    for f in range(FIELDS):
        both = mm(place[f], chosen)
        for sel, part in zip(range(PARTS), split3(forcing[f])):
            both = both + mm(fsel[sel], part, NT)
        if f == 0:
            both = jnp.where(row % SLOT == LINK_ROW, links, both)
        left, right = both[:SLOT], both[SLOT:]
        send_a[f * SLOT : (f + 1) * SLOT] = jnp.where(even, right, left).astype(BF16)
        send_b[f * SLOT : (f + 1) * SLOT] = jnp.where(even, left, right).astype(BF16)


def halo_select(width):
    shifts = (-2, -1, 0, 1, 2)
    out = np.zeros((4 * SLOT, 8, width), np.float32)

    def forcing_rows(column):
        if column < 0:
            source, j = 0, column + FW
        elif column < FW:
            source, j = 1, column
        elif column < width:
            source, j = 2, column - (width - FW)
        else:
            source, j = 3, column - width
        return [source * SLOT + part * FW + j for part in range(PARTS)] if 0 <= j < FW else []

    def q_row(column, n):
        if column < 0:
            source, j = 0, column + QW
        elif column < QW:
            source, j = 1, column
        elif column < width:
            source, j = 2, column - (width - QW)
        else:
            source, j = 3, column - width
        return source * SLOT + QROW + n * QW + j

    for pair in range(PAIRS):
        for p in range(SEG):
            lane = pair * SEG + p
            column = p - QW if p < HALF else width - QW + p - HALF
            for i, d in enumerate(shifts):
                for row in forcing_rows(column + d):
                    out[row, i, lane] = 1.0
            out[q_row(column, STEPS - 1), 5, lane] = 1.0
            out[q_row(column, STEPS - 2), 6, lane] = 1.0
    for lane, column in ((width - 2, -2), (width - 1, -1), (0, width), (1, width + 1)):
        for row in forcing_rows(column):
            out[row, 7, lane] = 1.0
    return out.reshape(4 * SLOT, 8 * width).astype(jnp.bfloat16)


def column_factor(columns, pair, start, total, group_base, blade_group):
    scaled = columns * BLADES
    first = ((start + total - HALF) * BLADES) // total - BLADES
    group = jnp.full(columns.shape, -1, jnp.int32)
    numerator = jnp.zeros(columns.shape, jnp.int32)
    width = columns.shape[-1]
    for j in range((width + SEG) * BLADES // total + 2):
        blade = first + j
        inside = (scaled >= blade * total) & (scaled < (blade + 1) * total)
        group = jnp.where(inside, blade_group[(blade + BLADES) % BLADES], group)
        numerator = jnp.where(inside, scaled - blade * total, numerator)
    phase = numerator.astype(F32) / total
    amp = pair & (AMP - 1)
    order = ((amp >> 1) + 1).astype(F32)
    angle = two_pi * order * phase
    harmonic = jnp.where((amp & 1) == 0, jnp.cos(angle), jnp.sin(angle))
    return jnp.where(group == group_base + pair // AMP, harmonic, 0.0)


def flux(fm, q, d):
    inner = q[0] * d[0]
    for f in range(1, FIELDS):
        inner = inner + q[f] * d[f]
    u = q[1] * CU
    out = []
    for e in range(FIELDS):
        value = u * d[e]
        for f in range(FIELDS):
            value = value + fm[f, e] * d[f]
        if e == 1:
            value = value + CU * inner
        out.append(value)
    return out


def halo_kernel(
    cycle, pos, fm, blade_group, link_s, send_a, send_b, recv_a, recv_b, forcing, link_v, sel,
    h1_ref, h2_ref, b0_ref, fe_ref, k_ref, inv_ref, fmc,
):
    width, rows = forcing.shape[2], forcing.shape[1]
    even = pos[1] % 2 == 0
    start = pos[1] * width
    total = cycle * width

    def invert(r, c):
        inv_ref[link_s[r]] = r
        return c

    lax.fori_loop(0, rows, invert, 0, unroll=8)

    for f in range(FIELDS):
        for e in range(FIELDS):
            fmc[f, e] = fm[f, e] * CM

    lane = lax.broadcasted_iota(jnp.int32, (8, width), 1)
    sub = lax.broadcasted_iota(jnp.int32, (8, width), 0)
    pair = PAIRS - 1 - lane // SEG
    p = lane & (SEG - 1)
    packed = jnp.where(p < HALF, p - QW, width - QW + p - HALF) + start
    args = (start, total, pos[0] * GRP_DEV, blade_group)
    kp = column_factor(packed + sub - 2, pair, *args)
    for i in range(5):
        k_ref[i] = column_factor(lane + start + (i - 2), sub, *args)

    sa, sb = send_a[...].astype(F32), send_b[...].astype(F32)
    ra, rb = recv_a[...].astype(F32), recv_b[...].astype(F32)
    own_left, own_right = jnp.where(even, sb, sa), jnp.where(even, sa, sb)
    left, right = jnp.where(even, rb, ra), jnp.where(even, ra, rb)
    row = lax.broadcasted_iota(jnp.int32, (rows, rows), 0).astype(F32)

    def hot(links):
        return jnp.where(links == row, 1.0, 0.0).astype(BF16)

    hot_own = hot(link_v[...].astype(F32))
    hot_left = hot(left[LINK_ROW : LINK_ROW + 1])
    hot_right = hot(right[LINK_ROW : LINK_ROW + 1])
    picked = []
    for f in range(FIELDS):
        s = slice(f * SLOT, (f + 1) * SLOT)
        g = jnp.concatenate([left[s], own_left[s], own_right[s], right[s]], axis=0)
        g = g.T.astype(BF16)
        x = mm(g, sel[...])
        picked.append([x[:, i * width : (i + 1) * width] for i in range(8)])
        fe_ref[f] = picked[f][7]
        b0_ref[f] = (C0 + 1.0) * forcing[f] + CP * exact_mm(hot_own, forcing[f])

    big_lane = lax.broadcasted_iota(jnp.int32, (rows, width), 1) & (SEG - 1)
    is_left = big_lane < HALF
    is_own = (big_lane >= QW) & (big_lane < SEG - QW)

    def permuted(x):
        outer = jnp.where(is_left, exact_mm(hot_left, x), exact_mm(hot_right, x))
        return jnp.where(is_own, exact_mm(hot_own, x), outer)

    def finish(x):
        return jnp.where(big_lane < QW, x, pltpu.roll(x, width - HALF, 1))

    shifted = [[picked[f][i] for f in range(FIELDS)] for i in range(5)]
    q2 = [picked[f][5] for f in range(FIELDS)]
    plus = flux(fmc, q2, shifted[3])
    minus = flux(fmc, q2, shifted[1])
    mu1 = []
    for f in range(FIELDS):
        b = [
            C2 * shifted[0][f],
            C1 * shifted[1][f] - minus[f],
            (C0 + 1.0) * shifted[2][f] + CP * permuted(shifted[2][f]),
            C1 * shifted[3][f] + plus[f],
            C2 * shifted[4][f],
        ]
        value = b[0] * kp[0:1]
        for i in range(1, 5):
            value = value + b[i] * kp[i : i + 1]
        mu1.append(value)
    q1 = [picked[f][6] for f in range(FIELDS)]
    m1 = [pltpu.roll(x, 1, 1) for x in mu1]
    p1 = [pltpu.roll(x, width - 1, 1) for x in mu1]
    m2 = [pltpu.roll(x, 2, 1) for x in mu1]
    p2 = [pltpu.roll(x, width - 2, 1) for x in mu1]
    part = flux(fmc, q1, [a - b for a, b in zip(m1, p1)])
    for f in range(FIELDS):
        value = C0 * mu1[f] + C1 * (m1[f] + p1[f]) + C2 * (m2[f] + p2[f])
        value = value + CP * permuted(mu1[f]) - part[f]
        value = value + shifted[2][f] * kp[2:3]
        h1_ref[f] = finish(mu1[f])
        h2_ref[f] = finish(value)


def main_kernel(n_out, cycle, *refs):
    pos, owner, fm, inv = refs[:4]
    slots = refs[4 : 4 + n_out]
    forcing, b0, fe, h1, h2, k_ref = refs[4 + n_out : 10 + n_out]
    out_hbm, sens_ref = refs[10 + n_out : 12 + n_out]
    bs, coef, mu1, mu2, stage, weighted, fmc, sem = refs[12 + n_out :]
    rows, width = forcing.shape[1], forcing.shape[2]
    me = pos[0]
    total = cycle * width

    for f in range(FIELDS):
        for e in range(FIELDS):
            fmc[f, e] = fm[f, e] * CM
    which = [(me - owner[n] + n_out) % n_out for n in range(STEPS)]
    lane = lax.broadcasted_iota(jnp.int32, (8, width), 1)
    weight = 1.0 + 2.0 * (lane + pos[1] * width).astype(F32) / total
    norm = 1.0 / math.sqrt(FIELDS * rows * total)

    def states(n, rs):
        return [pick([s[f, rs, :].astype(F32) for s in slots], which[n]) for f in range(FIELDS)]

    def around(x, edge):
        return (
            pltpu.roll(jnp.where(lane == width - 1, edge, x), 1, 1),
            pltpu.roll(jnp.where(lane == 0, edge, x), width - 1, 1),
            pltpu.roll(jnp.where(lane >= width - 2, edge, x), 2, 1),
            pltpu.roll(jnp.where(lane < 2, edge, x), width - 2, 1),
        )

    def dense(i, z):
        rs = pl.ds(pl.multiple_of(i * 16, 16), 16)
        for n in range(STEPS - 1):
            q = states(n, rs)
            u = CU * q[1]
            for e in range(FIELDS):
                coef[n, e, rs, :] = (u if e != 1 else u + u) + fmc[e, e]
            for j, f in enumerate((0, 2, 3, 4)):
                coef[n, FIELDS + j, rs, :] = CU * q[f] + fmc[f, 1]
        for half in range(2):
            r8 = pl.ds(pl.multiple_of(i * 16 + half * 8, 8), 8)
            q = [pick([s[f, rs, :].astype(F32) for s in slots], which[STEPS - 1])[half * 8 : half * 8 + 8] for f in range(FIELDS)]
            near = [around(forcing[f, r8, :], fe[f, r8, :]) for f in range(FIELDS)]
            minus = flux(fmc, q, [a[0] for a in near])
            plus = flux(fmc, q, [a[1] for a in near])
            for f in range(FIELDS):
                m1, p1, m2, p2 = near[f]
                bs[0, f, r8, :] = C2 * m2
                bs[1, f, r8, :] = C1 * m1 - minus[f]
                bs[2, f, r8, :] = C1 * p1 + plus[f]
                bs[3, f, r8, :] = C2 * p2
                w = forcing[f, r8, :] * weight
                weighted[f, r8, :] = w
                z = z + w * forcing[f, r8, :]
        return z

    zero = jnp.zeros((8, width), F32)
    z = lax.fori_loop(0, rows // 16, dense, zero)
    k = [k_ref[i] for i in range(5)]

    def spread(ref, index, r):
        return jnp.broadcast_to(ref[(*index, pl.ds(r, 1), slice(None))], (8, width))

    def first(r, acc):
        for f in range(FIELDS):
            value = spread(bs, (0, f), r) * k[0] + spread(bs, (1, f), r) * k[1]
            value = value + spread(b0, (f,), r) * k[2] + spread(bs, (2, f), r) * k[3]
            value = value + spread(bs, (3, f), r) * k[4]
            mu1[r, f] = value
            acc = acc + value * spread(weighted, (f,), r)
        return acc

    acc = lax.fori_loop(0, rows, first, zero, unroll=4)

    def step(n, source, edges, r):
        linked = inv[r]
        center = [source[r, f] for f in range(FIELDS)]
        d, base = [], []
        for f in range(FIELDS):
            seg = spread(edges, (f,), r)
            edge = pltpu.roll(seg, SEG - 4, 1, stride=SEG, stride_axis=0)
            m1, p1, m2, p2 = around(center[f], edge)
            d.append(m1 - p1)
            base.append(
                C0 * center[f] + C1 * (m1 + p1) + C2 * (m2 + p2) + CP * source[linked, f]
            )
        result = []
        for e in range(FIELDS):
            value = base[e] - spread(coef, (n, e), r) * d[e]
            for f in range(FIELDS):
                if f == e:
                    continue
                if e == 1:
                    m = spread(coef, (n, FIELDS + (0, 2, 3, 4).index(f)), r)
                else:
                    m = fmc[f, e]
                value = value - m * d[f]
            result.append(value)
        return result

    def second(r, acc):
        for f, value in enumerate(step(1, mu1, h1, r)):
            value = value + spread(forcing, (f,), r) * k[2]
            mu2[r, f] = value
            acc = acc + value * spread(weighted, (f,), r)
        return acc

    acc = lax.fori_loop(0, rows, second, acc, unroll=2)

    def third(r, acc):
        for f, value in enumerate(step(0, mu2, h2, r)):
            stage[pl.ds(f * rows + r, PAIRS, stride=FIELDS * rows), :] = value
            acc = acc + value * spread(weighted, (f,), r)
        return acc

    acc = lax.fori_loop(0, rows, third, acc, unroll=2)
    copy = pltpu.make_async_copy(stage, out_hbm, sem)
    copy.start()
    source_part = jnp.sum(z, axis=0, keepdims=True) * k[2]
    acc = (acc - 2.0 * source_part) * norm
    sens_ref[...] = jnp.broadcast_to(jnp.sum(acc, axis=1, keepdims=True), (8, width))
    copy.wait()


def shift_pairs(devices, k):
    return [(i, (i + k) % devices) for i in range(devices)]


def on_device(checkpoints, owner, flux_matrix, row_link, blade_group, forcing):
    n_out = lax.axis_size("out")
    cycle = lax.axis_size("blk")
    rows, width = forcing.shape[1], forcing.shape[2]
    pos = jnp.stack([lax.axis_index("out"), lax.axis_index("blk")]).astype(jnp.int32)
    slot = checkpoints[0]

    own_edges = pl.pallas_call(
        q_edges_kernel,
        out_shape=jax.ShapeDtypeStruct((QS_ROWS, rows), BF16),
        in_specs=[VMEM, VMEM],
        out_specs=VMEM,
        name="edges",
    )(slot, q_select(width))
    edges = [own_edges] + [
        lax.ppermute(own_edges, "out", shift_pairs(n_out, k)) for k in range(1, n_out)
    ]
    slots = [slot] + [lax.ppermute(slot, "out", shift_pairs(n_out, k)) for k in range(1, n_out)]

    fsel, place = strip_selects(width)
    strip = jax.ShapeDtypeStruct((FIELDS * SLOT, rows), BF16)


    send_a, send_b = pl.pallas_call(
        functools.partial(strips_kernel, n_out),
        out_shape=(strip, strip),
        in_specs=[SMEM, SMEM] + [VMEM] * (n_out + 4),
        out_specs=(VMEM, VMEM),
        name="strips",
    )(pos, owner, *edges, forcing, row_link, fsel, place)
    recv_a = lax.ppermute(send_a, "blk", [(i, i ^ 1) for i in range(cycle)])
    recv_b = lax.ppermute(
        send_b, "blk", [(i, (i + 1) % cycle if i % 2 else (i - 1) % cycle) for i in range(cycle)]
    )

    field = jax.ShapeDtypeStruct((FIELDS, rows, width), F32)
    h1, h2, b0, fe, k, inv = pl.pallas_call(
        functools.partial(halo_kernel, cycle),
        out_shape=(
            field,
            field,
            field,
            field,
            jax.ShapeDtypeStruct((5, PAIRS, width), F32),
            jax.ShapeDtypeStruct((rows,), jnp.int32),
        ),
        in_specs=[SMEM] * 4 + [VMEM] * 7,
        out_specs=(VMEM,) * 5 + (SMEM,),
        scratch_shapes=[pltpu.SMEM((FIELDS, FIELDS), F32)],
        compiler_params=pltpu.CompilerParams(vmem_limit_bytes=40 * 2**20),
        name="halo",
    )(
        pos, flux_matrix, blade_group, row_link[0], send_a, send_b, recv_a, recv_b,
        forcing, row_link, halo_select(width),
    )

    pairs_fields = PAIRS * FIELDS
    adjoint, sens = pl.pallas_call(
        functools.partial(main_kernel, n_out, cycle),
        out_shape=(
            jax.ShapeDtypeStruct((pairs_fields * rows, width), F32),
            jax.ShapeDtypeStruct((PAIRS, width), F32),
        ),
        in_specs=[SMEM] * 4 + [VMEM] * (n_out + 6),
        out_specs=(HBM, VMEM),
        scratch_shapes=[
            pltpu.VMEM((4, FIELDS, rows, width), F32),
            pltpu.VMEM((STEPS - 1, 2 * FIELDS - 1, rows, width), F32),
            pltpu.VMEM((rows, FIELDS, PAIRS, width), F32),
            pltpu.VMEM((rows, FIELDS, PAIRS, width), F32),
            pltpu.VMEM((pairs_fields * rows, width), F32),
            pltpu.VMEM((FIELDS, rows, width), F32),
            pltpu.SMEM((FIELDS, FIELDS), F32),
            pltpu.SemaphoreType.DMA(()),
        ],
        compiler_params=pltpu.CompilerParams(vmem_limit_bytes=50 * 2**20),
        name="steps",
    )(pos, owner, flux_matrix, inv, *slots, forcing, b0, fe, h1, h2, k)

    sens = lax.psum(sens[:, 0].reshape(GRP_DEV, AMP), "blk")
    return adjoint.reshape(GRP_DEV, AMP, FIELDS, rows, width), sens


def solution(mesh):
    return jax.shard_map(
        on_device,
        mesh=mesh,
        in_specs=(P("out", None, None, "blk"), P(), P(), P("blk", None), P(), P(None, None, "blk")),
        out_specs=(P("out", None, None, None, "blk"), P("out", None)),
        check_vma=False,
    )
```

profile of v0, /device:TPU:0, one launch (start us, length us, event | category | flops | bytes accessed | tf_op | source)
XLA Modules:
  0.0 86.4 jit_solution(4779746374857424669)
XLA Ops:
  0.6 1.8 %edges.1.refs_2_ = bf16[48,128]{1,0:T(8,128)(2,1)} custom-call(bf16[5,128,128]{2,1,0:T(8,128)(2,1)} %bitcast.5, bf16[5,48,128]{2,1,0:T(8,128)(2,1)} %constant.16.clone.sel_ref), custom_call_target="tpu_custom_call" | custom-call | tf_op jit(solution)/shard_map/edges/pallas_call | solution.py:432
  2.4 3.9 %collective-permute-start.2 = (bf16[48,128]{1,0:T(8,128)(2,1)}, bf16[48,128]{1,0:T(8,128)(2,1)S(1)}, u32[]{:S(2)}, u32[]{:S(2)}) collective-permute-start(bf16[48,128]{1,0:T(8,128)(2,1)} %edges.1.refs_2_), channel_id=1, source_target_pairs={{0,24},{8,0},{16,8},{24,16},{1,25},{9,1},{17,9},{25,17},{2,26},{10... | collective-permute-start | bytes 36872 | tf_op jit(solution)/shard_map/ppermute | solution.py:440
  6.3 0.5 collective-permute-start.7
  6.8 0.0 collective-permute-start.6
  6.8 2.0 %collective-permute-start.5 = (bf16[5,128,128]{2,1,0:T(8,128)(2,1)}, bf16[5,128,128]{2,1,0:T(8,128)(2,1)S(1)}, u32[]{:S(2)}, u32[]{:S(2)}) collective-permute-start(bf16[5,128,128]{2,1,0:T(8,128)(2,1)} %bitcast.8), channel_id=1, source_target_pairs={{0,8},{8,16},{16,24},{24,0},{1,9},{9,17},{17,25},{25,1},{2,10},{10... | collective-permute-start | bytes 491528 | tf_op jit(solution)/shard_map/ppermute | solution.py:442
  8.8 1.5 %collective-permute-start.1 = (bf16[48,128]{1,0:T(8,128)(2,1)}, bf16[48,128]{1,0:T(8,128)(2,1)S(1)}, u32[]{:S(2)}, u32[]{:S(2)}) collective-permute-start(bf16[48,128]{1,0:T(8,128)(2,1)} %edges.1.refs_2_), channel_id=1, source_target_pairs={{0,16},{8,24},{16,0},{24,8},{1,17},{9,25},{17,1},{25,9},{2,18},{10... | collective-permute-start | bytes 36872 | tf_op jit(solution)/shard_map/ppermute | solution.py:440
  10.3 0.0 collective-permute-done.2.refs_5_
  10.3 0.0 copy-start.13
  10.3 0.0 collective-permute-start
  10.4 0.7 pad_add_fusion.refs_0_.pos
  11.0 5.4 %collective-permute-done.1.refs_4_ = bf16[48,128]{1,0:T(8,128)(2,1)S(1)} collective-permute-done((bf16[48,128]{1,0:T(8,128)(2,1)}, bf16[48,128]{1,0:T(8,128)(2,1)S(1)}, u32[]{:S(2)}, u32[]{:S(2)}) %collective-permute-start.1) | collective-permute-done | bytes 12320 | tf_op jit(solution)/shard_map/ppermute | solution.py:440
  16.4 0.0 copy-start.14
  16.4 0.0 collective-permute-done.refs_3_
  16.4 0.0 copy-done.13
  16.5 0.6 copy-done.14
  17.0 0.0 copy-start.15
  17.0 0.6 copy-done.15
  17.6 2.2 %strips.1 = (bf16[160,128]{1,0:T(8,128)(2,1)}, bf16[160,128]{1,0:T(8,128)(2,1)}) custom-call(s32[2]{0:T(128)} %pad_add_fusion.refs_0_.pos, s32[4]{0:T(128)} %refs_1_.3, bf16[48,128]{1,0:T(8,128)(2,1)} %edges.1.refs_2_, bf16[48,128]{1,0:T(8,128)(2,1)} %copy-done.15, bf16[48,128]{1,0:T(8,128)(2,1)} %copy-done.14, bf16[48,128]{1,0:T(8,128)(2,1)} %copy-done.13, ...), custom_call_target="tpu_custom_call" | custom-call | tf_op jit(solution)/shard_map/strips/pallas_call | solution.py:448
  19.9 0.0 collective-permute-start.3
  19.9 3.7 %collective-permute-start.4 = (bf16[160,128]{1,0:T(8,128)(2,1)}, bf16[160,128]{1,0:T(8,128)(2,1)S(1)}, u32[]{:S(2)}, u32[]{:S(2)}) collective-permute-start(bf16[160,128]{1,0:T(8,128)(2,1)} %get-tuple-element.13.send_b), channel_id=1, source_target_pairs={{0,7},{1,2},{2,1},{3,4},{4,3},{5,6},{6,5},{7,0},{8,15},{9,10},{10,... | collective-permute-start | bytes 122888 | tf_op jit(solution)/shard_map/ppermute | solution.py:456
  23.6 0.0 collective-permute-done.3.recv_a
  23.6 2.0 %collective-permute-done.4.recv_b = bf16[160,128]{1,0:T(8,128)(2,1)S(1)} collective-permute-done((bf16[160,128]{1,0:T(8,128)(2,1)}, bf16[160,128]{1,0:T(8,128)(2,1)S(1)}, u32[]{:S(2)}, u32[]{:S(2)}) %collective-permute-start.4) | collective-permute-done | bytes 40992 | tf_op jit(solution)/shard_map/ppermute | solution.py:456
  25.6 0.0 copy-start
  25.6 1.0 %copy-done = f32[5,128,128]{2,1,0:T(8,128)S(1)} copy-done((f32[5,128,128]{2,1,0:T(8,128)S(1)}, f32[5,128,128]{2,1,0:T(8,128)}, u32[]{:S(2)}) %copy-start) | copy-done | bytes 327704
  26.6 0.0 copy-start.3
  26.6 0.9 %copy-done.3 = bf16[128,1024]{1,0:T(8,128)(2,1)S(1)} copy-done((bf16[128,1024]{1,0:T(8,128)(2,1)S(1)}, bf16[128,1024]{1,0:T(8,128)(2,1)}, u32[]{:S(2)}) %copy-start.3) | copy-done | bytes 262168
  27.5 0.0 copy-start.4
  27.5 0.8 copy-done.4
  28.3 0.0 copy-start.5
  28.3 0.8 copy-done.5
  29.1 0.7 copy-done.6
  29.8 0.7 copy-done.8
  30.4 0.7 copy-done.9
  31.1 0.7 copy-done.12
  31.8 2.7 %halo.1 = (f32[5,128,128]{2,1,0:T(8,128)S(1)}, f32[5,128,128]{2,1,0:T(8,128)S(1)}, f32[5,128,128]{2,1,0:T(8,128)S(1)}, f32[5,128,128]{2,1,0:T(8,128)S(1)}, f32[5,8,128]{2,1,0:T(8,128)S(1)}, /*index=5*/s32[128]{0:T(128)S(1)}) custom-call(s32[2]{0:T(128)S(1)} %copy-done.9, f32[5,5]{1,0:T(8,128)S(1)} %copy-done.6, s32[96]{0:T(128)S(1)} %copy-done.12, ...), custom_call_target="tpu_custom_call" | custom-call | tf_op jit(solution)/shard_map/halo/pallas_call | solution.py:461
  34.5 0.0 collective-permute-done.7.refs_7_
  34.5 0.0 collective-permute-done.6.refs_6_
  34.5 0.0 collective-permute-done.5.refs_5_
  34.5 0.0 copy-start.1
  34.6 1.0 %copy-done.1 = f32[5,128,128]{2,1,0:T(8,128)S(1)} copy-done((f32[5,128,128]{2,1,0:T(8,128)S(1)}, f32[5,128,128]{2,1,0:T(8,128)}, u32[]{:S(2)}) %copy-start.1) | copy-done | bytes 327704
  35.5 0.9 %copy-done.2 = bf16[1,5,128,128]{3,2,1,0:T(8,128)(2,1)S(1)} copy-done((bf16[1,5,128,128]{3,2,1,0:T(8,128)(2,1)S(1)}, bf16[1,5,128,128]{3,2,1,0:T(8,128)(2,1)}, u32[]{:S(2)}) %copy-start.2) | copy-done | bytes 163864
  36.4 0.7 copy-done.7
  37.1 0.7 copy-done.10
  37.8 0.7 copy-done.11
  38.5 30.1 %steps.1 = (f32[5120,128]{1,0:T(8,128)}, f32[8,128]{1,0:T(8,128)S(1)}) custom-call(s32[2]{0:T(128)S(1)} %copy-done.10, s32[4]{0:T(128)S(1)} %copy-done.11, f32[5,5]{1,0:T(8,128)S(1)} %copy-done.7, s32[128]{0:T(128)S(1)} %get-tuple-element.14.refs_3_, bf16[5,128,128]{2,1,0:T(8,128)(2,1)S(1)} %bitcast.9, ...), custom_call_target="tpu_custom_call" | custom-call | tf_op jit(solution)/shard_map/steps/pallas_call | solution.py:482
  68.6 0.1 slice_reduce_fusion
  68.7 0.1 reshape_squeeze.3
  68.8 17.6 %psum.7 = f32[2,4]{1,0:T(2,128)} all-reduce(f32[2,4]{1,0:T(2,128)S(1)} %reshape_squeeze.3), channel_id=1, replica_groups=mesh['out'=4,'blk'=8] {'blk'}, use_global_device_ids=true, to_apply=%region_0.0 | all-reduce | flops 8 | bytes 64 | tf_op jit(solution)/shard_map/psum | solution.py:504
  (8 shorter events, 0.0 us)
Async XLA Ops:
  2.4 8.0 %collective-permute-start.2 = (bf16[48,128]{1,0:T(8,128)(2,1)}, bf16[48,128]{1,0:T(8,128)(2,1)S(1)}, u32[]{:S(2)}, u32[]{:S(2)}) collective-permute-start(bf16[48,128]{1,0:T(8,128)(2,1)} %edges.1.refs_2_), channel_id=1, source_target_pairs={{0,24},{8,0},{16,8},{24,16},{1,25},{9,1},{17,9},{25,17},{2,26},{10... | collective-permute-start | bytes 36872 | tf_op jit(solution)/shard_map/ppermute | solution.py:440
  6.3 28.2 %collective-permute-start.7 = (bf16[5,128,128]{2,1,0:T(8,128)(2,1)}, bf16[5,128,128]{2,1,0:T(8,128)(2,1)S(1)}, u32[]{:S(2)}, u32[]{:S(2)}) collective-permute-start(bf16[5,128,128]{2,1,0:T(8,128)(2,1)} %bitcast.6), channel_id=1, source_target_pairs={{0,24},{8,0},{16,8},{24,16},{1,25},{9,1},{17,9},{25,17},{2,26},{10... | collective-permute-start | bytes 491528 | tf_op jit(solution)/shard_map/ppermute | solution.py:442
  6.8 27.7 %collective-permute-start.6 = (bf16[5,128,128]{2,1,0:T(8,128)(2,1)}, bf16[5,128,128]{2,1,0:T(8,128)(2,1)S(1)}, u32[]{:S(2)}, u32[]{:S(2)}) collective-permute-start(bf16[5,128,128]{2,1,0:T(8,128)(2,1)} %bitcast.7), channel_id=1, source_target_pairs={{0,16},{8,24},{16,0},{24,8},{1,17},{9,25},{17,1},{25,9},{2,18},{10... | collective-permute-start | bytes 491528 | tf_op jit(solution)/shard_map/ppermute | solution.py:442
  6.8 27.7 %collective-permute-start.5 = (bf16[5,128,128]{2,1,0:T(8,128)(2,1)}, bf16[5,128,128]{2,1,0:T(8,128)(2,1)S(1)}, u32[]{:S(2)}, u32[]{:S(2)}) collective-permute-start(bf16[5,128,128]{2,1,0:T(8,128)(2,1)} %bitcast.8), channel_id=1, source_target_pairs={{0,8},{8,16},{16,24},{24,0},{1,9},{9,17},{17,25},{25,1},{2,10},{10... | collective-permute-start | bytes 491528 | tf_op jit(solution)/shard_map/ppermute | solution.py:442
  8.8 7.6 %collective-permute-start.1 = (bf16[48,128]{1,0:T(8,128)(2,1)}, bf16[48,128]{1,0:T(8,128)(2,1)S(1)}, u32[]{:S(2)}, u32[]{:S(2)}) collective-permute-start(bf16[48,128]{1,0:T(8,128)(2,1)} %edges.1.refs_2_), channel_id=1, source_target_pairs={{0,16},{8,24},{16,0},{24,8},{1,17},{9,25},{17,1},{25,9},{2,18},{10... | collective-permute-start | bytes 36872 | tf_op jit(solution)/shard_map/ppermute | solution.py:440
  10.3 6.1 %copy-start.13 = (bf16[48,128]{1,0:T(8,128)(2,1)}, bf16[48,128]{1,0:T(8,128)(2,1)S(1)}, u32[]{:S(2)}) copy-start(bf16[48,128]{1,0:T(8,128)(2,1)S(1)} %collective-permute-done.2.refs_5_) | copy-start | bytes 36868
  10.3 6.1 %collective-permute-start = (bf16[48,128]{1,0:T(8,128)(2,1)}, bf16[48,128]{1,0:T(8,128)(2,1)S(1)}, u32[]{:S(2)}, u32[]{:S(2)}) collective-permute-start(bf16[48,128]{1,0:T(8,128)(2,1)} %edges.1.refs_2_), channel_id=1, source_target_pairs={{0,8},{8,16},{16,24},{24,0},{1,9},{9,17},{17,25},{25,1},{2,10},{10... | collective-permute-start | bytes 36872 | tf_op jit(solution)/shard_map/ppermute | solution.py:440
  16.4 0.6 copy-start.14
  17.0 0.6 copy-start.15
  19.9 3.7 %collective-permute-start.3 = (bf16[160,128]{1,0:T(8,128)(2,1)}, bf16[160,128]{1,0:T(8,128)(2,1)S(1)}, u32[]{:S(2)}, u32[]{:S(2)}) collective-permute-start(bf16[160,128]{1,0:T(8,128)(2,1)} %get-tuple-element.12.send_a), channel_id=1, source_target_pairs={{0,1},{1,0},{2,3},{3,2},{4,5},{5,4},{6,7},{7,6},{8,9},{9,8},{10,11... | collective-permute-start | bytes 122888 | tf_op jit(solution)/shard_map/ppermute | solution.py:455
  19.9 5.7 %collective-permute-start.4 = (bf16[160,128]{1,0:T(8,128)(2,1)}, bf16[160,128]{1,0:T(8,128)(2,1)S(1)}, u32[]{:S(2)}, u32[]{:S(2)}) collective-permute-start(bf16[160,128]{1,0:T(8,128)(2,1)} %get-tuple-element.13.send_b), channel_id=1, source_target_pairs={{0,7},{1,2},{2,1},{3,4},{4,3},{5,6},{6,5},{7,0},{8,15},{9,10},{10,... | collective-permute-start | bytes 122888 | tf_op jit(solution)/shard_map/ppermute | solution.py:456
  25.6 1.0 %copy-start = (f32[5,128,128]{2,1,0:T(8,128)S(1)}, f32[5,128,128]{2,1,0:T(8,128)}, u32[]{:S(2)}) copy-start(f32[5,128,128]{2,1,0:T(8,128)} %refs_8_.2) | copy-start | bytes 983044
  26.6 0.9 %copy-start.3 = (bf16[128,1024]{1,0:T(8,128)(2,1)S(1)}, bf16[128,1024]{1,0:T(8,128)(2,1)}, u32[]{:S(2)}) copy-start(bf16[128,1024]{1,0:T(8,128)(2,1)} %constant.19.clone.sel) | copy-start | bytes 786436
  27.5 0.8 copy-start.4
  28.3 0.8 copy-start.5
  29.1 0.7 copy-start.6
  29.8 0.7 copy-start.8
  30.4 0.7 copy-start.9
  31.1 0.7 copy-start.12
  34.5 1.0 %copy-start.1 = (f32[5,128,128]{2,1,0:T(8,128)S(1)}, f32[5,128,128]{2,1,0:T(8,128)}, u32[]{:S(2)}) copy-start(f32[5,128,128]{2,1,0:T(8,128)} %refs_8_.2) | copy-start | bytes 983044
  35.5 0.9 %copy-start.2 = (bf16[1,5,128,128]{3,2,1,0:T(8,128)(2,1)S(1)}, bf16[1,5,128,128]{3,2,1,0:T(8,128)(2,1)}, u32[]{:S(2)}) copy-start(bf16[1,5,128,128]{3,2,1,0:T(8,128)(2,1)} %param.10) | copy-start | bytes 491524
  36.4 0.7 copy-start.7
  37.1 0.7 copy-start.10
  37.8 0.7 copy-start.11
where the time goes:
time: 86.9 us; the launch traced here: 86.4 us
  Pallas kernels  36.9 us (42%)
  blocking collectives  17.6 us (20%)
  starting transfers between devices  11.7 us (13%)
  local copies, waits for them, and re-layouts  11.4 us (13%)
  waiting for transfers between devices  7.42 us (9%)
    pallas_call x1, Pallas kernels, on_device(): pl.pallas_call(functools.partial(main_kernel, n_out, cycle), out_shape=(j...  30.1 us
    psum x1, blocking collectives, on_device(): sens = lax.psum(sens[:, 0].reshape(GRP_DEV, AMP), 'blk')  17.6 us
    unnamed x32, local copies, waits for them, and re-layouts  11.2 us
    ppermute x3, starting transfers between devices, on_device(): lax.ppermute(own_edges, 'out', shift_pairs(n_out, k))  5.44 us
    ppermute x3, waiting for transfers between devices, on_device(): lax.ppermute(own_edges, 'out', shift_pairs(n_out, k))  5.42 us
    ppermute x1, starting transfers between devices, on_device(): lax.ppermute(send_b, 'blk', [(i, (i + 1) % cycle if i % 2 else (i - 1) %...  3.71 us
    pallas_call x1, Pallas kernels, on_device(): pl.pallas_call(functools.partial(halo_kernel, cycle), out_shape=(field, f...  2.75 us
    ppermute x3, starting transfers between devices, on_device(): lax.ppermute(slot, 'out', shift_pairs(n_out, k))  2.53 us
  transfers between devices with their start and end apart: 8, of which 2 were waited for; matrix products, arithmetic and copies ran while one was open for 1% of the time, Pallas kernels for 6%

commit v1 on v0

v1 whole, which is shorter than its diff:
```python
import functools
import math

import jax
import jax.numpy as jnp
import numpy as np
from jax import lax
from jax.experimental import pallas as pl
from jax.experimental.pallas import tpu as pltpu
from jax.sharding import PartitionSpec as P

FIELDS = 5
BLADES = 96
AMP = 4
GRP_DEV = 2
STEPS = 3
PAIRS = GRP_DEV * AMP

time_step = 0.25
second_diff = 0.1
fourth_diff = 0.02
link_weight = 0.5
two_pi = 2.0 * math.pi

C0 = 1.0 - time_step * (2.0 * second_diff + 6.0 * fourth_diff + link_weight)
C1 = time_step * (second_diff + 4.0 * fourth_diff)
C2 = -time_step * fourth_diff
CP = time_step * link_weight
CM = 0.5 * time_step
CU = 0.25 * time_step

FW = 6
QW = 4
PARTS = 3
SLOT = 32
QROW = PARTS * FW
LINK_ROW = QROW + STEPS * QW
QS_ROWS = 48
SEG = 16
HALF = SEG // 2
VMEM_LIMIT = 60 * 2**20

VMEM = pl.BlockSpec(memory_space=pltpu.VMEM)
SMEM = pl.BlockSpec(memory_space=pltpu.SMEM)
HBM = pl.BlockSpec(memory_space=pl.ANY)
UNIT = time_step * fourth_diff
CENTRE = round(C0 / UNIT)
NEAR = round(C1 / UNIT)
F32 = jnp.float32
BF16 = jnp.bfloat16
NT = (((1,), (1,)), ((), ()))
TN = (((0,), (0,)), ((), ()))
NN = (((1,), (0,)), ((), ()))


def mm(a, b, dims=NN):
    return lax.dot_general(a, b, dims, preferred_element_type=F32)


def split3(x):
    hi = x.astype(BF16)
    rest = x - hi.astype(F32)
    mid = rest.astype(BF16)
    return hi, mid, (rest - mid.astype(F32)).astype(BF16)


def exact_mm(a, x):
    hi, mid, lo = split3(x)
    return mm(a, hi) + mm(a, mid) + mm(a, lo)


def fetch(moves, sems):
    copies = [pltpu.make_async_copy(src, dst, sems.at[i]) for i, (src, dst) in enumerate(moves)]
    for copy in copies:
        copy.start()
    return copies


def arrive(copies):
    for copy in copies:
        copy.wait()


def like(x):
    return pltpu.VMEM(x.shape, x.dtype)


def cost(flops, moved):
    return pl.CostEstimate(flops=flops, bytes_accessed=moved, transcendentals=0)


def q_select(width):
    out = np.zeros((FIELDS, QS_ROWS, width), np.float32)
    for f in range(FIELDS):
        for j in range(QW):
            out[f, f * 8 + j, j] = 1.0
            out[f, f * 8 + QW + j, width - QW + j] = 1.0
    return out.astype(jnp.bfloat16)


def q_edges_kernel(ck_hbm, sel_hbm, out_ref, ck_ref, sel_ref, sems):
    arrive(fetch(((ck_hbm, ck_ref), (sel_hbm, sel_ref)), sems))
    total = None
    for f in range(FIELDS):
        part = mm(sel_ref[f], ck_ref[f], NT)
        total = part if total is None else total + part
    out_ref[...] = total.astype(BF16)


def strip_selects(width):
    forcing_sel = np.zeros((PARTS, 2 * SLOT, width), np.float32)
    for part in range(PARTS):
        for j in range(FW):
            forcing_sel[part, part * FW + j, j] = 1.0
            forcing_sel[part, SLOT + part * FW + j, width - FW + j] = 1.0
    place = np.zeros((FIELDS, 2 * SLOT, STEPS * QS_ROWS), np.float32)
    for f in range(FIELDS):
        for n in range(STEPS):
            for j in range(QW):
                place[f, QROW + n * QW + j, n * QS_ROWS + f * 8 + j] = 1.0
                place[f, SLOT + QROW + n * QW + j, n * QS_ROWS + f * 8 + QW + j] = 1.0
    return forcing_sel.astype(jnp.bfloat16), place.astype(jnp.bfloat16)


def pick(values, index):
    out = values[0]
    for k in range(1, len(values)):
        out = jnp.where(index == k, values[k], out)
    return out


def strips_kernel(n_out, *refs):
    owner, *qs = refs[: 1 + n_out]
    hbm = refs[1 + n_out : 5 + n_out]
    send_a, send_b = refs[5 + n_out : 7 + n_out]
    scratch = refs[7 + n_out : -1]
    arrive(fetch(zip((*qs, *hbm), scratch), refs[-1]))
    edges = [q[...].astype(F32) for q in scratch[:n_out]]
    forcing, link, fsel, place = scratch[n_out:]
    me = lax.axis_index("out")
    even = lax.axis_index("blk") % 2 == 0
    chosen = jnp.concatenate(
        [pick(edges, (me - owner[n] + n_out) % n_out) for n in range(STEPS)], axis=0
    ).astype(BF16)
    row = lax.broadcasted_iota(jnp.int32, (2 * SLOT, link.shape[1]), 0)
    links = jnp.broadcast_to(link[...].astype(F32), row.shape)
    for f in range(FIELDS):
        both = mm(place[f], chosen)
        for sel, part in zip(range(PARTS), split3(forcing[f])):
            both = both + mm(fsel[sel], part, NT)
        if f == 0:
            both = jnp.where(row % SLOT == LINK_ROW, links, both)
        left, right = both[:SLOT], both[SLOT:]
        send_a[f * SLOT : (f + 1) * SLOT] = jnp.where(even, right, left).astype(BF16)
        send_b[f * SLOT : (f + 1) * SLOT] = jnp.where(even, left, right).astype(BF16)


def column_factor(columns, pair, start, total, group_base, blade_group):
    scaled = columns * BLADES
    first = ((start + total - HALF) * BLADES) // total - BLADES
    group = jnp.full(columns.shape, -1, jnp.int32)
    numerator = jnp.zeros(columns.shape, jnp.int32)
    width = columns.shape[-1]
    for j in range((width + SEG) * BLADES // total + 2):
        blade = first + j
        inside = (scaled >= blade * total) & (scaled < (blade + 1) * total)
        group = jnp.where(inside, blade_group[(blade + BLADES) % BLADES], group)
        numerator = jnp.where(inside, scaled - blade * total, numerator)
    phase = numerator.astype(F32) / total
    amp = pair & (AMP - 1)
    order = ((amp >> 1) + 1).astype(F32)
    angle = two_pi * order * phase
    harmonic = jnp.where((amp & 1) == 0, jnp.cos(angle), jnp.sin(angle))
    return jnp.where(group == group_base + pair // AMP, harmonic, 0.0)


def flux(fm, q, d):
    inner = q[0] * d[0]
    for f in range(1, FIELDS):
        inner = inner + q[f] * d[f]
    u = q[1] * CU
    out = []
    for e in range(FIELDS):
        value = u * d[e]
        for f in range(FIELDS):
            value = value + fm[f, e] * d[f]
        if e == 1:
            value = value + CU * inner
        out.append(value)
    return out


def prepare_kernel(cycle, blade_group, link_s, forcing_hbm, link_hbm, k_ref, kp_ref, b0_ref, inv_ref, forcing, link, sems):
    copies = fetch(((forcing_hbm, forcing), (link_hbm, link)), sems)
    rows, width = forcing.shape[1:]
    total = cycle * width
    start = lax.axis_index("blk") * width

    def invert(r, c):
        inv_ref[link_s[r]] = r
        return c

    lax.fori_loop(0, rows, invert, 0, unroll=8)
    lane = lax.broadcasted_iota(jnp.int32, (8, width), 1)
    sub = lax.broadcasted_iota(jnp.int32, (8, width), 0)
    p = lane & (SEG - 1)
    packed = jnp.where(p < HALF, p - QW, width - QW + p - HALF) + start
    args = (start, total, lax.axis_index("out") * GRP_DEV, blade_group)
    for i in range(5):
        k_ref[i] = column_factor(lane + start + (i - 2), sub, *args)
        kp_ref[i] = column_factor(packed + (i - 2), sub, *args)
    arrive(copies)
    hot = one_hot(link[...].astype(F32), rows)
    for f in range(FIELDS):
        b0_ref[f] = (C0 + 1.0) * forcing[f] + CP * exact_mm(hot, forcing[f])


def one_hot(links, rows):
    row = lax.broadcasted_iota(jnp.int32, (rows, rows), 0).astype(F32)
    return jnp.where(links == row, 1.0, 0.0).astype(BF16)


def halo_selects(width, rows):
    blocks = width // SEG
    step = rows // blocks
    sel = np.zeros((4 * SLOT, 7, SEG), np.float32)
    edge = np.zeros((4 * SLOT, width), np.float32)

    def place(column, size):
        if column < 0:
            return 0, column + size
        if column < size:
            return 1, column
        if column < width:
            return 2, column - (width - size)
        return 3, column - width

    def forcing_rows(column):
        source, j = place(column, FW)
        return [source * SLOT + part * FW + j for part in range(PARTS)] if 0 <= j < FW else []

    for p in range(SEG):
        column = p - QW if p < HALF else width - QW + p - HALF
        for i in range(5):
            for row in forcing_rows(column + i - 2):
                sel[row, i, p] = 1.0
        source, j = place(column, QW)
        for i, n in ((5, STEPS - 1), (6, STEPS - 2)):
            sel[source * SLOT + QROW + n * QW + j, i, p] = 1.0
    for lane, column in ((width - 2, -2), (width - 1, -1), (0, width), (1, width + 1)):
        for row in forcing_rows(column):
            edge[row, lane] = 1.0
    big = np.zeros((blocks, 4 * SLOT, 7, blocks, SEG), np.float32)
    for j in range(blocks):
        big[j, :, :, j, :] = sel
    big = big.reshape(blocks * 4 * SLOT, 7 * width)
    return big.astype(jnp.bfloat16), edge.astype(jnp.bfloat16)


def stencil_selects(width):
    blocks = width // SEG
    inner = np.zeros((2, width, 2 * width), np.float32)
    outer = np.zeros((blocks, 2, width, 2 * width), np.float32)

    def spread(column):
        out = []
        for c, w in ((column + 1, 1.0), (column - 1, -1.0)):
            if 0 <= c < width:
                out.append((c, w))
        for c, w in (
            (column, CENTRE),
            (column - 1, NEAR),
            (column + 1, NEAR),
            (column - 2, -1.0),
            (column + 2, -1.0),
        ):
            if 0 <= c < width:
                out.append((width + c, w))
        return out

    for column in range(width):
        for lane, w in spread(column):
            inner[:, column, lane] = w
    for j in range(blocks):
        for p, column in ((2, -2), (3, -1), (HALF + QW, width), (HALF + QW + 1, width + 1)):
            for lane, w in spread(column):
                outer[j, :, j * SEG + p, lane] = w
    return (
        inner.reshape(2 * width, 2 * width).astype(jnp.bfloat16),
        outer.reshape(blocks, 2 * width, 2 * width).astype(jnp.bfloat16),
    )


def halves(x):
    hi = x.astype(BF16)
    return jnp.concatenate([hi, (x - hi.astype(F32)).astype(BF16)], axis=1)


def halo_kernel(
    fm, link_hbm, send_a, send_b, recv_a, recv_b, big_hbm, edge_hbm, kp_hbm,
    e1_ref, e2_ref, fe_ref,
    link, sa_v, sb_v, ra_v, rb_v, big, edge, kp_ref, y_ref, fmc, sems,
):
    copies = fetch(
        (
            (link_hbm, link), (send_a, sa_v), (send_b, sb_v), (recv_a, ra_v), (recv_b, rb_v),
            (edge_hbm, edge), (kp_hbm, kp_ref), (big_hbm, big),
        ),
        sems,
    )
    rows, width = link.shape[1], kp_ref.shape[2]
    blocks = width // SEG
    step = rows // blocks
    even = lax.axis_index("blk") % 2 == 0
    for f in range(FIELDS):
        for e in range(FIELDS):
            fmc[f, e] = fm[f, e] * CM
    arrive(copies[:-1])
    sa, sb = sa_v[...].astype(F32), sb_v[...].astype(F32)
    ra, rb = ra_v[...].astype(F32), rb_v[...].astype(F32)
    own_left, own_right = jnp.where(even, sb, sa), jnp.where(even, sa, sb)
    left, right = jnp.where(even, rb, ra), jnp.where(even, ra, rb)
    hot_own = one_hot(link[...].astype(F32), rows)
    hot_left = one_hot(left[LINK_ROW : LINK_ROW + 1], rows)
    hot_right = one_hot(right[LINK_ROW : LINK_ROW + 1], rows)
    source = lax.broadcasted_iota(jnp.int32, (rows, 4 * SLOT), 1) // SLOT

    def permuted(x):
        by_left, by_right = mm(hot_left, x), mm(hot_right, x)
        outer = jnp.where(source == 0, by_left, by_right)
        by_tile = jnp.where((source == 1) | (source == 2), mm(hot_own, x), outer)
        return by_left.astype(BF16), by_right.astype(BF16), by_tile.astype(BF16)

    def rowed(x):
        return jnp.concatenate([x[j * step : (j + 1) * step] for j in range(blocks)], axis=1)

    sets = [[] for _ in range(5)]
    for f in range(FIELDS):
        s = slice(f * SLOT, (f + 1) * SLOT)
        g = jnp.concatenate([left[s], own_left[s], own_right[s], right[s]], axis=0)
        g = g.T.astype(BF16)
        fe_ref[f] = mm(g, edge[...])
        by_left, by_right, by_tile = permuted(g)
        for rows_of, x in zip(sets, (g, by_tile, permuted(by_tile)[2], by_left, by_right)):
            rows_of.append(rowed(x))
    copies[-1].wait()
    group = FIELDS * step
    y = mm(jnp.concatenate(sum(sets, []), axis=0), big[...])
    is_left = lax.broadcasted_iota(jnp.int32, (step, width), 1) & (SEG - 1) < HALF

    def part(i, f, which):
        return y[i * group + f * step : i * group + (f + 1) * step, which * width : (which + 1) * width]

    def at(linked, f, which):
        if linked:
            return jnp.where(is_left, part(3, f, which), part(4, f, which))
        return part(0, f, which)

    for i in range(2):
        shifted = [[at(i, f, d) for f in range(FIELDS)] for d in range(5)]
        q2 = [at(i, f, 5) for f in range(FIELDS)]
        plus = flux(fmc, q2, shifted[3])
        minus = flux(fmc, q2, shifted[1])
        for f in range(FIELDS):
            b = (
                C2 * shifted[0][f],
                C1 * shifted[1][f] - minus[f],
                (C0 + 1.0) * shifted[2][f] + CP * part(i + 1, f, 2),
                C1 * shifted[3][f] + plus[f],
                C2 * shifted[4][f],
            )
            for d in range(5):
                y_ref[i * 5 + d, f] = b[d]
    for f in range(FIELDS):
        y_ref[10, f] = part(0, f, 2)
        y_ref[11, f] = part(0, f, 6)
    kp = [kp_ref[i] for i in range(5)]

    def body(r, c):
        def row(i, f):
            return jnp.broadcast_to(y_ref[i, f, pl.ds(r, 1), :], (8, width))

        mu, linked, d, base = [], [], [], []
        for f in range(FIELDS):
            for i, out in ((0, mu), (5, linked)):
                value = row(i, f) * kp[0]
                for n in range(1, 5):
                    value = value + row(i + n, f) * kp[n]
                out.append(value)
            x = mu[f]
            m1, p1 = pltpu.roll(x, 1, 1), pltpu.roll(x, width - 1, 1)
            m2, p2 = pltpu.roll(x, 2, 1), pltpu.roll(x, width - 2, 1)
            d.append(m1 - p1)
            base.append(
                C0 * x + C1 * (m1 + p1) + C2 * (m2 + p2) + CP * linked[f] + row(10, f) * kp[2]
            )
        moved = flux(fmc, [row(11, f) for f in range(FIELDS)], d)
        at = pl.ds(pl.multiple_of(r * (FIELDS * 8), 8), FIELDS * 8)
        e1_ref[at, :] = halves(jnp.concatenate(mu, axis=0))
        e2_ref[at, :] = halves(
            jnp.concatenate([b - m for b, m in zip(base, moved)], axis=0)
        )
        return c

    lax.fori_loop(0, step, body, 0, unroll=4)


def main_kernel(n_out, cycle, *refs):
    owner, fm, inv = refs[:3]
    slots = refs[3 : 3 + n_out]
    hbm = refs[3 + n_out : 11 + n_out]
    out_hbm, sens_ref = refs[11 + n_out : 13 + n_out]
    (
        forcing, fe, b0, k_ref, inner, outer, e1, e2,
        q0, q1, q2, bs, coef, mu1, mu2, dz, stage, weighted, fmc, sems, out_sems,
    ) = refs[13 + n_out :]
    copies = fetch(zip(hbm, (forcing, fe, b0, k_ref, inner, outer, e1, e2)), sems)
    rows, width = forcing.shape[1], forcing.shape[2]
    me = lax.axis_index("out")
    total = cycle * width
    q_copies = []
    for n, q in reversed(tuple(enumerate((q0, q1, q2)))):
        which = (me - owner[n] + n_out) % n_out
        for s, slot in enumerate(slots):

            @pl.when(which == s)
            def _():
                pltpu.make_async_copy(slot, q, sems.at[8 + n]).start()

        q_copies.append(pltpu.make_async_copy(slots[0], q, sems.at[8 + n]))

    for f in range(FIELDS):
        for e in range(FIELDS):
            fmc[f, e] = fm[f, e] * CM
    lane = lax.broadcasted_iota(jnp.int32, (8, width), 1)
    start = lax.axis_index("blk") * width
    weight = 1.0 + 2.0 * (lane + start).astype(F32) / total
    norm = 1.0 / math.sqrt(FIELDS * rows * total)

    def around(x, edge):
        return (
            pltpu.roll(jnp.where(lane == width - 1, edge, x), 1, 1),
            pltpu.roll(jnp.where(lane == 0, edge, x), width - 1, 1),
            pltpu.roll(jnp.where(lane >= width - 2, edge, x), 2, 1),
            pltpu.roll(jnp.where(lane < 2, edge, x), width - 2, 1),
        )

    def dense(i, z):
        rs = pl.ds(pl.multiple_of(i * 16, 16), 16)
        for n, q_ref in enumerate((q0, q1)):
            q = [q_ref[f, rs, :].astype(F32) for f in range(FIELDS)]
            u = CU * q[1]
            for e in range(FIELDS):
                coef[n, e, rs, :] = (u if e != 1 else u + u) + fmc[e, e]
            for j, f in enumerate((0, 2, 3, 4)):
                coef[n, FIELDS + j, rs, :] = CU * q[f] + fmc[f, 1]
        q = [q2[f, rs, :].astype(F32) for f in range(FIELDS)]
        for half in range(2):
            r8 = pl.ds(pl.multiple_of(i * 16 + half * 8, 8), 8)
            near = [around(forcing[f, r8, :], fe[f, r8, :]) for f in range(FIELDS)]
            mine = [x[half * 8 : half * 8 + 8] for x in q]
            minus = flux(fmc, mine, [a[0] for a in near])
            plus = flux(fmc, mine, [a[1] for a in near])
            for f in range(FIELDS):
                m1, p1, m2, p2 = near[f]
                bs[0, f, r8, :] = C2 * m2
                bs[1, f, r8, :] = C1 * m1 - minus[f]
                bs[2, f, r8, :] = C1 * p1 + plus[f]
                bs[3, f, r8, :] = C2 * p2
                w = forcing[f, r8, :] * weight
                weighted[f, r8, :] = w
                z = z + w * forcing[f, r8, :]
        return z

    zero = jnp.zeros((8, width), F32)
    arrive(copies + q_copies)
    z = lax.fori_loop(0, rows // 16, dense, zero)
    k = [k_ref[i] for i in range(5)]

    def spread(ref, index, r):
        return jnp.broadcast_to(ref[(*index, pl.ds(r, 1), slice(None))], (8, width))

    def first(i, acc):
        for j in range(8):
            r = i * 8 + j
            for f in range(FIELDS):
                value = spread(bs, (0, f), r) * k[0] + spread(bs, (1, f), r) * k[1]
                value = value + spread(b0, (f,), r) * k[2] + spread(bs, (2, f), r) * k[3]
                value = value + spread(bs, (3, f), r) * k[4]
                mu1[r, f] = value
                acc = acc + value * spread(weighted, (f,), r)
        return acc

    acc = lax.fori_loop(0, rows // 8, first, zero)

    blocks = width // SEG
    size = rows // blocks
    group = size * FIELDS * 8

    def step(n, source, edges, j, keep, acc):
        r0 = pl.multiple_of(j * size, size)
        x = source[pl.ds(r0, size)].reshape(group, width)
        dz[...] = mm(halves(x), inner[...]) + mm(edges[...], outer[j])
        for i in range(size):
            r = r0 + i
            linked = inv[r]
            at = [slice((i * FIELDS + f) * 8, (i * FIELDS + f + 1) * 8) for f in range(FIELDS)]
            d = [dz[at[f], :width] for f in range(FIELDS)]
            for e in range(FIELDS):
                value = UNIT * dz[at[e], width:] + CP * source[linked, e]
                for f in range(FIELDS):
                    if f == e:
                        m = spread(coef, (n, e), r)
                    elif e == 1:
                        m = spread(coef, (n, FIELDS + (0, 2, 3, 4).index(f)), r)
                    else:
                        m = fmc[f, e]
                    value = value - m * d[f]
                value = keep(r, e, value)
                acc = acc + value * spread(weighted, (e,), r)
        return acc

    def second(j, acc):
        def keep(r, e, value):
            value = value + spread(forcing, (e,), r) * k[2]
            mu2[r, e] = value
            return value

        return step(1, mu1, e1, j, keep, acc)

    acc = lax.fori_loop(0, blocks, second, acc)
    shaped = stage.reshape(PAIRS * FIELDS, rows, width)

    def send(j):
        at = pl.ds(pl.multiple_of(j * size, size), size)
        return pltpu.make_async_copy(shaped.at[:, at, :], out_hbm.at[:, at, :], out_sems.at[j])

    def third(j, acc):
        def keep(r, e, value):
            stage[pl.ds(e * rows + r, PAIRS, stride=FIELDS * rows), :] = value
            return value

        acc = step(0, mu2, e2, j, keep, acc)
        send(j).start()
        return acc

    acc = lax.fori_loop(0, blocks, third, acc)
    source_part = jnp.sum(z, axis=0, keepdims=True) * k[2]
    acc = (acc - 2.0 * source_part) * norm
    sens_ref[...] = jnp.broadcast_to(jnp.sum(acc, axis=1, keepdims=True), (8, width))
    for j in range(blocks):
        send(j).wait()


def shift_pairs(devices, k):
    return [(i, (i + k) % devices) for i in range(devices)]


def total_over(x, axis):
    devices = lax.axis_size(axis)
    if devices & (devices - 1):
        return lax.psum(x, axis)
    bit = 1
    while bit < devices:
        x = x + lax.ppermute(x, axis, [(i, i ^ bit) for i in range(devices)])
        bit *= 2
    return x


def on_device(checkpoints, owner, flux_matrix, row_link, blade_group, forcing):
    n_out = lax.axis_size("out")
    cycle = lax.axis_size("blk")
    rows, width = forcing.shape[1], forcing.shape[2]
    blocks = width // SEG
    slot = checkpoints[0]

    def struct(shape, kind=F32):
        return jax.ShapeDtypeStruct(shape, kind)

    sems = pltpu.SemaphoreType.DMA
    edge_sel = q_select(width)
    own_edges = pl.pallas_call(
        q_edges_kernel,
        out_shape=struct((QS_ROWS, rows), BF16),
        in_specs=[HBM, HBM],
        out_specs=VMEM,
        scratch_shapes=[like(slot), like(edge_sel), sems((2,))],
        cost_estimate=cost(2 * 240 * 128 * 128, 200000),
        name="edges",
    )(slot, edge_sel)
    edges = [own_edges] + [
        lax.ppermute(own_edges, "out", shift_pairs(n_out, k)) for k in range(1, n_out)
    ]
    sent = lax.optimization_barrier((slot, *edges[1:]))[0]
    slots = [slot] + [lax.ppermute(sent, "out", shift_pairs(n_out, k)) for k in range(1, n_out)]

    fsel, place = strip_selects(width)
    strip = struct((FIELDS * SLOT, rows), BF16)
    operands = (*edges, forcing, row_link, fsel, place)
    send_a, send_b = pl.pallas_call(
        functools.partial(strips_kernel, n_out),
        out_shape=(strip, strip),
        in_specs=[SMEM] + [HBM] * len(operands),
        out_specs=(VMEM, VMEM),
        scratch_shapes=[*map(like, operands), sems((len(operands),))],
        cost_estimate=cost(10**7, 600000),
        name="strips",
    )(owner, *operands)
    recv_a = lax.ppermute(send_a, "blk", [(i, i ^ 1) for i in range(cycle)])
    recv_b = lax.ppermute(
        send_b, "blk", [(i, (i + 1) % cycle if i % 2 else (i - 1) % cycle) for i in range(cycle)]
    )

    k, kp, b0, inv = pl.pallas_call(
        functools.partial(prepare_kernel, cycle),
        out_shape=(
            struct((5, PAIRS, width)),
            struct((5, PAIRS, width)),
            struct((FIELDS, rows, width)),
            struct((rows,), jnp.int32),
        ),
        in_specs=[SMEM, SMEM, HBM, HBM],
        out_specs=(VMEM, VMEM, VMEM, SMEM),
        scratch_shapes=[like(forcing), like(row_link), sems((2,))],
        cost_estimate=cost(10**8, 10**6),
        name="prepare",
    )(blade_group, row_link[0], forcing, row_link)

    big, edge = halo_selects(width, rows)
    step_rows = rows // blocks
    edge_shape = (step_rows * FIELDS * 8, 2 * width)
    operands = (row_link, send_a, send_b, recv_a, recv_b, big, edge, kp)
    loaded = (row_link, send_a, send_b, recv_a, recv_b, big, edge, kp)
    e1, e2, fe = pl.pallas_call(
        halo_kernel,
        out_shape=(struct(edge_shape, BF16), struct(edge_shape, BF16), struct((FIELDS, rows, width))),
        in_specs=[SMEM] + [HBM] * len(operands),
        out_specs=(VMEM,) * 3,
        scratch_shapes=[
            *map(like, loaded),
            pltpu.VMEM((12, FIELDS, step_rows, width), F32),
            pltpu.SMEM((FIELDS, FIELDS), F32),
            sems((len(operands),)),
        ],
        compiler_params=pltpu.CompilerParams(vmem_limit_bytes=VMEM_LIMIT),
        cost_estimate=cost(10**8, 4 * 10**6),
        name="halo",
    )(flux_matrix, *operands)

    pairs_fields = PAIRS * FIELDS
    inner, outer = stencil_selects(width)
    operands = (forcing, fe, b0, k, inner, outer, e1, e2)
    adjoint, sens = pl.pallas_call(
        functools.partial(main_kernel, n_out, cycle),
        out_shape=(struct((pairs_fields, rows, width)), struct((PAIRS, width))),
        in_specs=[SMEM] * 3 + [HBM] * (n_out + len(operands)),
        out_specs=(HBM, VMEM),
        scratch_shapes=[
            *map(like, operands),
            like(slot),
            like(slot),
            like(slot),
            pltpu.VMEM((4, FIELDS, rows, width), F32),
            pltpu.VMEM((STEPS - 1, 2 * FIELDS - 1, rows, width), F32),
            pltpu.VMEM((rows, FIELDS, PAIRS, width), F32),
            pltpu.VMEM((rows, FIELDS, PAIRS, width), F32),
            pltpu.VMEM((step_rows * FIELDS * PAIRS, 2 * width), F32),
            pltpu.VMEM((pairs_fields * rows, width), F32),
            pltpu.VMEM((FIELDS, rows, width), F32),
            pltpu.SMEM((FIELDS, FIELDS), F32),
            sems((len(operands) + STEPS,)),
            sems((blocks,)),
        ],
        compiler_params=pltpu.CompilerParams(vmem_limit_bytes=VMEM_LIMIT),
        cost_estimate=cost(10**9, 10**7),
        name="steps",
    )(owner, flux_matrix, inv, *slots, *operands)

    sens = total_over(sens, "blk")[:, 0].reshape(GRP_DEV, AMP)
    return adjoint.reshape(GRP_DEV, AMP, FIELDS, rows, width), sens


def solution(mesh):
    return jax.shard_map(
        on_device,
        mesh=mesh,
        in_specs=(P("out", None, None, "blk"), P(), P(), P("blk", None), P(), P(None, None, "blk")),
        out_specs=(P("out", None, None, None, "blk"), P("out", None)),
        check_vma=False,
    )
```

time: 86.9 us -> 57.3 us (0.66)
  blocking collectives: 17.6 us -> 0 us
  Pallas kernels: 36.9 us -> 27.2 us
  local copies, waits for them, and re-layouts: 11.4 us -> 2.12 us
  waiting for transfers between devices: 7.42 us -> 12.4 us
  starting transfers between devices: 11.7 us -> 13.7 us
    psum x1 -> x0, blocking collectives: 17.6 us -> none  [on_device(): sens = lax.psum(sens[:, 0].reshape(GRP_DEV, AMP), 'blk')]
    pallas_call x3 -> x4, Pallas kernels: 34.6 us -> 24.2 us  [the longest x1 14.2 us: on_device(): pl.pallas_call(functools.partial(main_kernel, n_out, cycle), out_shape=(s...]
    unnamed x32 -> x16, local copies, waits for them, and re-layouts: 11.2 us -> 1.36 us
    ppermute x3 -> x6, waiting for transfers between devices: 0.01 us -> 8.2 us  [the longest x3 8.19 us: total_over(): x = x + lax.ppermute(x, axis, [(i, i ^ bit) for i in range(devices)])]
    ppermute x3 -> x6, starting transfers between devices: 2.53 us -> 4.9 us  [the longest x3 3.55 us: on_device(): lax.ppermute(sent, 'out', shift_pairs(n_out, k))]
    ppermute x1, waiting for transfers between devices: 2 us -> 0.01 us  [on_device(): lax.ppermute(send_b, 'blk', [(i, (i + 1) % cycle if i % 2 else (i - 1) %...]
    ppermute x3, waiting for transfers between devices: 5.42 us -> 4.21 us  [on_device(): lax.ppermute(own_edges, 'out', shift_pairs(n_out, k))]
  transfers between devices with their start and end apart: 8 -> 11, of which waited for: 2 -> 6; matrix products, arithmetic and copies ran while one was open for 1% -> 0% of each run, Pallas kernels for 6% -> 20%
where the time goes in v1:
time: 57.3 us; the launch traced here: 56.9 us
  Pallas kernels  27.2 us (47%)
  starting transfers between devices  13.7 us (24%)
  waiting for transfers between devices  12.4 us (22%)
  local copies, waits for them, and re-layouts  2.12 us (4%)
  between operations  0.78 us (1%)
  other arithmetic  0.68 us (1%)
    pallas_call x1, Pallas kernels, on_device(): pl.pallas_call(functools.partial(main_kernel, n_out, cycle), out_shape=(s...  14.2 us
    ppermute x3, waiting for transfers between devices, total_over(): x = x + lax.ppermute(x, axis, [(i, i ^ bit) for i in range(devices)])  8.19 us
    pallas_call x1, Pallas kernels, on_device(): pl.pallas_call(halo_kernel, out_shape=(struct(edge_shape, BF16), struct(e...  5.58 us
    ppermute x3, starting transfers between devices, on_device(): lax.ppermute(own_edges, 'out', shift_pairs(n_out, k))  5.04 us
    ppermute x3, waiting for transfers between devices, on_device(): lax.ppermute(own_edges, 'out', shift_pairs(n_out, k))  4.21 us
    ppermute x1, starting transfers between devices, on_device(): lax.ppermute(send_b, 'blk', [(i, (i + 1) % cycle if i % 2 else (i - 1) %...  3.7 us
    ppermute x3, starting transfers between devices, on_device(): lax.ppermute(sent, 'out', shift_pairs(n_out, k))  3.55 us
    pallas_call x1, Pallas kernels, on_device(): pl.pallas_call(functools.partial(strips_kernel, n_out), out_shape=(strip,...  2.94 us
  transfers between devices with their start and end apart: 11, of which 6 were waited for; matrix products, arithmetic and copies ran while one was open for 0% of the time, Pallas kernels for 20%

profile of v1, /device:TPU:0, one launch (start us, length us, event | category | flops | bytes accessed | tf_op | source)
XLA Modules:
  0.0 56.9 jit_solution(4171072139987252834)
XLA Ops:
  0.6 1.8 %edges.1.refs_1_ = bf16[48,128]{1,0:T(8,128)(2,1)} custom-call(bf16[5,128,128]{2,1,0:T(8,128)(2,1)} %bitcast.3, bf16[5,48,128]{2,1,0:T(8,128)(2,1)} %constant.14.clone.sel_hbm), custom_call_target="tpu_custom_call" | custom-call | flops 7864320 | bytes 200000 | tf_op jit(solution)/shard_map/edges/pallas_call | solution.py:582
  2.4 3.9 %collective-permute-start.2 = (bf16[48,128]{1,0:T(8,128)(2,1)}, bf16[48,128]{1,0:T(8,128)(2,1)S(1)}, u32[]{:S(2)}, u32[]{:S(2)}) collective-permute-start(bf16[48,128]{1,0:T(8,128)(2,1)} %edges.1.refs_1_), channel_id=1, source_target_pairs={{0,24},{8,0},{16,8},{24,16},{1,25},{9,1},{17,9},{25,17},{2,26},{10... | collective-permute-start | bytes 36872 | tf_op jit(solution)/shard_map/ppermute | solution.py:592
  6.4 0.5 collective-permute-start.1
  6.9 0.6 %collective-permute-start = (bf16[48,128]{1,0:T(8,128)(2,1)}, bf16[48,128]{1,0:T(8,128)(2,1)S(1)}, u32[]{:S(2)}, u32[]{:S(2)}) collective-permute-start(bf16[48,128]{1,0:T(8,128)(2,1)} %edges.1.refs_1_), channel_id=1, source_target_pairs={{0,8},{8,16},{16,24},{24,0},{1,9},{9,17},{17,25},{25,1},{2,10},{10... | collective-permute-start | bytes 36872 | tf_op jit(solution)/shard_map/ppermute | solution.py:592
  7.5 0.5 collective-permute-done.2.refs_4_
  8.0 0.0 copy-start.2
  8.0 2.3 %collective-permute-done.1.refs_3_ = bf16[48,128]{1,0:T(8,128)(2,1)S(1)} collective-permute-done((bf16[48,128]{1,0:T(8,128)(2,1)}, bf16[48,128]{1,0:T(8,128)(2,1)S(1)}, u32[]{:S(2)}, u32[]{:S(2)}) %collective-permute-start.1) | collective-permute-done | bytes 12320 | tf_op jit(solution)/shard_map/ppermute | solution.py:592
  10.3 0.0 copy-start.3
  10.3 1.4 %collective-permute-done.refs_2_ = bf16[48,128]{1,0:T(8,128)(2,1)S(1)} collective-permute-done((bf16[48,128]{1,0:T(8,128)(2,1)}, bf16[48,128]{1,0:T(8,128)(2,1)S(1)}, u32[]{:S(2)}, u32[]{:S(2)}) %collective-permute-start) | collective-permute-done | bytes 12320 | tf_op jit(solution)/shard_map/ppermute | solution.py:592
  11.7 0.0 copy-start.4
  11.7 0.1 collective-permute-start.5
  11.8 1.4 %collective-permute-start.4 = (bf16[5,128,128]{2,1,0:T(8,128)(2,1)}, bf16[5,128,128]{2,1,0:T(8,128)(2,1)S(1)}, u32[]{:S(2)}, u32[]{:S(2)}) collective-permute-start(bf16[5,128,128]{2,1,0:T(8,128)(2,1)} %bitcast.5), channel_id=1, source_target_pairs={{0,16},{8,24},{16,0},{24,8},{1,17},{9,25},{17,1},{25,9},{2,18},{10... | collective-permute-start | bytes 491528 | tf_op jit(solution)/shard_map/ppermute | solution.py:595
  13.2 2.0 %collective-permute-start.3 = (bf16[5,128,128]{2,1,0:T(8,128)(2,1)}, bf16[5,128,128]{2,1,0:T(8,128)(2,1)S(1)}, u32[]{:S(2)}, u32[]{:S(2)}) collective-permute-start(bf16[5,128,128]{2,1,0:T(8,128)(2,1)} %bitcast.6), channel_id=1, source_target_pairs={{0,8},{8,16},{16,24},{24,0},{1,9},{9,17},{17,25},{25,1},{2,10},{10... | collective-permute-start | bytes 491528 | tf_op jit(solution)/shard_map/ppermute | solution.py:595
  15.2 0.0 copy-done.2
  15.2 0.0 copy-done.3
  15.2 0.0 copy-done.4
  15.2 2.9 %strips.1 = (bf16[160,128]{1,0:T(8,128)(2,1)}, bf16[160,128]{1,0:T(8,128)(2,1)}) custom-call(s32[4]{0:T(128)} %refs_0_.3, bf16[48,128]{1,0:T(8,128)(2,1)} %edges.1.refs_1_, bf16[48,128]{1,0:T(8,128)(2,1)} %copy-done.4, bf16[48,128]{1,0:T(8,128)(2,1)} %copy-done.3, bf16[48,128]{1,0:T(8,128)(2,1)} %copy-done.2, f32[5,128,128]{2,1,0:T(8,128)} %refs_7_.2, ...), custom_call_target="tpu_custom_call" | custom-call | flops 10000000 | bytes 600000 | tf_op jit(solution)/shard_map/strips/pallas_call | solution.py:600
  18.2 0.1 collective-permute-start.6
  18.2 3.7 %collective-permute-start.7 = (bf16[160,128]{1,0:T(8,128)(2,1)}, bf16[160,128]{1,0:T(8,128)(2,1)S(1)}, u32[]{:S(2)}, u32[]{:S(2)}) collective-permute-start(bf16[160,128]{1,0:T(8,128)(2,1)} %get-tuple-element.17.send_b), channel_id=1, source_target_pairs={{0,7},{1,2},{2,1},{3,4},{4,3},{5,6},{6,5},{7,0},{8,15},{9,10},{10,... | collective-permute-start | bytes 122888 | tf_op jit(solution)/shard_map/ppermute | solution.py:610
  22.0 2.7 %prepare.1 = (f32[5,8,128]{2,1,0:T(8,128)}, f32[5,8,128]{2,1,0:T(8,128)}, f32[5,128,128]{2,1,0:T(8,128)}, s32[128]{0:T(128)}) custom-call(s32[96]{0:T(128)} %blade_group.1, s32[128]{0:T(128)} %bitcast.8, f32[5,128,128]{2,1,0:T(8,128)} %refs_7_.2, s32[1,128]{1,0:T(1,128)} %link_hbm.3), custom_call_target="tpu_custom_call" | custom-call | flops 100000000 | bytes 1000000 | tf_op jit(solution)/shard_map/prepare/pallas_call | solution.py:614
  24.7 0.0 collective-permute-done.6.recv_a
  24.7 0.0 copy-start
  24.7 0.0 collective-permute-done.7.recv_b
  24.7 0.0 copy-start.1
  24.7 0.6 %copy-done = bf16[160,128]{1,0:T(8,128)(2,1)} copy-done((bf16[160,128]{1,0:T(8,128)(2,1)}, bf16[160,128]{1,0:T(8,128)(2,1)S(1)}, u32[]{:S(2)}) %copy-start) | copy-done | bytes 40984
  25.3 0.0 copy-done.1
  25.3 5.6 %halo.1 = (bf16[640,256]{1,0:T(8,128)(2,1)}, bf16[640,256]{1,0:T(8,128)(2,1)}, f32[5,128,128]{2,1,0:T(8,128)}) custom-call(f32[5,5]{1,0:T(8,128)} %refs_1_.1, s32[1,128]{1,0:T(1,128)} %link_hbm.3, bf16[160,128]{1,0:T(8,128)(2,1)} %get-tuple-element.16.send_a, bf16[160,128]{1,0:T(8,128)(2,1)} %get-tuple-element.17.send_b, bf16[160,128]{1,0:T(8,128)(2,1)} %copy-done, ...), custom_call_target="tpu_custom_call" | custom-call | flops 100000000 | bytes 4000000 | tf_op jit(solution)/shard_map/halo/pallas_call | solution.py:634
  30.9 0.0 collective-permute-done.5.refs_6_
  30.9 0.0 copy-start.5
  30.9 0.0 collective-permute-done.4.refs_5_
  30.9 0.0 copy-start.6
  30.9 0.0 collective-permute-done.3.refs_4_
  30.9 0.0 copy-start.7
  30.9 0.6 %copy-done.5 = bf16[5,128,128]{2,1,0:T(8,128)(2,1)} copy-done((bf16[5,128,128]{2,1,0:T(8,128)(2,1)}, bf16[5,128,128]{2,1,0:T(8,128)(2,1)S(1)}, u32[]{:S(2)}) %copy-start.5) | copy-done | bytes 163864
  31.6 0.1 copy-done.6
  31.6 0.1 copy-done.7
  31.7 14.2 %steps.1 = (f32[40,128,128]{2,1,0:T(8,128)}, f32[8,128]{1,0:T(8,128)}) custom-call(s32[4]{0:T(128)} %refs_0_.3, f32[5,5]{1,0:T(8,128)} %refs_1_.1, s32[128]{0:T(128)} %get-tuple-element.14.refs_2_, bf16[5,128,128]{2,1,0:T(8,128)(2,1)} %bitcast.7, bf16[5,128,128]{2,1,0:T(8,128)(2,1)} %copy-done.7, bf16[5,128,128]{2,1,0:T(8,128)(2,1)} %copy-done.6, ...), custom_call_target="tpu_custom_call" | custom-call | flops 1000000000 | bytes 10000000 | tf_op jit(solution)/shard_map/steps/pallas_call | solution.py:653
  45.9 0.1 collective-permute-start.8
  46.0 1.4 %collective-permute-done.8 = f32[8,128]{1,0:T(8,128)S(1)} collective-permute-done((f32[8,128]{1,0:T(8,128)}, f32[8,128]{1,0:T(8,128)S(1)}, u32[]{:S(2)}, u32[]{:S(2)}) %collective-permute-start.8) | collective-permute-done | bytes 4128 | tf_op jit(solution)/shard_map/ppermute | solution.py:565
  47.3 0.7 %add.9 = f32[8,128]{1,0:T(8,128)S(1)} add(f32[8,128]{1,0:T(8,128)} %get-tuple-element.25, f32[8,128]{1,0:T(8,128)S(1)} %collective-permute-done.8) | non-fusion elementwise | flops 1024 | bytes 12288 | tf_op jit(solution)/shard_map/add | solution.py:565
  48.0 0.0 collective-permute-start.9
  48.0 3.6 %collective-permute-done.9 = f32[8,128]{1,0:T(8,128)S(1)} collective-permute-done((f32[8,128]{1,0:T(8,128)S(1)}, f32[8,128]{1,0:T(8,128)S(1)}, u32[]{:S(2)}, u32[]{:S(2)}) %collective-permute-start.9) | collective-permute-done | bytes 4128 | tf_op jit(solution)/shard_map/ppermute | solution.py:565
  51.6 1.3 %collective-permute-start.10 = (f32[8,128]{1,0:T(8,128)S(1)}, f32[8,128]{1,0:T(8,128)S(1)}, u32[]{:S(2)}, u32[]{:S(2)}) collective-permute-start(f32[8,128]{1,0:T(8,128)S(1)} %add.10), channel_id=1, source_target_pairs={{0,4},{1,5},{2,6},{3,7},{4,0},{5,1},{6,2},{7,3},{8,12},{9,13},{10,... | collective-permute-start | bytes 12296 | tf_op jit(solution)/shard_map/ppermute | solution.py:565
  52.9 3.2 %collective-permute-done.10 = f32[8,128]{1,0:T(8,128)S(1)} collective-permute-done((f32[8,128]{1,0:T(8,128)S(1)}, f32[8,128]{1,0:T(8,128)S(1)}, u32[]{:S(2)}, u32[]{:S(2)}) %collective-permute-start.10) | collective-permute-done | bytes 4128 | tf_op jit(solution)/shard_map/ppermute | solution.py:565
  56.1 0.1 slice_reduce_fusion
  56.2 0.6 %reshape_squeeze.3 = f32[2,4]{1,0:T(2,128)} reshape(f32[8]{0:T(128)S(1)} %slice_reduce_fusion) | data formatting | bytes 64 | tf_op jit(solution)/shard_map/reshape;squeeze | solution.py:679
  (2 shorter events, 0.0 us)
Async XLA Ops:
  2.4 5.6 %collective-permute-start.2 = (bf16[48,128]{1,0:T(8,128)(2,1)}, bf16[48,128]{1,0:T(8,128)(2,1)S(1)}, u32[]{:S(2)}, u32[]{:S(2)}) collective-permute-start(bf16[48,128]{1,0:T(8,128)(2,1)} %edges.1.refs_1_), channel_id=1, source_target_pairs={{0,24},{8,0},{16,8},{24,16},{1,25},{9,1},{17,9},{25,17},{2,26},{10... | collective-permute-start | bytes 36872 | tf_op jit(solution)/shard_map/ppermute | solution.py:592
  6.4 3.9 %collective-permute-start.1 = (bf16[48,128]{1,0:T(8,128)(2,1)}, bf16[48,128]{1,0:T(8,128)(2,1)S(1)}, u32[]{:S(2)}, u32[]{:S(2)}) collective-permute-start(bf16[48,128]{1,0:T(8,128)(2,1)} %edges.1.refs_1_), channel_id=1, source_target_pairs={{0,16},{8,24},{16,0},{24,8},{1,17},{9,25},{17,1},{25,9},{2,18},{10... | collective-permute-start | bytes 36872 | tf_op jit(solution)/shard_map/ppermute | solution.py:592
  6.9 4.8 %collective-permute-start = (bf16[48,128]{1,0:T(8,128)(2,1)}, bf16[48,128]{1,0:T(8,128)(2,1)S(1)}, u32[]{:S(2)}, u32[]{:S(2)}) collective-permute-start(bf16[48,128]{1,0:T(8,128)(2,1)} %edges.1.refs_1_), channel_id=1, source_target_pairs={{0,8},{8,16},{16,24},{24,0},{1,9},{9,17},{17,25},{25,1},{2,10},{10... | collective-permute-start | bytes 36872 | tf_op jit(solution)/shard_map/ppermute | solution.py:592
  8.0 7.2 %copy-start.2 = (bf16[48,128]{1,0:T(8,128)(2,1)}, bf16[48,128]{1,0:T(8,128)(2,1)S(1)}, u32[]{:S(2)}) copy-start(bf16[48,128]{1,0:T(8,128)(2,1)S(1)} %collective-permute-done.2.refs_4_) | copy-start | bytes 36868
  10.3 5.0 %copy-start.3 = (bf16[48,128]{1,0:T(8,128)(2,1)}, bf16[48,128]{1,0:T(8,128)(2,1)S(1)}, u32[]{:S(2)}) copy-start(bf16[48,128]{1,0:T(8,128)(2,1)S(1)} %collective-permute-done.1.refs_3_) | copy-start | bytes 36868
  11.7 3.6 %copy-start.4 = (bf16[48,128]{1,0:T(8,128)(2,1)}, bf16[48,128]{1,0:T(8,128)(2,1)S(1)}, u32[]{:S(2)}) copy-start(bf16[48,128]{1,0:T(8,128)(2,1)S(1)} %collective-permute-done.refs_2_) | copy-start | bytes 36868
  11.7 19.2 %collective-permute-start.5 = (bf16[5,128,128]{2,1,0:T(8,128)(2,1)}, bf16[5,128,128]{2,1,0:T(8,128)(2,1)S(1)}, u32[]{:S(2)}, u32[]{:S(2)}) collective-permute-start(bf16[5,128,128]{2,1,0:T(8,128)(2,1)} %bitcast.4), channel_id=1, source_target_pairs={{0,24},{8,0},{16,8},{24,16},{1,25},{9,1},{17,9},{25,17},{2,26},{10... | collective-permute-start | bytes 491528 | tf_op jit(solution)/shard_map/ppermute | solution.py:595
  11.8 19.1 %collective-permute-start.4 = (bf16[5,128,128]{2,1,0:T(8,128)(2,1)}, bf16[5,128,128]{2,1,0:T(8,128)(2,1)S(1)}, u32[]{:S(2)}, u32[]{:S(2)}) collective-permute-start(bf16[5,128,128]{2,1,0:T(8,128)(2,1)} %bitcast.5), channel_id=1, source_target_pairs={{0,16},{8,24},{16,0},{24,8},{1,17},{9,25},{17,1},{25,9},{2,18},{10... | collective-permute-start | bytes 491528 | tf_op jit(solution)/shard_map/ppermute | solution.py:595
  13.2 17.7 %collective-permute-start.3 = (bf16[5,128,128]{2,1,0:T(8,128)(2,1)}, bf16[5,128,128]{2,1,0:T(8,128)(2,1)S(1)}, u32[]{:S(2)}, u32[]{:S(2)}) collective-permute-start(bf16[5,128,128]{2,1,0:T(8,128)(2,1)} %bitcast.6), channel_id=1, source_target_pairs={{0,8},{8,16},{16,24},{24,0},{1,9},{9,17},{17,25},{25,1},{2,10},{10... | collective-permute-start | bytes 491528 | tf_op jit(solution)/shard_map/ppermute | solution.py:595
  18.2 6.5 %collective-permute-start.6 = (bf16[160,128]{1,0:T(8,128)(2,1)}, bf16[160,128]{1,0:T(8,128)(2,1)S(1)}, u32[]{:S(2)}, u32[]{:S(2)}) collective-permute-start(bf16[160,128]{1,0:T(8,128)(2,1)} %get-tuple-element.16.send_a), channel_id=1, source_target_pairs={{0,1},{1,0},{2,3},{3,2},{4,5},{5,4},{6,7},{7,6},{8,9},{9,8},{10,11... | collective-permute-start | bytes 122888 | tf_op jit(solution)/shard_map/ppermute | solution.py:609
  18.2 6.4 %collective-permute-start.7 = (bf16[160,128]{1,0:T(8,128)(2,1)}, bf16[160,128]{1,0:T(8,128)(2,1)S(1)}, u32[]{:S(2)}, u32[]{:S(2)}) collective-permute-start(bf16[160,128]{1,0:T(8,128)(2,1)} %get-tuple-element.17.send_b), channel_id=1, source_target_pairs={{0,7},{1,2},{2,1},{3,4},{4,3},{5,6},{6,5},{7,0},{8,15},{9,10},{10,... | collective-permute-start | bytes 122888 | tf_op jit(solution)/shard_map/ppermute | solution.py:610
  24.7 0.6 %copy-start = (bf16[160,128]{1,0:T(8,128)(2,1)}, bf16[160,128]{1,0:T(8,128)(2,1)S(1)}, u32[]{:S(2)}) copy-start(bf16[160,128]{1,0:T(8,128)(2,1)S(1)} %collective-permute-done.6.recv_a) | copy-start | bytes 122884
  24.7 0.6 %copy-start.1 = (bf16[160,128]{1,0:T(8,128)(2,1)}, bf16[160,128]{1,0:T(8,128)(2,1)S(1)}, u32[]{:S(2)}) copy-start(bf16[160,128]{1,0:T(8,128)(2,1)S(1)} %collective-permute-done.7.recv_b) | copy-start | bytes 122884
  30.9 0.7 %copy-start.5 = (bf16[5,128,128]{2,1,0:T(8,128)(2,1)}, bf16[5,128,128]{2,1,0:T(8,128)(2,1)S(1)}, u32[]{:S(2)}) copy-start(bf16[5,128,128]{2,1,0:T(8,128)(2,1)S(1)} %collective-permute-done.5.refs_6_) | copy-start | bytes 491524
  30.9 0.7 %copy-start.6 = (bf16[5,128,128]{2,1,0:T(8,128)(2,1)}, bf16[5,128,128]{2,1,0:T(8,128)(2,1)S(1)}, u32[]{:S(2)}) copy-start(bf16[5,128,128]{2,1,0:T(8,128)(2,1)S(1)} %collective-permute-done.4.refs_5_) | copy-start | bytes 491524
  30.9 0.7 %copy-start.7 = (bf16[5,128,128]{2,1,0:T(8,128)(2,1)}, bf16[5,128,128]{2,1,0:T(8,128)(2,1)S(1)}, u32[]{:S(2)}) copy-start(bf16[5,128,128]{2,1,0:T(8,128)(2,1)S(1)} %collective-permute-done.3.refs_4_) | copy-start | bytes 491524
  45.9 1.4 %collective-permute-start.8 = (f32[8,128]{1,0:T(8,128)}, f32[8,128]{1,0:T(8,128)S(1)}, u32[]{:S(2)}, u32[]{:S(2)}) collective-permute-start(f32[8,128]{1,0:T(8,128)} %get-tuple-element.25), channel_id=1, source_target_pairs={{0,1},{1,0},{2,3},{3,2},{4,5},{5,4},{6,7},{7,6},{8,9},{9,8},{10,11... | collective-permute-start | bytes 12296 | tf_op jit(solution)/shard_map/ppermute | solution.py:565
  48.0 3.6 %collective-permute-start.9 = (f32[8,128]{1,0:T(8,128)S(1)}, f32[8,128]{1,0:T(8,128)S(1)}, u32[]{:S(2)}, u32[]{:S(2)}) collective-permute-start(f32[8,128]{1,0:T(8,128)S(1)} %add.9), channel_id=1, source_target_pairs={{0,2},{1,3},{2,0},{3,1},{4,6},{5,7},{6,4},{7,5},{8,10},{9,11},{10,... | collective-permute-start | bytes 12296 | tf_op jit(solution)/shard_map/ppermute | solution.py:565
  51.6 4.5 %collective-permute-start.10 = (f32[8,128]{1,0:T(8,128)S(1)}, f32[8,128]{1,0:T(8,128)S(1)}, u32[]{:S(2)}, u32[]{:S(2)}) collective-permute-start(f32[8,128]{1,0:T(8,128)S(1)} %add.10), channel_id=1, source_target_pairs={{0,4},{1,5},{2,6},{3,7},{4,0},{5,1},{6,2},{7,3},{8,12},{9,13},{10,... | collective-permute-start | bytes 12296 | tf_op jit(solution)/shard_map/ppermute | solution.py:565

commit v2 on v1

v2 whole, which is shorter than its diff:
```python
import functools
import math

import jax
import jax.numpy as jnp
import numpy as np
from jax import lax
from jax.experimental import pallas as pl
from jax.experimental.pallas import tpu as pltpu
from jax.sharding import PartitionSpec as P

FIELDS = 5
BLADES = 96
AMP = 4
GRP_DEV = 2
STEPS = 3
PAIRS = GRP_DEV * AMP

time_step = 0.25
second_diff = 0.1
fourth_diff = 0.02
link_weight = 0.5
two_pi = 2.0 * math.pi

C0 = 1.0 - time_step * (2.0 * second_diff + 6.0 * fourth_diff + link_weight)
C1 = time_step * (second_diff + 4.0 * fourth_diff)
C2 = -time_step * fourth_diff
CP = time_step * link_weight
CM = 0.5 * time_step
CU = 0.25 * time_step

FW = 6
QW = 4
PARTS = 3
SLOT = 32
LINK_ROW = PARTS * FW
SEG = 16
HALF = SEG // 2
VMEM_LIMIT = 40 * 2**20
SMALL_LIMIT = 16 * 2**20

VMEM = pl.BlockSpec(memory_space=pltpu.VMEM)
SMEM = pl.BlockSpec(memory_space=pltpu.SMEM)
HBM = pl.BlockSpec(memory_space=pltpu.HBM)
UNIT = time_step * fourth_diff
CENTRE = round(C0 / UNIT)
NEAR = round(C1 / UNIT)
F32 = jnp.float32
BF16 = jnp.bfloat16
NT = (((1,), (1,)), ((), ()))
TN = (((0,), (0,)), ((), ()))
NN = (((1,), (0,)), ((), ()))


def mm(a, b, dims=NN):
    return lax.dot_general(a, b, dims, preferred_element_type=F32)


def split3(x):
    hi = x.astype(BF16)
    rest = x - hi.astype(F32)
    mid = rest.astype(BF16)
    return hi, mid, (rest - mid.astype(F32)).astype(BF16)


def exact_mm(a, x):
    hi, mid, lo = split3(x)
    return mm(a, hi) + mm(a, mid) + mm(a, lo)


def fetch(moves, sems):
    copies = [pltpu.make_async_copy(src, dst, sems.at[i]) for i, (src, dst) in enumerate(moves)]
    for copy in copies:
        copy.start()
    return copies


def arrive(copies):
    for copy in copies:
        copy.wait()


def like(x):
    return pltpu.VMEM(x.shape, x.dtype)


def cost(flops, moved):
    return pl.CostEstimate(flops=flops, bytes_accessed=moved, transcendentals=0)


def forcing_select(width):
    out = np.zeros((PARTS, width, width), np.float32)
    for part in range(PARTS):
        for j in range(FW):
            out[part, j, part * FW + j] = 1.0
            out[part, width - FW + j, SLOT + part * FW + j] = 1.0
    return out.reshape(PARTS * width, width).astype(jnp.bfloat16)


def state_select(width):
    out = np.zeros((2 * SLOT, STEPS, width), np.float32)
    for n in range(STEPS):
        for j in range(QW):
            out[n * QW + j, n, j] = 1.0
            out[SLOT + n * QW + j, n, width - QW + j] = 1.0
    return out.reshape(2 * SLOT, STEPS * width).astype(jnp.bfloat16)


def give(send_a, send_b, f, both):
    even = lax.axis_index("blk") % 2 == 0
    left, right = both[:SLOT], both[SLOT:]
    send_a[f * SLOT : (f + 1) * SLOT] = jnp.where(even, right, left).astype(BF16)
    send_b[f * SLOT : (f + 1) * SLOT] = jnp.where(even, left, right).astype(BF16)


def strips_kernel(n_out, *refs):
    owner = refs[0]
    slots = refs[1 : 1 + n_out]
    sel, send_a, send_b, *chosen = refs[1 + n_out :]
    me = lax.axis_index("out")
    for n, target in enumerate(chosen):
        which = (me - owner[n] + n_out) % n_out
        for s, slot in enumerate(slots):

            @pl.when(which == s)
            def _():
                target[...] = slot[...]

    for f in range(FIELDS):
        give(send_a, send_b, f, mm(sel[...], jnp.concatenate([q[f] for q in chosen], axis=1), NT))


def column_factor(columns, pair, start, total, group_base, blade_group):
    scaled = columns * BLADES
    first = ((start + total - HALF) * BLADES) // total - BLADES
    group = jnp.full(columns.shape, -1, jnp.int32)
    numerator = jnp.zeros(columns.shape, jnp.int32)
    width = columns.shape[-1]
    for j in range((width + SEG) * BLADES // total + 2):
        blade = first + j
        inside = (scaled >= blade * total) & (scaled < (blade + 1) * total)
        group = jnp.where(inside, blade_group[(blade + BLADES) % BLADES], group)
        numerator = jnp.where(inside, scaled - blade * total, numerator)
    phase = numerator.astype(F32) / total
    amp = pair & (AMP - 1)
    order = ((amp >> 1) + 1).astype(F32)
    angle = two_pi * order * phase
    harmonic = jnp.where((amp & 1) == 0, jnp.cos(angle), jnp.sin(angle))
    return jnp.where(group == group_base + pair // AMP, harmonic, 0.0)


def flux(fm, q, d):
    inner = q[0] * d[0]
    for f in range(1, FIELDS):
        inner = inner + q[f] * d[f]
    u = q[1] * CU
    out = []
    for e in range(FIELDS):
        value = u * d[e]
        for f in range(FIELDS):
            value = value + fm[f, e] * d[f]
        if e == 1:
            value = value + CU * inner
        out.append(value)
    return out


def prepare_kernel(cycle, blade_group, link_s, *refs):
    owner, fm = refs[:2]
    kept = refs[2 : (len(refs) - 11) // 2 + 2]
    k_ref, kp_ref, b0_ref, send_a, send_b, inv_ref, owner_out, fm_out, *held, sems = refs[
        2 + len(kept) :
    ]
    copies = fetch(zip(kept, held), sems)
    for i in range(owner.shape[0]):
        owner_out[i] = owner[i]
    for f in range(FIELDS):
        for e in range(FIELDS):
            fm_out[f, e] = fm[f, e]
    forcing, link, sel = held[:3]
    rows, width = forcing.shape[1:]
    total = cycle * width
    start = lax.axis_index("blk") * width

    def invert(r, c):
        inv_ref[link_s[r]] = r
        return c

    lax.fori_loop(0, rows, invert, 0, unroll=8)
    lane = lax.broadcasted_iota(jnp.int32, (8, width), 1)
    sub = lax.broadcasted_iota(jnp.int32, (8, width), 0)
    p = lane & (SEG - 1)
    packed = jnp.where(p < HALF, p - QW, width - QW + p - HALF) + start
    args = (start, total, lax.axis_index("out") * GRP_DEV, blade_group)
    for i in range(5):
        k_ref[i] = column_factor(lane + start + (i - 2), sub, *args)
        kp_ref[i] = column_factor(packed + (i - 2), sub, *args)
    arrive(copies[:3])
    links = link[...].astype(F32)
    parts = [split3(forcing[f]) for f in range(FIELDS)]
    linked = mm(one_hot(links, rows), jnp.concatenate(sum(parts, ()), axis=1))
    chosen = mm(
        jnp.concatenate([jnp.concatenate(three, axis=1) for three in parts], axis=0), sel[...]
    )
    row = lax.broadcasted_iota(jnp.int32, (2 * SLOT, rows), 0)
    links = jnp.broadcast_to(links, row.shape)
    for f in range(FIELDS):
        three = [
            linked[:, (f * PARTS + i) * width : (f * PARTS + i + 1) * width] for i in range(PARTS)
        ]
        b0_ref[f] = (C0 + 1.0) * forcing[f] + CP * (three[0] + three[1] + three[2])
        turned = chosen[f * rows : (f + 1) * rows].T[: 2 * SLOT]
        if f == 0:
            turned = jnp.where(row % SLOT == LINK_ROW, links, turned)
        give(send_a, send_b, f, turned)
    arrive(copies[3:])


def one_hot(links, rows):
    row = lax.broadcasted_iota(jnp.int32, (rows, rows), 0).astype(F32)
    return jnp.where(links == row, 1.0, 0.0).astype(BF16)


def halo_selects(width):
    blocks = width // SEG
    forcing_sel = np.zeros((4 * SLOT, 5, SEG), np.float32)
    state_sel = np.zeros((4 * SLOT, 2, SEG), np.float32)
    edge = np.zeros((4 * SLOT, width), np.float32)

    def place(column, size):
        if column < 0:
            return 0, column + size
        if column < size:
            return 1, column
        if column < width:
            return 2, column - (width - size)
        return 3, column - width

    def forcing_rows(column):
        source, j = place(column, FW)
        return [source * SLOT + part * FW + j for part in range(PARTS)] if 0 <= j < FW else []

    for p in range(SEG):
        column = p - QW if p < HALF else width - QW + p - HALF
        for i in range(5):
            for row in forcing_rows(column + i - 2):
                forcing_sel[row, i, p] = 1.0
        source, j = place(column, QW)
        for i, n in ((0, STEPS - 1), (1, STEPS - 2)):
            state_sel[source * SLOT + n * QW + j, i, p] = 1.0
    for lane, column in ((width - 2, -2), (width - 1, -1), (0, width), (1, width + 1)):
        for row in forcing_rows(column):
            edge[row, lane] = 1.0

    def tiled(x):
        return np.repeat(x[:, :, None, :], blocks, axis=2).reshape(4 * SLOT, -1)

    return tuple(x.astype(jnp.bfloat16) for x in (tiled(forcing_sel), tiled(state_sel), edge))


def stencil_selects(width):
    blocks = width // SEG
    inner = np.zeros((2, width, 2 * width), np.float32)
    outer = np.zeros((blocks, 2, width, 2 * width), np.float32)

    def spread(column):
        out = []
        for c, w in ((column + 1, 1.0), (column - 1, -1.0)):
            if 0 <= c < width:
                out.append((c, w))
        for c, w in (
            (column, CENTRE),
            (column - 1, NEAR),
            (column + 1, NEAR),
            (column - 2, -1.0),
            (column + 2, -1.0),
        ):
            if 0 <= c < width:
                out.append((width + c, w))
        return out

    for column in range(width):
        for lane, w in spread(column):
            inner[:, column, lane] = w
    for j in range(blocks):
        for p, column in ((2, -2), (3, -1), (HALF + QW, width), (HALF + QW + 1, width + 1)):
            for lane, w in spread(column):
                outer[j, :, j * SEG + p, lane] = w
    return (
        inner.reshape(2 * width, 2 * width).astype(jnp.bfloat16),
        outer.reshape(blocks, 2 * width, 2 * width)
        .swapaxes(0, 1)
        .reshape(2 * width, blocks * 2 * width)
        .astype(jnp.bfloat16),
    )


def halves(x):
    hi = x.astype(BF16)
    return jnp.concatenate([hi, (x - hi.astype(F32)).astype(BF16)], axis=1)


def gather_sources(sa, sb, ra, rb):
    even = lax.axis_index("blk") % 2 == 0
    sa, sb, ra, rb = (x[...].astype(F32) for x in (sa, sb, ra, rb))
    own_left, own_right = jnp.where(even, sb, sa), jnp.where(even, sa, sb)
    left, right = jnp.where(even, rb, ra), jnp.where(even, ra, rb)
    turned = []
    for f in range(FIELDS):
        s = slice(f * SLOT, (f + 1) * SLOT)
        g = jnp.concatenate([left[s], own_left[s], own_right[s], right[s]], axis=0)
        turned.append(g.T.astype(BF16))
    return left, right, turned


def in_segments(sets, tiled, big, step):
    blocks = big.shape[0] // (4 * SLOT)
    width = blocks * SEG
    lane_block = lax.broadcasted_iota(jnp.int32, tiled.shape, 1) % width // SEG
    for j in range(blocks):
        big[j * 4 * SLOT : (j + 1) * 4 * SLOT, :] = jnp.where(
            lane_block == j, tiled[...].astype(F32), 0.0
        ).astype(BF16)
    pieces = []
    for x in sets:
        for f in range(FIELDS):
            mine = x[:, f * 4 * SLOT : (f + 1) * 4 * SLOT]
            pieces.append(
                jnp.concatenate([mine[j * step : (j + 1) * step] for j in range(blocks)], axis=1)
            )
    y = mm(jnp.concatenate(pieces, axis=0), big[...])

    def part(i, f, which):
        start = (i * FIELDS + f) * step
        return y[start : start + step, which * width : (which + 1) * width]

    return part


def left_lanes(step, width):
    return lax.broadcasted_iota(jnp.int32, (step, width), 1) & (SEG - 1) < HALF


def halo_forcing_kernel(fm, link, sa, sb, ra, rb, tiled, edge, y_ref, fe_ref, hot_ref, big):
    rows, width = link.shape[1], edge.shape[1]
    step = rows // (width // SEG)
    left, right, turned = gather_sources(sa, sb, ra, rb)
    hot = jnp.concatenate(
        [
            one_hot(left[LINK_ROW : LINK_ROW + 1], rows),
            one_hot(link[...].astype(F32), rows),
            one_hot(right[LINK_ROW : LINK_ROW + 1], rows),
        ],
        axis=0,
    )
    hot_ref[...] = hot
    k_wide = 4 * SLOT
    source = lax.broadcasted_iota(jnp.int32, (rows, FIELDS * k_wide), 1) % k_wide // SLOT

    def permuted(x):
        y = mm(hot, x)
        by_left, by_right = y[:rows], y[2 * rows :]
        outer = jnp.where(source == 0, by_left, by_right)
        by_tile = jnp.where((source == 1) | (source == 2), y[rows : 2 * rows], outer)
        return by_left.astype(BF16), by_right.astype(BF16), by_tile.astype(BF16)

    fe = mm(jnp.concatenate(turned, axis=0), edge[...])
    for f in range(FIELDS):
        fe_ref[f] = fe[f * rows : (f + 1) * rows]
    g = jnp.concatenate(turned, axis=1)
    by_left, by_right, by_tile = permuted(g)
    part = in_segments((g, by_tile, permuted(by_tile)[2], by_left, by_right), tiled, big, step)
    is_left = left_lanes(step, width)

    def at(linked, f, which):
        if linked:
            return jnp.where(is_left, part(3, f, which), part(4, f, which))
        return part(0, f, which)

    for i in range(2):
        shifted = [[at(i, f, d) for f in range(FIELDS)] for d in range(5)]
        for f in range(FIELDS):
            minus = sum(fm[e, f] * CM * shifted[1][e] for e in range(FIELDS))
            plus = sum(fm[e, f] * CM * shifted[3][e] for e in range(FIELDS))
            b = (
                C2 * shifted[0][f],
                C1 * shifted[1][f] - minus,
                (C0 + 1.0) * shifted[2][f] + CP * part(i + 1, f, 2),
                C1 * shifted[3][f] + plus,
                C2 * shifted[4][f],
                shifted[1][f],
                shifted[3][f],
                shifted[2][f],
            )
            for d, value in enumerate(b):
                y_ref[i * 8 + d, f] = value


def halo_kernel(fm, sa, sb, ra, rb, tiled, kp_ref, hot, y_in, e1_ref, e2_ref, y_ref, big, q_ref, fmc):
    for i in (1, 3, 9, 11):
        y_ref[i] = y_in[i]
    rows, width = hot.shape[1], kp_ref.shape[2]
    step = rows // (width // SEG)
    for f in range(FIELDS):
        for e in range(FIELDS):
            fmc[f, e] = fm[f, e] * CM
    _, _, turned = gather_sources(sa, sb, ra, rb)
    g = jnp.concatenate(turned, axis=1)
    y = mm(hot[...], g).astype(BF16)
    part = in_segments((g, y[:rows], y[2 * rows :]), tiled, big, step)
    is_left = left_lanes(step, width)
    for i in range(2):
        if i:
            q2 = [jnp.where(is_left, part(1, f, 0), part(2, f, 0)) for f in range(FIELDS)]
        else:
            q2 = [part(0, f, 0) for f in range(FIELDS)]
        u = CU * q2[1]
        for d, near, sign in ((1, 5, -1.0), (3, 6, 1.0)):
            inner = sum(q2[f] * y_in[i * 8 + near, f] for f in range(FIELDS))
            for f in range(FIELDS):
                value = u * y_in[i * 8 + near, f]
                if f == 1:
                    value = value + CU * inner
                y_ref[i * 8 + d, f] = y_ref[i * 8 + d, f] + sign * value
    for f in range(FIELDS):
        q_ref[f] = part(0, f, 1)
    kp = [kp_ref[i] for i in range(5)]

    def body(r, c):
        def row(ref, index):
            return jnp.broadcast_to(ref[(*index, pl.ds(r, 1), slice(None))], (8, width))

        mu, linked, d, base = [], [], [], []
        for f in range(FIELDS):
            for i, out in ((0, mu), (8, linked)):
                value = row(y_in, (i, f)) * kp[0]
                for n in range(1, 5):
                    value = value + row(y_ref if n % 2 else y_in, (i + n, f)) * kp[n]
                out.append(value)
            x = mu[f]
            m1, p1 = pltpu.roll(x, 1, 1), pltpu.roll(x, width - 1, 1)
            m2, p2 = pltpu.roll(x, 2, 1), pltpu.roll(x, width - 2, 1)
            d.append(m1 - p1)
            base.append(
                C0 * x + C1 * (m1 + p1) + C2 * (m2 + p2) + CP * linked[f]
                + row(y_in, (7, f)) * kp[2]
            )
        moved = flux(fmc, [row(q_ref, (f,)) for f in range(FIELDS)], d)
        at = pl.ds(pl.multiple_of(r * (FIELDS * 8), 8), FIELDS * 8)
        e1_ref[at, :] = halves(jnp.concatenate(mu, axis=0))
        e2_ref[at, :] = halves(
            jnp.concatenate([b - m for b, m in zip(base, moved)], axis=0)
        )
        return c

    lax.fori_loop(0, step, body, 0, unroll=8)


def main_kernel(
    cycle, fm, inv, forcing, fe, b0, k_ref, inner, outer, e1, e2, q0, q1, q2,
    out_hbm, sens_ref,
    bs, coef, mu1, mu2, dz, dze, stage, weighted, fmc, out_sems,
):
    rows, width = forcing.shape[1], forcing.shape[2]
    total = cycle * width

    for f in range(FIELDS):
        for e in range(FIELDS):
            fmc[f, e] = fm[f, e] * CM
    lane = lax.broadcasted_iota(jnp.int32, (8, width), 1)
    start = lax.axis_index("blk") * width
    weight = 1.0 + 2.0 * (lane + start).astype(F32) / total
    norm = 1.0 / math.sqrt(FIELDS * rows * total)

    def around(x, edge):
        return (
            pltpu.roll(jnp.where(lane == width - 1, edge, x), 1, 1),
            pltpu.roll(jnp.where(lane == 0, edge, x), width - 1, 1),
            pltpu.roll(jnp.where(lane >= width - 2, edge, x), 2, 1),
            pltpu.roll(jnp.where(lane < 2, edge, x), width - 2, 1),
        )

    def dense(i, z):
        rs = pl.ds(pl.multiple_of(i * 16, 16), 16)
        q = [q2[f, rs, :].astype(F32) for f in range(FIELDS)]
        for half in range(2):
            r8 = pl.ds(pl.multiple_of(i * 16 + half * 8, 8), 8)
            near = [around(forcing[f, r8, :], fe[f, r8, :]) for f in range(FIELDS)]
            mine = [x[half * 8 : half * 8 + 8] for x in q]
            minus = flux(fmc, mine, [a[0] for a in near])
            plus = flux(fmc, mine, [a[1] for a in near])
            for f in range(FIELDS):
                m1, p1, m2, p2 = near[f]
                bs[0, f, r8, :] = C2 * m2
                bs[1, f, r8, :] = C1 * m1 - minus[f]
                bs[2, f, r8, :] = C1 * p1 + plus[f]
                bs[3, f, r8, :] = C2 * p2
                w = forcing[f, r8, :] * weight
                weighted[f, r8, :] = w
                z = z + w * forcing[f, r8, :]
        return z

    def coefficients(i, c):
        rs = pl.ds(pl.multiple_of(i * 16, 16), 16)
        for n, q_ref in enumerate((q0, q1)):
            q = [q_ref[f, rs, :].astype(F32) for f in range(FIELDS)]
            u = CU * q[1]
            for e in range(FIELDS):
                coef[n, e, rs, :] = (u if e != 1 else u + u) + fmc[e, e]
            for j, f in enumerate((0, 2, 3, 4)):
                coef[n, FIELDS + j, rs, :] = CU * q[f] + fmc[f, 1]
        return c

    zero = jnp.zeros((8, width), F32)
    z = lax.fori_loop(0, rows // 16, dense, zero)
    lax.fori_loop(0, rows // 16, coefficients, 0)
    k = [k_ref[i] for i in range(5)]

    def spread(ref, index, r):
        return jnp.broadcast_to(ref[(*index, pl.ds(r, 1), slice(None))], (8, width))

    def place(r, f):
        return pl.ds(pl.multiple_of((r * FIELDS + f) * 8, 8), 8)

    def first(i, acc):
        acc = list(acc)
        for j in range(8):
            r = i * 8 + j
            for f in range(FIELDS):
                value = spread(bs, (0, f), r) * k[0] + spread(bs, (1, f), r) * k[1]
                value = value + spread(b0, (f,), r) * k[2] + spread(bs, (2, f), r) * k[3]
                value = value + spread(bs, (3, f), r) * k[4]
                mu1[place(r, f), :] = value
                acc[f] = acc[f] + value * spread(weighted, (f,), r)
        return tuple(acc)

    acc = lax.fori_loop(0, rows // 8, first, (zero,) * FIELDS)

    blocks = width // SEG
    size = rows // blocks
    fmv = [[jnp.full((8, width), fmc[f, e]) for e in range(FIELDS)] for f in range(FIELDS)]

    def products(source, edges):
        dz[...] = mm(halves(source[...]), inner[...])
        dze[...] = mm(edges[...], outer[...])

    def row(n, source, j, i, acc, keep):
        r = j * size + i
        linked = inv[r]
        chunk = i * FIELDS * 8

        def both(f, half):
            own = dz[place(r, f), half * width : (half + 1) * width]
            lanes = pl.ds(pl.multiple_of(j * (2 * width) + half * width, width), width)
            return own + dze[chunk + f * 8 : chunk + f * 8 + 8, lanes]

        d = [both(f, 0) for f in range(FIELDS)]
        for e in range(FIELDS):
            value = UNIT * both(e, 1) + CP * source[place(linked, e), :]
            for f in range(FIELDS):
                if f == e:
                    m = spread(coef, (n, e), r)
                elif e == 1:
                    m = spread(coef, (n, FIELDS + (0, 2, 3, 4).index(f)), r)
                else:
                    m = fmv[f][e]
                value = value - m * d[f]
            value = keep(r, e, value)
            acc[e] = acc[e] + value * spread(weighted, (e,), r)

    def second(j, acc):
        acc = list(acc)

        def keep(r, e, value):
            value = value + spread(forcing, (e,), r) * k[2]
            mu2[place(r, e), :] = value
            return value

        for i in range(size):
            row(1, mu1, j, i, acc, keep)
        return tuple(acc)

    products(mu1, e1)
    acc = lax.fori_loop(0, blocks, second, acc)

    def send(j):
        at = pl.ds(pl.multiple_of(j * size, size), size)
        return pltpu.make_async_copy(stage.at[:, at, :], out_hbm.at[:, at, :], out_sems.at[j])

    def third(j, acc):
        acc = list(acc)
        for part in range(size // 8):
            made = [[] for _ in range(FIELDS)]

            def keep(r, e, value):
                made[e].append(value)
                return value

            for i in range(8):
                row(0, mu2, j, part * 8 + i, acc, keep)
            at = pl.ds(pl.multiple_of(j * size + part * 8, 8), 8)
            for e in range(FIELDS):
                turned = jnp.swapaxes(jnp.stack(made[e]), 0, 1)
                for pair in range(PAIRS):
                    stage[pair * FIELDS + e, at, :] = turned[pair]
        send(j).start()
        return tuple(acc)

    products(mu2, e2)
    acc = lax.fori_loop(0, blocks, third, acc)
    source_part = jnp.sum(z, axis=0, keepdims=True) * k[2]
    acc = (sum(acc) - 2.0 * source_part) * norm
    acc = jnp.broadcast_to(jnp.sum(acc, axis=1, keepdims=True), (8, width))
    sub = lax.broadcasted_iota(jnp.int32, (8, width), 0)
    for group in range(GRP_DEV):
        mine = jnp.where(sub == group * AMP + lane, acc, 0.0)
        sens_ref[group : group + 1, :] = jnp.sum(mine, axis=0, keepdims=True)[:, :AMP]
    for j in range(blocks):
        send(j).wait()


def shift_pairs(devices, k):
    return [(i, (i + k) % devices) for i in range(devices)]


def total_over(x, axis):
    devices = lax.axis_size(axis)
    if devices & (devices - 1):
        return lax.psum(x, axis)
    bit = 1
    while bit < devices:
        x = x + lax.ppermute(x, axis, [(i, i ^ bit) for i in range(devices)])
        bit *= 2
    return x


def to_neighbours(send_a, send_b, cycle):
    return (
        lax.ppermute(send_a, "blk", [(i, i ^ 1) for i in range(cycle)]),
        lax.ppermute(
            send_b,
            "blk",
            [(i, (i + 1) % cycle if i % 2 else (i - 1) % cycle) for i in range(cycle)],
        ),
    )


def on_device(checkpoints, owner, flux_matrix, row_link, blade_group, forcing):
    n_out = lax.axis_size("out")
    cycle = lax.axis_size("blk")
    rows, width = forcing.shape[1], forcing.shape[2]
    blocks = width // SEG
    step_rows = rows // blocks
    slot = checkpoints[0]

    def struct(shape, kind=F32):
        return jax.ShapeDtypeStruct(shape, kind)

    sems = pltpu.SemaphoreType.DMA
    field = struct((FIELDS, rows, width))
    strip = struct((FIELDS * SLOT, rows), BF16)
    factors = struct((5, PAIRS, width))
    slots = [slot] + [lax.ppermute(slot, "out", shift_pairs(n_out, k)) for k in range(1, n_out)]

    def stay(x):
        return pltpu.with_memory_space_constraint(x, pltpu.HBM)

    def call(kernel, out_shape, smem, hbm, vmem, scratch, limit, flops, name, out_specs=None):
        return pl.pallas_call(
            kernel,
            out_shape=out_shape,
            in_specs=[SMEM] * len(smem) + [HBM] * len(hbm) + [VMEM] * len(vmem),
            out_specs=out_specs or (VMEM,) * len(out_shape),
            scratch_shapes=scratch,
            compiler_params=pltpu.CompilerParams(vmem_limit_bytes=limit),
            cost_estimate=cost(flops, 10**6),
            name=name,
        )(*map(stay, smem), *map(stay, hbm), *vmem)

    kept = (
        forcing, row_link, forcing_select(width), slot, state_select(width),
        *halo_selects(width), *stencil_selects(width),
    )
    made = (
        factors, factors, field, strip, strip,
        struct((rows,), jnp.int32), struct(owner.shape, jnp.int32), struct(flux_matrix.shape),
    )
    made += tuple(struct(x.shape, x.dtype) for x in kept)
    k, kp, b0, f_a, f_b, inv, owner_s, fm_s, *held = call(
        functools.partial(prepare_kernel, cycle),
        made,
        (blade_group, row_link[0], owner, flux_matrix),
        kept,
        (),
        [sems((len(kept),))],
        SMALL_LIMIT,
        10**8,
        "prepare",
        (VMEM,) * 5 + (SMEM,) * 3 + (VMEM,) * len(kept),
    )
    forcing_v, link, _, slot_v, state_sel, forcing_tiled, state_tiled, edge, inner, outer = held
    f_sent = (f_a, f_b, *to_neighbours(f_a, f_b, cycle))

    q_a, q_b, *chosen = call(
        functools.partial(strips_kernel, n_out),
        (strip, strip) + (struct(slot.shape, slot.dtype),) * STEPS,
        (owner_s,),
        (),
        (slot_v, *slots[1:], state_sel),
        [],
        SMALL_LIMIT,
        10**7,
        "strips",
    )
    q_sent = (q_a, q_b, *to_neighbours(q_a, q_b, cycle))

    y, fe, hot = call(
        halo_forcing_kernel,
        (struct((16, FIELDS, step_rows, width)), field, struct((3 * rows, rows), BF16)),
        (fm_s,),
        (),
        (link, *f_sent, forcing_tiled, edge),
        [pltpu.VMEM((blocks * 4 * SLOT, forcing_tiled.shape[1]), BF16)],
        SMALL_LIMIT,
        10**8,
        "halo_forcing",
    )
    edge_struct = struct((step_rows * FIELDS * 8, 2 * width), BF16)
    e1, e2 = call(
        halo_kernel,
        (edge_struct, edge_struct),
        (fm_s,),
        (),
        (*q_sent, state_tiled, kp, hot, y),
        [
            like(y),
            pltpu.VMEM((blocks * 4 * SLOT, state_tiled.shape[1]), BF16),
            pltpu.VMEM((FIELDS, step_rows, width), F32),
            pltpu.SMEM((FIELDS, FIELDS), F32),
        ],
        SMALL_LIMIT,
        10**8,
        "halo",
    )
    pairs_fields = PAIRS * FIELDS
    flat = rows * FIELDS * PAIRS
    adjoint, sens = call(
        functools.partial(main_kernel, cycle),
        (struct((pairs_fields, rows, width)), struct((GRP_DEV, AMP))),
        (fm_s, inv),
        (),
        (forcing_v, fe, b0, k, inner, outer, e1, e2, *chosen),
        [
            pltpu.VMEM((4, FIELDS, rows, width), F32),
            pltpu.VMEM((STEPS - 1, 2 * FIELDS - 1, rows, width), F32),
            pltpu.VMEM((flat, width), F32),
            pltpu.VMEM((flat, width), F32),
            pltpu.VMEM((flat, 2 * width), F32),
            pltpu.VMEM((flat // blocks, blocks * 2 * width), F32),
            pltpu.VMEM((pairs_fields, rows, width), F32),
            pltpu.VMEM((FIELDS, rows, width), F32),
            pltpu.SMEM((FIELDS, FIELDS), F32),
            sems((blocks,)),
        ],
        VMEM_LIMIT,
        10**9,
        "steps",
        (HBM, VMEM),
    )

    return adjoint.reshape(GRP_DEV, AMP, FIELDS, rows, width), total_over(sens, "blk")


def solution(mesh):
    return jax.shard_map(
        on_device,
        mesh=mesh,
        in_specs=(P("out", None, None, "blk"), P(), P(), P("blk", None), P(), P(None, None, "blk")),
        out_specs=(P("out", None, None, None, "blk"), P("out", None)),
        check_vma=False,
    )
```

time: 57.3 us -> 45.2 us (0.79)
  Pallas kernels: 27.2 us -> 20.4 us
  waiting for transfers between devices: 12.4 us -> 8.82 us
  local copies, waits for them, and re-layouts: 2.12 us -> 0.02 us
  starting transfers between devices: 13.7 us -> 14.4 us
    pallas_call x5, Pallas kernels: 27.2 us -> 20.4 us  [call(): pl.pallas_call(kernel, out_shape=out_shape, in_specs=[SMEM] * len(smem) +...]
    ppermute x8 -> x7, waiting for transfers between devices: 4.22 us -> 1.35 us  [the longest x3 1.34 us: on_device(): lax.ppermute(slot, 'out', shift_pairs(n_out, k))]
    unnamed x16 -> x6, local copies, waits for them, and re-layouts: 1.36 us -> 0.02 us
    ppermute x3, waiting for transfers between devices: 8.19 us -> 7.47 us  [total_over(): x = x + lax.ppermute(x, axis, [(i, i ^ bit) for i in range(devices)])]
    another operation x1 -> x0, local copies, waits for them, and re-layouts: 0.65 us -> none  [on_device(): sens = total_over(sens, 'blk')[:, 0].reshape(GRP_DEV, AMP)]
    ppermute x8 -> x7, starting transfers between devices: 12.4 us -> 12.6 us  [the longest x2 7.41 us: to_neighbours(): lax.ppermute(send_b, 'blk', [(i, (i + 1) % cycle if i % 2 else (i - 1) %...]
  transfers between devices with their start and end apart: 11 -> 10, of which waited for: 6 -> 4; matrix products, arithmetic and copies ran while one was open for 0% -> 0% of each run, Pallas kernels for 20% -> 14%
where the time goes in v2:
time: 45.2 us; the launch traced here: 44.9 us
  Pallas kernels  20.4 us (45%)
  starting transfers between devices  14.4 us (32%)
  waiting for transfers between devices  8.82 us (20%)
  between operations  0.75 us (2%)
  other arithmetic  0.57 us (1%)
    pallas_call x5, Pallas kernels, call(): pl.pallas_call(kernel, out_shape=out_shape, in_specs=[SMEM] * len(smem) +...  20.4 us
    ppermute x3, waiting for transfers between devices, total_over(): x = x + lax.ppermute(x, axis, [(i, i ^ bit) for i in range(devices)])  7.47 us
    ppermute x2, starting transfers between devices, to_neighbours(): lax.ppermute(send_b, 'blk', [(i, (i + 1) % cycle if i % 2 else (i - 1) %...  7.41 us
    ppermute x3, starting transfers between devices, on_device(): lax.ppermute(slot, 'out', shift_pairs(n_out, k))  5.04 us
    ppermute x3, starting transfers between devices, total_over(): x = x + lax.ppermute(x, axis, [(i, i ^ bit) for i in range(devices)])  1.76 us
    ppermute x3, waiting for transfers between devices, on_device(): lax.ppermute(slot, 'out', shift_pairs(n_out, k))  1.34 us
  transfers between devices with their start and end apart: 10, of which 4 were waited for; matrix products, arithmetic and copies ran while one was open for 0% of the time, Pallas kernels for 14%

profile of v2, /device:TPU:0, one launch (start us, length us, event | category | flops | bytes accessed | tf_op | source)
XLA Modules:
  0.0 44.9 jit_solution(11421975088914117311)
XLA Ops:
  0.6 3.9 %collective-permute-start.4 = (bf16[5,128,128]{2,1,0:T(8,128)(2,1)}, bf16[5,128,128]{2,1,0:T(8,128)(2,1)S(1)}, u32[]{:S(2)}, u32[]{:S(2)}) collective-permute-start(bf16[5,128,128]{2,1,0:T(8,128)(2,1)} %bitcast.3), channel_id=1, source_target_pairs={{0,24},{8,0},{16,8},{24,16},{1,25},{9,1},{17,9},{25,17},{2,26},{10... | collective-permute-start | bytes 491528 | tf_op jit(solution)/shard_map/ppermute | solution.py:663
  4.6 0.5 %collective-permute-start.3 = (bf16[5,128,128]{2,1,0:T(8,128)(2,1)}, bf16[5,128,128]{2,1,0:T(8,128)(2,1)S(1)}, u32[]{:S(2)}, u32[]{:S(2)}) collective-permute-start(bf16[5,128,128]{2,1,0:T(8,128)(2,1)} %bitcast.4), channel_id=1, source_target_pairs={{0,16},{8,24},{16,0},{24,8},{1,17},{9,25},{17,1},{25,9},{2,18},{10... | collective-permute-start | bytes 491528 | tf_op jit(solution)/shard_map/ppermute | solution.py:663
  5.1 0.6 %collective-permute-start.2 = (bf16[5,128,128]{2,1,0:T(8,128)(2,1)}, bf16[5,128,128]{2,1,0:T(8,128)(2,1)S(1)}, u32[]{:S(2)}, u32[]{:S(2)}) collective-permute-start(bf16[5,128,128]{2,1,0:T(8,128)(2,1)} %bitcast.5), channel_id=1, source_target_pairs={{0,8},{8,16},{16,24},{24,0},{1,9},{9,17},{17,25},{25,1},{2,10},{10... | collective-permute-start | bytes 491528 | tf_op jit(solution)/shard_map/ppermute | solution.py:663
  5.7 3.1 %prepare.1 = (f32[5,8,128]{2,1,0:T(8,128)S(1)}, f32[5,8,128]{2,1,0:T(8,128)S(1)}, f32[5,128,128]{2,1,0:T(8,128)S(1)}, bf16[160,128]{1,0:T(8,128)(2,1)S(1)}, bf16...) custom-call(s32[96]{0:T(128)} %blade_group.1, ...), custom_call_target="tpu_custom_call" | custom-call | flops 100000000 | bytes 1000000 | tf_op jit(solution)/shard_map/prepare/pallas_call | solution.py:669
  8.8 0.0 copy-start.1
  8.8 0.0 copy-start
  8.8 0.0 copy-start.2
  8.8 0.1 collective-permute-start
  8.9 3.7 %collective-permute-start.1 = (bf16[160,128]{1,0:T(8,128)(2,1)S(1)}, bf16[160,128]{1,0:T(8,128)(2,1)S(1)}, u32[]{:S(2)}, u32[]{:S(2)}) collective-permute-start(bf16[160,128]{1,0:T(8,128)(2,1)S(1)} %get-tuple-element.36.sb), channel_id=1, source_target_pairs={{0,7},{1,2},{2,1},{3,4},{4,3},{5,6},{6,5},{7,0},{8,15},{9,10},{10,... | collective-permute-start | bytes 122888 | tf_op jit(solution)/shard_map/ppermute | solution.py:640
  12.6 0.0 collective-permute-done.4.refs_4_
  12.6 1.3 %collective-permute-done.3.refs_3_ = bf16[5,128,128]{2,1,0:T(8,128)(2,1)S(1)} collective-permute-done((bf16[5,128,128]{2,1,0:T(8,128)(2,1)}, bf16[5,128,128]{2,1,0:T(8,128)(2,1)S(1)}, u32[]{:S(2)}, u32[]{:S(2)}) %collective-permute-start.3) | collective-permute-done | bytes 163872 | tf_op jit(solution)/shard_map/ppermute | solution.py:663
  14.0 0.0 collective-permute-done.2.refs_2_
  14.0 0.0 copy-done.1
  14.0 1.1 %strips.1 = (bf16[160,128]{1,0:T(8,128)(2,1)S(1)}, bf16[160,128]{1,0:T(8,128)(2,1)S(1)}, bf16[5,128,128]{2,1,0:T(8,128)(2,1)S(1)}, bf16[5,128,128]{2,1,0:T(8,128)(2,1)S(1)}, bf16[5,128,128]{2,1,0:T(8,128)(2,1)S(1)}) custom-call(s32[4]{0:T(128)} %copy-done.1, bf16[5,128,128]{2,1,0:T(8,128)(2,1)S(1)} %get-tuple-element.45.refs_1_, ...), custom_call_target="tpu_custom_call" | custom-call | flops 10000000 | bytes 1000000 | tf_op jit(solution)/shard_map/strips/pallas_call | solution.py:669
  15.1 0.1 collective-permute-start.5
  15.2 3.7 %collective-permute-start.6 = (bf16[160,128]{1,0:T(8,128)(2,1)S(1)}, bf16[160,128]{1,0:T(8,128)(2,1)S(1)}, u32[]{:S(2)}, u32[]{:S(2)}) collective-permute-start(bf16[160,128]{1,0:T(8,128)(2,1)S(1)} %get-tuple-element.48.sb), channel_id=1, source_target_pairs={{0,7},{1,2},{2,1},{3,4},{4,3},{5,6},{6,5},{7,0},{8,15},{9,10},{10,... | collective-permute-start | bytes 122888 | tf_op jit(solution)/shard_map/ppermute | solution.py:640
  18.9 0.0 collective-permute-done.ra
  18.9 0.0 collective-permute-done.1.rb
  18.9 0.0 copy-done
  18.9 2.1 %halo_forcing.1 = (f32[16,5,16,128]{3,2,1,0:T(8,128)S(1)}, f32[5,128,128]{2,1,0:T(8,128)S(1)}, bf16[384,128]{1,0:T(8,128)(2,1)S(1)}) custom-call(f32[5,5]{1,0:T(8,128)} %copy-done, s32[1,128]{1,0:T(1,128)S(1)} %get-tuple-element.34.link, bf16[160,128]{1,0:T(8,128)(2,1)S(1)} %get-tuple-element.35.sa, bf16[160,128]{1,0:T(8,128)(2,1)S(1)} %get-tuple-element.36.sb, ...), custom_call_target="tpu_custom_call" | custom-call | flops 100000000 | bytes 1000000 | tf_op jit(solution)/shard_map/halo_forcing/pallas_call | solution.py:669
  21.0 0.0 collective-permute-done.5.ra
  21.0 0.0 collective-permute-done.6.rb
  21.0 2.2 %halo.1 = (bf16[640,256]{1,0:T(8,128)(2,1)S(1)}, bf16[640,256]{1,0:T(8,128)(2,1)S(1)}) custom-call(f32[5,5]{1,0:T(8,128)} %copy-done, bf16[160,128]{1,0:T(8,128)(2,1)S(1)} %get-tuple-element.47.sa, bf16[160,128]{1,0:T(8,128)(2,1)S(1)} %get-tuple-element.48.sb, bf16[160,128]{1,0:T(8,128)(2,1)S(1)} %collective-permute-done.5.ra, ...), custom_call_target="tpu_custom_call" | custom-call | flops 100000000 | bytes 1000000 | tf_op jit(solution)/shard_map/halo/pallas_call | solution.py:669
  23.2 0.0 copy-done.2
  23.2 11.9 %steps.1 = (f32[40,128,128]{2,1,0:T(8,128)}, f32[2,4]{1,0:T(2,128)S(1)}) custom-call(f32[5,5]{1,0:T(8,128)} %copy-done, s32[128]{0:T(128)} %copy-done.2, f32[5,128,128]{2,1,0:T(8,128)S(1)} %get-tuple-element.33.forcing, f32[5,128,128]{2,1,0:T(8,128)S(1)} %get-tuple-element.39.fe, f32[5,128,128]{2,1,0:T(8,128)S(1)} %get-tuple-element.40.b0, ...), custom_call_target="tpu_custom_call" | custom-call | flops 1000000000 | bytes 1000000 | tf_op jit(solution)/shard_map/steps/pallas_call | solution.py:669
  35.1 0.1 collective-permute-start.7
  35.2 1.1 %collective-permute-done.7 = f32[2,4]{1,0:T(2,128)S(1)} collective-permute-done((f32[2,4]{1,0:T(2,128)S(1)}, f32[2,4]{1,0:T(2,128)S(1)}, u32[]{:S(2)}, u32[]{:S(2)}) %collective-permute-start.7) | collective-permute-done | bytes 64 | tf_op jit(solution)/shard_map/ppermute | solution.py:632
  36.3 0.0 collective-permute-start.8
  36.3 3.6 %collective-permute-done.8 = f32[2,4]{1,0:T(2,128)S(1)} collective-permute-done((f32[2,4]{1,0:T(2,128)S(1)}, f32[2,4]{1,0:T(2,128)S(1)}, u32[]{:S(2)}, u32[]{:S(2)}) %collective-permute-start.8) | collective-permute-done | bytes 64 | tf_op jit(solution)/shard_map/ppermute | solution.py:632
  39.9 1.7 %collective-permute-start.9 = (f32[2,4]{1,0:T(2,128)S(1)}, f32[2,4]{1,0:T(2,128)S(1)}, u32[]{:S(2)}, u32[]{:S(2)}) collective-permute-start(f32[2,4]{1,0:T(2,128)S(1)} %add.10), channel_id=1, source_target_pairs={{0,4},{1,5},{2,6},{3,7},{4,0},{5,1},{6,2},{7,3},{8,12},{9,13},{10,... | collective-permute-start | bytes 104 | tf_op jit(solution)/shard_map/ppermute | solution.py:632
  41.6 2.8 %collective-permute-done.9 = f32[2,4]{1,0:T(2,128)S(1)} collective-permute-done((f32[2,4]{1,0:T(2,128)S(1)}, f32[2,4]{1,0:T(2,128)S(1)}, u32[]{:S(2)}, u32[]{:S(2)}) %collective-permute-start.9) | collective-permute-done | bytes 64 | tf_op jit(solution)/shard_map/ppermute | solution.py:632
  44.3 0.6 %add.11 = f32[2,4]{1,0:T(2,128)} add(f32[2,4]{1,0:T(2,128)S(1)} %add.10, f32[2,4]{1,0:T(2,128)S(1)} %collective-permute-done.9) | non-fusion elementwise | flops 8 | bytes 96 | tf_op jit(solution)/shard_map/add | solution.py:632
  (2 shorter events, 0.0 us)
Async XLA Ops:
  0.6 12.0 %collective-permute-start.4 = (bf16[5,128,128]{2,1,0:T(8,128)(2,1)}, bf16[5,128,128]{2,1,0:T(8,128)(2,1)S(1)}, u32[]{:S(2)}, u32[]{:S(2)}) collective-permute-start(bf16[5,128,128]{2,1,0:T(8,128)(2,1)} %bitcast.3), channel_id=1, source_target_pairs={{0,24},{8,0},{16,8},{24,16},{1,25},{9,1},{17,9},{25,17},{2,26},{10... | collective-permute-start | bytes 491528 | tf_op jit(solution)/shard_map/ppermute | solution.py:663
  4.6 9.4 %collective-permute-start.3 = (bf16[5,128,128]{2,1,0:T(8,128)(2,1)}, bf16[5,128,128]{2,1,0:T(8,128)(2,1)S(1)}, u32[]{:S(2)}, u32[]{:S(2)}) collective-permute-start(bf16[5,128,128]{2,1,0:T(8,128)(2,1)} %bitcast.4), channel_id=1, source_target_pairs={{0,16},{8,24},{16,0},{24,8},{1,17},{9,25},{17,1},{25,9},{2,18},{10... | collective-permute-start | bytes 491528 | tf_op jit(solution)/shard_map/ppermute | solution.py:663
  5.1 8.9 %collective-permute-start.2 = (bf16[5,128,128]{2,1,0:T(8,128)(2,1)}, bf16[5,128,128]{2,1,0:T(8,128)(2,1)S(1)}, u32[]{:S(2)}, u32[]{:S(2)}) collective-permute-start(bf16[5,128,128]{2,1,0:T(8,128)(2,1)} %bitcast.5), channel_id=1, source_target_pairs={{0,8},{8,16},{16,24},{24,0},{1,9},{9,17},{17,25},{25,1},{2,10},{10... | collective-permute-start | bytes 491528 | tf_op jit(solution)/shard_map/ppermute | solution.py:663
  8.8 5.2 %copy-start.1 = (s32[4]{0:T(128)}, s32[4]{0:T(128)S(1)}, u32[]{:S(2)}) copy-start(s32[4]{0:T(128)S(1)} %get-tuple-element.44.refs_0_) | copy-start | bytes 52
  8.8 10.0 %copy-start = (f32[5,5]{1,0:T(8,128)}, f32[5,5]{1,0:T(8,128)S(1)}, u32[]{:S(2)}) copy-start(f32[5,5]{1,0:T(8,128)S(1)} %get-tuple-element.31.fm) | copy-start | bytes 304
  8.8 14.4 %copy-start.2 = (s32[128]{0:T(128)}, s32[128]{0:T(128)S(1)}, u32[]{:S(2)}) copy-start(s32[128]{0:T(128)S(1)} %get-tuple-element.32.inv) | copy-start | bytes 1540
  8.8 10.0 %collective-permute-start = (bf16[160,128]{1,0:T(8,128)(2,1)S(1)}, bf16[160,128]{1,0:T(8,128)(2,1)S(1)}, u32[]{:S(2)}, u32[]{:S(2)}) collective-permute-start(bf16[160,128]{1,0:T(8,128)(2,1)S(1)} %get-tuple-element.35.sa), channel_id=1, source_target_pairs={{0,1},{1,0},{2,3},{3,2},{4,5},{5,4},{6,7},{7,6},{8,9},{9,8},{10,11... | collective-permute-start | bytes 122888 | tf_op jit(solution)/shard_map/ppermute | solution.py:639
  8.9 9.9 %collective-permute-start.1 = (bf16[160,128]{1,0:T(8,128)(2,1)S(1)}, bf16[160,128]{1,0:T(8,128)(2,1)S(1)}, u32[]{:S(2)}, u32[]{:S(2)}) collective-permute-start(bf16[160,128]{1,0:T(8,128)(2,1)S(1)} %get-tuple-element.36.sb), channel_id=1, source_target_pairs={{0,7},{1,2},{2,1},{3,4},{4,3},{5,6},{6,5},{7,0},{8,15},{9,10},{10,... | collective-permute-start | bytes 122888 | tf_op jit(solution)/shard_map/ppermute | solution.py:640
  15.1 5.9 %collective-permute-start.5 = (bf16[160,128]{1,0:T(8,128)(2,1)S(1)}, bf16[160,128]{1,0:T(8,128)(2,1)S(1)}, u32[]{:S(2)}, u32[]{:S(2)}) collective-permute-start(bf16[160,128]{1,0:T(8,128)(2,1)S(1)} %get-tuple-element.47.sa), channel_id=1, source_target_pairs={{0,1},{1,0},{2,3},{3,2},{4,5},{5,4},{6,7},{7,6},{8,9},{9,8},{10,11... | collective-permute-start | bytes 122888 | tf_op jit(solution)/shard_map/ppermute | solution.py:639
  15.2 5.9 %collective-permute-start.6 = (bf16[160,128]{1,0:T(8,128)(2,1)S(1)}, bf16[160,128]{1,0:T(8,128)(2,1)S(1)}, u32[]{:S(2)}, u32[]{:S(2)}) collective-permute-start(bf16[160,128]{1,0:T(8,128)(2,1)S(1)} %get-tuple-element.48.sb), channel_id=1, source_target_pairs={{0,7},{1,2},{2,1},{3,4},{4,3},{5,6},{6,5},{7,0},{8,15},{9,10},{10,... | collective-permute-start | bytes 122888 | tf_op jit(solution)/shard_map/ppermute | solution.py:640
  35.1 1.2 %collective-permute-start.7 = (f32[2,4]{1,0:T(2,128)S(1)}, f32[2,4]{1,0:T(2,128)S(1)}, u32[]{:S(2)}, u32[]{:S(2)}) collective-permute-start(f32[2,4]{1,0:T(2,128)S(1)} %get-tuple-element.59), channel_id=1, source_target_pairs={{0,1},{1,0},{2,3},{3,2},{4,5},{5,4},{6,7},{7,6},{8,9},{9,8},{10,11... | collective-permute-start | bytes 104 | tf_op jit(solution)/shard_map/ppermute | solution.py:632
  36.3 3.6 %collective-permute-start.8 = (f32[2,4]{1,0:T(2,128)S(1)}, f32[2,4]{1,0:T(2,128)S(1)}, u32[]{:S(2)}, u32[]{:S(2)}) collective-permute-start(f32[2,4]{1,0:T(2,128)S(1)} %add.9), channel_id=1, source_target_pairs={{0,2},{1,3},{2,0},{3,1},{4,6},{5,7},{6,4},{7,5},{8,10},{9,11},{10,... | collective-permute-start | bytes 104 | tf_op jit(solution)/shard_map/ppermute | solution.py:632
  39.9 4.5 %collective-permute-start.9 = (f32[2,4]{1,0:T(2,128)S(1)}, f32[2,4]{1,0:T(2,128)S(1)}, u32[]{:S(2)}, u32[]{:S(2)}) collective-permute-start(f32[2,4]{1,0:T(2,128)S(1)} %add.10), channel_id=1, source_target_pairs={{0,4},{1,5},{2,6},{3,7},{4,0},{5,1},{6,2},{7,3},{8,12},{9,13},{10,... | collective-permute-start | bytes 104 | tf_op jit(solution)/shard_map/ppermute | solution.py:632

commit v3 on v2

--- a/solution.py
+++ b/solution.py
@@ -38,6 +38,7 @@
 HALF = SEG // 2
 VMEM_LIMIT = 40 * 2**20
 SMALL_LIMIT = 16 * 2**20
+PARTS_LAST = 1
 
 VMEM = pl.BlockSpec(memory_space=pltpu.VMEM)
 SMEM = pl.BlockSpec(memory_space=pltpu.SMEM)
@@ -149,6 +150,12 @@
     return jnp.where(group == group_base + pair // AMP, harmonic, 0.0)
 
 
+def column_weight(columns, total):
+    columns = jnp.where(columns < 0, columns + total, columns)
+    columns = jnp.where(columns >= total, columns - total, columns)
+    return 1.0 + 2.0 * columns.astype(F32) / total
+
+
 def flux(fm, q, d):
     inner = q[0] * d[0]
     for f in range(1, FIELDS):
@@ -167,8 +174,8 @@
 
 def prepare_kernel(cycle, blade_group, link_s, *refs):
     owner, fm = refs[:2]
-    kept = refs[2 : (len(refs) - 11) // 2 + 2]
-    k_ref, kp_ref, b0_ref, send_a, send_b, inv_ref, owner_out, fm_out, *held, sems = refs[
+    kept = refs[2 : (len(refs) - 12) // 2 + 2]
+    k_ref, kp_ref, b0_ref, v0_ref, send_a, send_b, inv_ref, owner_out, fm_out, *held, sems = refs[
         2 + len(kept) :
     ]
     copies = fetch(zip(kept, held), sems)
@@ -198,17 +205,24 @@
     arrive(copies[:3])
     links = link[...].astype(F32)
     parts = [split3(forcing[f]) for f in range(FIELDS)]
-    linked = mm(one_hot(links, rows), jnp.concatenate(sum(parts, ()), axis=1))
+    hot = one_hot(links, rows)
+    flat = jnp.concatenate(sum(parts, ()), axis=1)
+    linked = mm(hot, flat)
+    linking = mm(hot, flat, TN)
+    weight = column_weight(lax.broadcasted_iota(jnp.int32, (1, width), 1) + start, total)
     chosen = mm(
         jnp.concatenate([jnp.concatenate(three, axis=1) for three in parts], axis=0), sel[...]
     )
     row = lax.broadcasted_iota(jnp.int32, (2 * SLOT, rows), 0)
     links = jnp.broadcast_to(links, row.shape)
     for f in range(FIELDS):
-        three = [
-            linked[:, (f * PARTS + i) * width : (f * PARTS + i + 1) * width] for i in range(PARTS)
-        ]
-        b0_ref[f] = (C0 + 1.0) * forcing[f] + CP * (three[0] + three[1] + three[2])
+
+        def moved(x):
+            three = [x[:, (f * PARTS + i) * width : (f * PARTS + i + 1) * width] for i in range(PARTS)]
+            return three[0] + three[1] + three[2]
+
+        b0_ref[f] = (C0 + 1.0) * forcing[f] + CP * moved(linked)
+        v0_ref[f] = (C0 * forcing[f] + CP * moved(linking)) * weight
         turned = chosen[f * rows : (f + 1) * rows].T[: 2 * SLOT]
         if f == 0:
             turned = jnp.where(row % SLOT == LINK_ROW, links, turned)
@@ -251,11 +265,17 @@
     for lane, column in ((width - 2, -2), (width - 1, -1), (0, width), (1, width + 1)):
         for row in forcing_rows(column):
             edge[row, lane] = 1.0
+    state_edge = np.zeros((4 * SLOT, width), np.float32)
+    for lane, column in ((width - 1, -1), (0, width)):
+        source, j = place(column, QW)
+        state_edge[source * SLOT + j, lane] = 1.0
 
     def tiled(x):
         return np.repeat(x[:, :, None, :], blocks, axis=2).reshape(4 * SLOT, -1)
 
-    return tuple(x.astype(jnp.bfloat16) for x in (tiled(forcing_sel), tiled(state_sel), edge))
+    return tuple(
+        x.astype(jnp.bfloat16) for x in (tiled(forcing_sel), tiled(state_sel), edge, state_edge)
+    )
 
 
 def stencil_selects(width):
@@ -396,7 +416,10 @@
                 y_ref[i * 8 + d, f] = value
 
 
-def halo_kernel(fm, sa, sb, ra, rb, tiled, kp_ref, hot, y_in, e1_ref, e2_ref, y_ref, big, q_ref, fmc):
+def halo_kernel(
+    fm, sa, sb, ra, rb, tiled, edge, kp_ref, hot, y_in,
+    e1_ref, e2_ref, qe_ref, y_ref, big, q_ref, fmc,
+):
     for i in (1, 3, 9, 11):
         y_ref[i] = y_in[i]
     rows, width = hot.shape[1], kp_ref.shape[2]
@@ -406,6 +429,9 @@
             fmc[f, e] = fm[f, e] * CM
     _, _, turned = gather_sources(sa, sb, ra, rb)
     g = jnp.concatenate(turned, axis=1)
+    qe = mm(jnp.concatenate(turned, axis=0), edge[...])
+    for f in range(FIELDS):
+        qe_ref[f] = qe[f * rows : (f + 1) * rows]
     y = mm(hot[...], g).astype(BF16)
     part = in_segments((g, y[:rows], y[2 * rows :]), tiled, big, step)
     is_left = left_lanes(step, width)
@@ -456,76 +482,131 @@
     lax.fori_loop(0, step, body, 0, unroll=8)
 
 
-def main_kernel(
-    cycle, fm, inv, forcing, fe, b0, k_ref, inner, outer, e1, e2, q0, q1, q2,
-    out_hbm, sens_ref,
-    bs, coef, mu1, mu2, dz, dze, stage, weighted, fmc, out_sems,
+def shift_edges(x, edge, lane, width):
+    return (
+        pltpu.roll(jnp.where(lane == width - 1, edge, x), 1, 1),
+        pltpu.roll(jnp.where(lane == 0, edge, x), width - 1, 1),
+    )
+
+
+def spread(ref, index, r):
+    return jnp.broadcast_to(ref[(*index, pl.ds(r, 1), slice(None))], (8, ref.shape[-1]))
+
+
+def place(r, f):
+    return pl.ds(pl.multiple_of((r * FIELDS + f) * 8, 8), 8)
+
+
+def scaled_matrix(fm, fmc):
+    for f in range(FIELDS):
+        for e in range(FIELDS):
+            fmc[f, e] = fm[f, e] * CM
+
+
+def matrix_rows(fmc, width):
+    return [[jnp.full((8, width), fmc[f, e]) for e in range(FIELDS)] for f in range(FIELDS)]
+
+
+def stencil_products(dz, dze, source, first, count, edges, inner, outer, lanes):
+    dz[...] = mm(halves(source[first : first + count, :]), inner[...])
+    dze[...] = mm(edges[...], outer[:, lanes])
+
+
+def step_row(source, dz, dze, coef, fmv, linked, r, local, j, chunk):
+    width = source.shape[1]
+
+    def both(f, half):
+        own = dz[place(local, f), half * width : (half + 1) * width]
+        lanes = pl.ds(pl.multiple_of(j * (2 * width) + half * width, width), width)
+        return own + dze[chunk + f * 8 : chunk + f * 8 + 8, lanes]
+
+    d = [both(f, 0) for f in range(FIELDS)]
+    out = []
+    for e in range(FIELDS):
+        value = UNIT * both(e, 1) + CP * source[place(linked, e), :]
+        for f in range(FIELDS):
+            if f == e:
+                m = spread(coef, (e,), r)
+            elif e == 1:
+                m = spread(coef, (FIELDS + (0, 2, 3, 4).index(f),), r)
+            else:
+                m = fmv[f][e]
+            value = value - m * d[f]
+        out.append(value)
+    return out
+
+
+def first_steps_kernel(
+    cycle, fm, inv, forcing, fe, b0, v0, qe, k_ref, inner, outer, e1, q0, q1, q2,
+    mu2, coef0, sens_ref,
+    bs, coef1, mu1, dz, dze, weighted, heavy, fmc,
 ):
     rows, width = forcing.shape[1], forcing.shape[2]
     total = cycle * width
-
-    for f in range(FIELDS):
-        for e in range(FIELDS):
-            fmc[f, e] = fm[f, e] * CM
+    blocks = width // SEG
+    size = rows // blocks
+    scaled_matrix(fm, fmc)
     lane = lax.broadcasted_iota(jnp.int32, (8, width), 1)
     start = lax.axis_index("blk") * width
-    weight = 1.0 + 2.0 * (lane + start).astype(F32) / total
     norm = 1.0 / math.sqrt(FIELDS * rows * total)
-
-    def around(x, edge):
-        return (
-            pltpu.roll(jnp.where(lane == width - 1, edge, x), 1, 1),
-            pltpu.roll(jnp.where(lane == 0, edge, x), width - 1, 1),
-            pltpu.roll(jnp.where(lane >= width - 2, edge, x), 2, 1),
-            pltpu.roll(jnp.where(lane < 2, edge, x), width - 2, 1),
-        )
+    weight = {d: column_weight(lane + (start + d), total) for d in range(-2, 3)}
+    beside = column_weight(jnp.where(lane < width // 2, lane + width, lane - width) + start, total)
 
     def dense(i, z):
         rs = pl.ds(pl.multiple_of(i * 16, 16), 16)
-        q = [q2[f, rs, :].astype(F32) for f in range(FIELDS)]
+        for n, (q_ref, coef) in enumerate(((q0, coef0), (q1, coef1))):
+            q = [q_ref[f, rs, :].astype(F32) for f in range(FIELDS)]
+            u = CU * q[1]
+            for e in range(FIELDS):
+                coef[e, rs, :] = (u if e != 1 else u + u) + fmc[e, e]
+            for j, f in enumerate((0, 2, 3, 4)):
+                coef[FIELDS + j, rs, :] = CU * q[f] + fmc[f, 1]
+        both_q = [[q[f, rs, :].astype(F32) for f in range(FIELDS)] for q in (q0, q2)]
         for half in range(2):
             r8 = pl.ds(pl.multiple_of(i * 16 + half * 8, 8), 8)
-            near = [around(forcing[f, r8, :], fe[f, r8, :]) for f in range(FIELDS)]
-            mine = [x[half * 8 : half * 8 + 8] for x in q]
-            minus = flux(fmc, mine, [a[0] for a in near])
-            plus = flux(fmc, mine, [a[1] for a in near])
+            mine, last = [[x[half * 8 : half * 8 + 8] for x in q] for q in both_q]
+            near, w, we = [], [], []
+            for f in range(FIELDS):
+                x, edge = forcing[f, r8, :], fe[f, r8, :]
+                near.append(
+                    (
+                        *shift_edges(x, edge, lane, width),
+                        pltpu.roll(jnp.where(lane >= width - 2, edge, x), 2, 1),
+                        pltpu.roll(jnp.where(lane < 2, edge, x), width - 2, 1),
+                    )
+                )
+                w.append(x * weight[0])
+                we.append(edge * beside)
+            minus = flux(fmc, last, [a[0] for a in near])
+            plus = flux(fmc, last, [a[1] for a in near])
+            q_edge = [qe[f, r8, :] for f in range(FIELDS)]
             for f in range(FIELDS):
                 m1, p1, m2, p2 = near[f]
                 bs[0, f, r8, :] = C2 * m2
                 bs[1, f, r8, :] = C1 * m1 - minus[f]
                 bs[2, f, r8, :] = C1 * p1 + plus[f]
                 bs[3, f, r8, :] = C2 * p2
-                w = forcing[f, r8, :] * weight
-                weighted[f, r8, :] = w
-                z = z + w * forcing[f, r8, :]
+                weighted[f, r8, :] = w[f]
+                z = z + w[f] * forcing[f, r8, :]
+                x = CU * (mine[1] * w[f] + mine[f] * w[1])
+                xe = CU * (q_edge[1] * we[f] + q_edge[f] * we[1])
+                for e in range(FIELDS):
+                    x = x + fmc[f, e] * w[e]
+                    xe = xe + fmc[f, e] * we[e]
+                before, after = shift_edges(x, xe, lane, width)
+                turned = v0[f, r8, :] + C1 * (m1 * weight[-1] + p1 * weight[1])
+                turned = turned + C2 * (m2 * weight[-2] + p2 * weight[2])
+                heavy[f, r8, :] = w[f] + turned + (before - after)
         return z
-
-    def coefficients(i, c):
-        rs = pl.ds(pl.multiple_of(i * 16, 16), 16)
-        for n, q_ref in enumerate((q0, q1)):
-            q = [q_ref[f, rs, :].astype(F32) for f in range(FIELDS)]
-            u = CU * q[1]
-            for e in range(FIELDS):
-                coef[n, e, rs, :] = (u if e != 1 else u + u) + fmc[e, e]
-            for j, f in enumerate((0, 2, 3, 4)):
-                coef[n, FIELDS + j, rs, :] = CU * q[f] + fmc[f, 1]
-        return c
 
     zero = jnp.zeros((8, width), F32)
     z = lax.fori_loop(0, rows // 16, dense, zero)
-    lax.fori_loop(0, rows // 16, coefficients, 0)
     k = [k_ref[i] for i in range(5)]
 
-    def spread(ref, index, r):
-        return jnp.broadcast_to(ref[(*index, pl.ds(r, 1), slice(None))], (8, width))
-
-    def place(r, f):
-        return pl.ds(pl.multiple_of((r * FIELDS + f) * 8, 8), 8)
-
-    def first(i, acc):
+    def first(j, acc):
         acc = list(acc)
-        for j in range(8):
-            r = i * 8 + j
+        for i in range(size):
+            r = j * size + i
             for f in range(FIELDS):
                 value = spread(bs, (0, f), r) * k[0] + spread(bs, (1, f), r) * k[1]
                 value = value + spread(b0, (f,), r) * k[2] + spread(bs, (2, f), r) * k[3]
@@ -534,80 +615,22 @@
                 acc[f] = acc[f] + value * spread(weighted, (f,), r)
         return tuple(acc)
 
-    acc = lax.fori_loop(0, rows // 8, first, (zero,) * FIELDS)
-
-    blocks = width // SEG
-    size = rows // blocks
-    fmv = [[jnp.full((8, width), fmc[f, e]) for e in range(FIELDS)] for f in range(FIELDS)]
-
-    def products(source, edges):
-        dz[...] = mm(halves(source[...]), inner[...])
-        dze[...] = mm(edges[...], outer[...])
-
-    def row(n, source, j, i, acc, keep):
-        r = j * size + i
-        linked = inv[r]
-        chunk = i * FIELDS * 8
-
-        def both(f, half):
-            own = dz[place(r, f), half * width : (half + 1) * width]
-            lanes = pl.ds(pl.multiple_of(j * (2 * width) + half * width, width), width)
-            return own + dze[chunk + f * 8 : chunk + f * 8 + 8, lanes]
-
-        d = [both(f, 0) for f in range(FIELDS)]
-        for e in range(FIELDS):
-            value = UNIT * both(e, 1) + CP * source[place(linked, e), :]
-            for f in range(FIELDS):
-                if f == e:
-                    m = spread(coef, (n, e), r)
-                elif e == 1:
-                    m = spread(coef, (n, FIELDS + (0, 2, 3, 4).index(f)), r)
-                else:
-                    m = fmv[f][e]
-                value = value - m * d[f]
-            value = keep(r, e, value)
-            acc[e] = acc[e] + value * spread(weighted, (e,), r)
+    acc = lax.fori_loop(0, blocks, first, (zero,) * FIELDS)
+    fmv = matrix_rows(fmc, width)
+    stencil_products(dz, dze, mu1, 0, rows * FIELDS * 8, e1, inner, outer, slice(None))
 
     def second(j, acc):
         acc = list(acc)
-
-        def keep(r, e, value):
-            value = value + spread(forcing, (e,), r) * k[2]
-            mu2[place(r, e), :] = value
-            return value
-
         for i in range(size):
-            row(1, mu1, j, i, acc, keep)
+            r = j * size + i
+            made = step_row(mu1, dz, dze, coef1, fmv, inv[r], r, r, j, i * FIELDS * 8)
+            for f, value in enumerate(made):
+                value = value + spread(forcing, (f,), r) * k[2]
+                mu2[place(r, f), :] = value
+                acc[f] = acc[f] + value * spread(heavy, (f,), r)
         return tuple(acc)
 
-    products(mu1, e1)
     acc = lax.fori_loop(0, blocks, second, acc)
-
-    def send(j):
-        at = pl.ds(pl.multiple_of(j * size, size), size)
-        return pltpu.make_async_copy(stage.at[:, at, :], out_hbm.at[:, at, :], out_sems.at[j])
-
-    def third(j, acc):
-        acc = list(acc)
-        for part in range(size // 8):
-            made = [[] for _ in range(FIELDS)]
-
-            def keep(r, e, value):
-                made[e].append(value)
-                return value
-
-            for i in range(8):
-                row(0, mu2, j, part * 8 + i, acc, keep)
-            at = pl.ds(pl.multiple_of(j * size + part * 8, 8), 8)
-            for e in range(FIELDS):
-                turned = jnp.swapaxes(jnp.stack(made[e]), 0, 1)
-                for pair in range(PAIRS):
-                    stage[pair * FIELDS + e, at, :] = turned[pair]
-        send(j).start()
-        return tuple(acc)
-
-    products(mu2, e2)
-    acc = lax.fori_loop(0, blocks, third, acc)
     source_part = jnp.sum(z, axis=0, keepdims=True) * k[2]
     acc = (sum(acc) - 2.0 * source_part) * norm
     acc = jnp.broadcast_to(jnp.sum(acc, axis=1, keepdims=True), (8, width))
@@ -615,7 +638,46 @@
     for group in range(GRP_DEV):
         mine = jnp.where(sub == group * AMP + lane, acc, 0.0)
         sens_ref[group : group + 1, :] = jnp.sum(mine, axis=0, keepdims=True)[:, :AMP]
-    for j in range(blocks):
+
+
+def last_step_kernel(part, parts, fm, inv, *refs):
+    mu2, coef0, e2, inner, outer = refs[-11:-6]
+    out_hbm, dz, dze, stage, fmc, out_sems = refs[-6:]
+    rows, width = coef0.shape[1:]
+    blocks = width // SEG
+    size = rows // blocks
+    here = blocks // parts
+    begin = part * here
+    scaled_matrix(fm, fmc)
+    fmv = matrix_rows(fmc, width)
+    chunk = size * FIELDS * 8
+    lanes = slice(begin * 2 * width, (begin + here) * 2 * width)
+    stencil_products(dz, dze, mu2, begin * chunk, here * chunk, e2, inner, outer, lanes)
+
+    def send(j):
+        at = pl.ds(pl.multiple_of(j * 8, 8), 8)
+        to = pl.ds(pl.multiple_of(begin * size + j * 8, 8), 8)
+        return pltpu.make_async_copy(stage.at[:, at, :], out_hbm.at[:, to, :], out_sems.at[j])
+
+    def third(j, c):
+        for half in range(size // 8):
+            made = []
+            for i in range(half * 8, half * 8 + 8):
+                local = j * size + i
+                r = begin * size + local
+                made.append(
+                    step_row(mu2, dz, dze, coef0, fmv, inv[r], r, local, j, i * FIELDS * 8)
+                )
+            at = pl.ds(pl.multiple_of(j * size + half * 8, 8), 8)
+            for e in range(FIELDS):
+                turned = jnp.swapaxes(jnp.stack([x[e] for x in made]), 0, 1)
+                for pair in range(PAIRS):
+                    stage[pair * FIELDS + e, at, :] = turned[pair]
+            send(j * (size // 8) + half).start()
+        return c
+
+    lax.fori_loop(0, here, third, 0)
+    for j in range(here * size // 8):
         send(j).wait()
 
 
@@ -623,15 +685,8 @@
     return [(i, (i + k) % devices) for i in range(devices)]
 
 
-def total_over(x, axis):
-    devices = lax.axis_size(axis)
-    if devices & (devices - 1):
-        return lax.psum(x, axis)
-    bit = 1
-    while bit < devices:
-        x = x + lax.ppermute(x, axis, [(i, i ^ bit) for i in range(devices)])
-        bit *= 2
-    return x
+def round_over(x, axis, bit):
+    return x + lax.ppermute(x, axis, [(i, i ^ bit) for i in range(lax.axis_size(axis))])
 
 
 def to_neighbours(send_a, send_b, cycle):
@@ -682,11 +737,11 @@
         *halo_selects(width), *stencil_selects(width),
     )
     made = (
-        factors, factors, field, strip, strip,
+        factors, factors, field, field, strip, strip,
         struct((rows,), jnp.int32), struct(owner.shape, jnp.int32), struct(flux_matrix.shape),
     )
     made += tuple(struct(x.shape, x.dtype) for x in kept)
-    k, kp, b0, f_a, f_b, inv, owner_s, fm_s, *held = call(
+    k, kp, b0, v0, f_a, f_b, inv, owner_s, fm_s, *held = call(
         functools.partial(prepare_kernel, cycle),
         made,
         (blade_group, row_link[0], owner, flux_matrix),
@@ -696,9 +751,10 @@
         SMALL_LIMIT,
         10**8,
         "prepare",
-        (VMEM,) * 5 + (SMEM,) * 3 + (VMEM,) * len(kept),
-    )
-    forcing_v, link, _, slot_v, state_sel, forcing_tiled, state_tiled, edge, inner, outer = held
+        (VMEM,) * 6 + (SMEM,) * 3 + (VMEM,) * len(kept),
+    )
+    forcing_v, link, _, slot_v, state_sel, *held = held
+    forcing_tiled, state_tiled, edge, state_edge, inner, outer = held
     f_sent = (f_a, f_b, *to_neighbours(f_a, f_b, cycle))
 
     q_a, q_b, *chosen = call(
@@ -726,12 +782,12 @@
         "halo_forcing",
     )
     edge_struct = struct((step_rows * FIELDS * 8, 2 * width), BF16)
-    e1, e2 = call(
+    e1, e2, qe = call(
         halo_kernel,
-        (edge_struct, edge_struct),
+        (edge_struct, edge_struct, field),
         (fm_s,),
         (),
-        (*q_sent, state_tiled, kp, hot, y),
+        (*q_sent, state_tiled, state_edge, kp, hot, y),
         [
             like(y),
             pltpu.VMEM((blocks * 4 * SLOT, state_tiled.shape[1]), BF16),
@@ -742,33 +798,62 @@
         10**8,
         "halo",
     )
-    pairs_fields = PAIRS * FIELDS
     flat = rows * FIELDS * PAIRS
-    adjoint, sens = call(
-        functools.partial(main_kernel, cycle),
-        (struct((pairs_fields, rows, width)), struct((GRP_DEV, AMP))),
+    coefficients = (2 * FIELDS - 1, rows, width)
+    outside = (flat // blocks, blocks * 2 * width)
+    mu2, coef0, sens = call(
+        functools.partial(first_steps_kernel, cycle),
+        (struct((flat, width)), struct(coefficients), struct((GRP_DEV, AMP))),
         (fm_s, inv),
         (),
-        (forcing_v, fe, b0, k, inner, outer, e1, e2, *chosen),
+        (forcing_v, fe, b0, v0, qe, k, inner, outer, e1, *chosen),
         [
             pltpu.VMEM((4, FIELDS, rows, width), F32),
-            pltpu.VMEM((STEPS - 1, 2 * FIELDS - 1, rows, width), F32),
-            pltpu.VMEM((flat, width), F32),
+            pltpu.VMEM(coefficients, F32),
             pltpu.VMEM((flat, width), F32),
             pltpu.VMEM((flat, 2 * width), F32),
-            pltpu.VMEM((flat // blocks, blocks * 2 * width), F32),
-            pltpu.VMEM((pairs_fields, rows, width), F32),
+            pltpu.VMEM(outside, F32),
+            pltpu.VMEM((FIELDS, rows, width), F32),
             pltpu.VMEM((FIELDS, rows, width), F32),
             pltpu.SMEM((FIELDS, FIELDS), F32),
-            sems((blocks,)),
         ],
         VMEM_LIMIT,
         10**9,
-        "steps",
-        (HBM, VMEM),
-    )
-
-    return adjoint.reshape(GRP_DEV, AMP, FIELDS, rows, width), total_over(sens, "blk")
+        "first_steps",
+    )
+
+    pairs_fields = PAIRS * FIELDS
+    bits = [1 << i for i in reversed(range(cycle.bit_length() - 1))]
+    exact = 1 << len(bits) == cycle
+    if not exact:
+        sens = lax.psum(sens, "blk")
+    adjoint = None
+    for part in range(PARTS_LAST):
+        if part:
+            adjoint, sens = lax.optimization_barrier((adjoint, sens))
+        if exact and bits:
+            sens = round_over(sens, "blk", bits.pop(0))
+        before = () if adjoint is None else (adjoint,)
+        adjoint = pl.pallas_call(
+            functools.partial(last_step_kernel, part, PARTS_LAST),
+            out_shape=struct((pairs_fields, rows, width)),
+            in_specs=[SMEM] * 2 + [HBM] * len(before) + [VMEM] * 5,
+            out_specs=HBM,
+            scratch_shapes=[
+                pltpu.VMEM((flat // PARTS_LAST, 2 * width), F32),
+                pltpu.VMEM((flat // blocks, blocks // PARTS_LAST * 2 * width), F32),
+                pltpu.VMEM((pairs_fields, rows // PARTS_LAST, width), F32),
+                pltpu.SMEM((FIELDS, FIELDS), F32),
+                sems((rows // 8 // PARTS_LAST,)),
+            ],
+            input_output_aliases={2: 0} if before else {},
+            compiler_params=pltpu.CompilerParams(vmem_limit_bytes=SMALL_LIMIT),
+            cost_estimate=cost(10**9, 10**6),
+            name="last_step",
+        )(fm_s, inv, *before, mu2, coef0, e2, inner, outer)
+    for bit in bits if exact else ():
+        sens = round_over(sens, "blk", bit)
+    return adjoint.reshape(GRP_DEV, AMP, FIELDS, rows, width), sens
 
 
 def solution(mesh):

time: 45.2 us -> 41.8 us (0.925)
  waiting for transfers between devices: 8.82 us -> 4.12 us
  starting transfers between devices: 14.4 us -> 15.1 us
  Pallas kernels: 20.4 us -> 20.9 us
    pallas_call x0 -> x1, Pallas kernels: none -> 5.4 us  [on_device(): pl.pallas_call(functools.partial(last_step_kernel, part, PARTS_LAST), out...]
    pallas_call x5, Pallas kernels: 20.4 us -> 15.5 us  [call(): pl.pallas_call(kernel, out_shape=out_shape, in_specs=[SMEM] * len(smem) +...]
    ppermute x3, waiting for transfers between devices: 7.47 us -> 2.8 us  [round_over(): lax.ppermute(x, axis, [(i, i ^ bit) for i in range(lax.axis_size(axis))])]
    ppermute x3, starting transfers between devices: 1.76 us -> 2.53 us  [round_over(): lax.ppermute(x, axis, [(i, i ^ bit) for i in range(lax.axis_size(axis))])]
  transfers between devices with their start and end apart: 10 -> 10, of which waited for: 4 -> 3; matrix products, arithmetic and copies ran while one was open for 0% -> 0% of each run, Pallas kernels for 14% -> 28%
where the time goes in v3:
time: 41.8 us; the launch traced here: 41.5 us
  Pallas kernels  20.9 us (50%)
  starting transfers between devices  15.1 us (36%)
  waiting for transfers between devices  4.12 us (10%)
  between operations  0.78 us (2%)
  other arithmetic  0.57 us (1%)
    pallas_call x5, Pallas kernels, call(): pl.pallas_call(kernel, out_shape=out_shape, in_specs=[SMEM] * len(smem) +...  15.5 us
    ppermute x2, starting transfers between devices, to_neighbours(): lax.ppermute(send_b, 'blk', [(i, (i + 1) % cycle if i % 2 else (i - 1) %...  7.4 us
    pallas_call x1, Pallas kernels, on_device(): pl.pallas_call(functools.partial(last_step_kernel, part, PARTS_LAST), out...  5.4 us
    ppermute x3, starting transfers between devices, on_device(): lax.ppermute(slot, 'out', shift_pairs(n_out, k))  5.04 us
    ppermute x3, waiting for transfers between devices, round_over(): lax.ppermute(x, axis, [(i, i ^ bit) for i in range(lax.axis_size(axis))])  2.8 us
    ppermute x3, starting transfers between devices, round_over(): lax.ppermute(x, axis, [(i, i ^ bit) for i in range(lax.axis_size(axis))])  2.53 us
    ppermute x3, waiting for transfers between devices, on_device(): lax.ppermute(slot, 'out', shift_pairs(n_out, k))  1.31 us
  transfers between devices with their start and end apart: 10, of which 3 were waited for; matrix products, arithmetic and copies ran while one was open for 0% of the time, Pallas kernels for 28%

profile of v3, /device:TPU:0, one launch (start us, length us, event | category | flops | bytes accessed | tf_op | source)
XLA Modules:
  0.0 41.5 jit_solution(6453395352808292576)
XLA Ops:
  0.6 3.9 %collective-permute-start.4 = (bf16[5,128,128]{2,1,0:T(8,128)(2,1)}, bf16[5,128,128]{2,1,0:T(8,128)(2,1)S(1)}, u32[]{:S(2)}, u32[]{:S(2)}) collective-permute-start(bf16[5,128,128]{2,1,0:T(8,128)(2,1)} %bitcast.4), channel_id=1, source_target_pairs={{0,24},{8,0},{16,8},{24,16},{1,25},{9,1},{17,9},{25,17},{2,26},{10... | collective-permute-start | bytes 491528 | tf_op jit(solution)/shard_map/ppermute | solution.py:718
  4.6 0.5 %collective-permute-start.3 = (bf16[5,128,128]{2,1,0:T(8,128)(2,1)}, bf16[5,128,128]{2,1,0:T(8,128)(2,1)S(1)}, u32[]{:S(2)}, u32[]{:S(2)}) collective-permute-start(bf16[5,128,128]{2,1,0:T(8,128)(2,1)} %bitcast.5), channel_id=1, source_target_pairs={{0,16},{8,24},{16,0},{24,8},{1,17},{9,25},{17,1},{25,9},{2,18},{10... | collective-permute-start | bytes 491528 | tf_op jit(solution)/shard_map/ppermute | solution.py:718
  5.1 0.6 %collective-permute-start.2 = (bf16[5,128,128]{2,1,0:T(8,128)(2,1)}, bf16[5,128,128]{2,1,0:T(8,128)(2,1)S(1)}, u32[]{:S(2)}, u32[]{:S(2)}) collective-permute-start(bf16[5,128,128]{2,1,0:T(8,128)(2,1)} %bitcast.6), channel_id=1, source_target_pairs={{0,8},{8,16},{16,24},{24,0},{1,9},{9,17},{17,25},{25,1},{2,10},{10... | collective-permute-start | bytes 491528 | tf_op jit(solution)/shard_map/ppermute | solution.py:718
  5.7 3.2 %prepare.1 = (f32[5,8,128]{2,1,0:T(8,128)S(1)}, f32[5,8,128]{2,1,0:T(8,128)S(1)}, f32[5,128,128]{2,1,0:T(8,128)S(1)}, f32[5,128,128]{2,1,0:T(8,128)S(1)}, bf16[1...) custom-call(s32[96]{0:T(128)} %blade_group.1, ...), custom_call_target="tpu_custom_call" | custom-call | flops 100000000 | bytes 1000000 | tf_op jit(solution)/shard_map/prepare/pallas_call | solution.py:724
  8.8 0.0 copy-start
  8.9 0.0 copy-start.4
  8.9 0.0 copy-start.2
  8.9 0.1 collective-permute-start
  9.0 3.7 %collective-permute-start.1 = (bf16[160,128]{1,0:T(8,128)(2,1)S(1)}, bf16[160,128]{1,0:T(8,128)(2,1)S(1)}, u32[]{:S(2)}, u32[]{:S(2)}) collective-permute-start(bf16[160,128]{1,0:T(8,128)(2,1)S(1)} %get-tuple-element.40.sb), channel_id=1, source_target_pairs={{0,7},{1,2},{2,1},{3,4},{4,3},{5,6},{6,5},{7,0},{8,15},{9,10},{10,... | collective-permute-start | bytes 122888 | tf_op jit(solution)/shard_map/ppermute | solution.py:695
  12.7 0.0 collective-permute-done.4.refs_4_
  12.7 1.3 %collective-permute-done.3.refs_3_ = bf16[5,128,128]{2,1,0:T(8,128)(2,1)S(1)} collective-permute-done((bf16[5,128,128]{2,1,0:T(8,128)(2,1)}, bf16[5,128,128]{2,1,0:T(8,128)(2,1)S(1)}, u32[]{:S(2)}, u32[]{:S(2)}) %collective-permute-start.3) | collective-permute-done | bytes 163872 | tf_op jit(solution)/shard_map/ppermute | solution.py:718
  14.0 0.0 collective-permute-done.2.refs_2_
  14.0 0.0 copy-done
  14.0 0.0 copy-done.4
  14.0 1.1 %strips.1 = (bf16[160,128]{1,0:T(8,128)(2,1)S(1)}, bf16[160,128]{1,0:T(8,128)(2,1)S(1)}, bf16[5,128,128]{2,1,0:T(8,128)(2,1)S(1)}, bf16[5,128,128]{2,1,0:T(8,128)(2,1)S(1)}, bf16[5,128,128]{2,1,0:T(8,128)(2,1)S(1)}) custom-call(s32[4]{0:T(128)} %copy-done.4, bf16[5,128,128]{2,1,0:T(8,128)(2,1)S(1)} %get-tuple-element.47.refs_1_, ...), custom_call_target="tpu_custom_call" | custom-call | flops 10000000 | bytes 1000000 | tf_op jit(solution)/shard_map/strips/pallas_call | solution.py:724
  15.1 0.0 copy-start.1
  15.1 0.1 collective-permute-start.5
  15.2 3.7 %collective-permute-start.6 = (bf16[160,128]{1,0:T(8,128)(2,1)S(1)}, bf16[160,128]{1,0:T(8,128)(2,1)S(1)}, u32[]{:S(2)}, u32[]{:S(2)}) collective-permute-start(bf16[160,128]{1,0:T(8,128)(2,1)S(1)} %get-tuple-element.50.sb), channel_id=1, source_target_pairs={{0,7},{1,2},{2,1},{3,4},{4,3},{5,6},{6,5},{7,0},{8,15},{9,10},{10,... | collective-permute-start | bytes 122888 | tf_op jit(solution)/shard_map/ppermute | solution.py:695
  18.9 0.0 collective-permute-done.ra
  18.9 0.0 collective-permute-done.1.rb
  18.9 2.1 %halo_forcing.1 = (f32[16,5,16,128]{3,2,1,0:T(8,128)S(1)}, f32[5,128,128]{2,1,0:T(8,128)S(1)}, bf16[384,128]{1,0:T(8,128)(2,1)S(1)}) custom-call(f32[5,5]{1,0:T(8,128)} %copy-done, s32[1,128]{1,0:T(1,128)S(1)} %get-tuple-element.38.link, bf16[160,128]{1,0:T(8,128)(2,1)S(1)} %get-tuple-element.39.sa, bf16[160,128]{1,0:T(8,128)(2,1)S(1)} %get-tuple-element.40.sb, ...), custom_call_target="tpu_custom_call" | custom-call | flops 100000000 | bytes 1000000 | tf_op jit(solution)/shard_map/halo_forcing/pallas_call | solution.py:724
  21.0 0.0 collective-permute-done.5.ra
  21.0 0.0 collective-permute-done.6.rb
  21.0 2.2 %halo.1 = (bf16[640,256]{1,0:T(8,128)(2,1)S(1)}, bf16[640,256]{1,0:T(8,128)(2,1)S(1)}, f32[5,128,128]{2,1,0:T(8,128)S(1)}) custom-call(f32[5,5]{1,0:T(8,128)} %copy-done, bf16[160,128]{1,0:T(8,128)(2,1)S(1)} %get-tuple-element.49.sa, bf16[160,128]{1,0:T(8,128)(2,1)S(1)} %get-tuple-element.50.sb, bf16[160,128]{1,0:T(8,128)(2,1)S(1)} %collective-permute-done.5.ra, ...), custom_call_target="tpu_custom_call" | custom-call | flops 100000000 | bytes 1000000 | tf_op jit(solution)/shard_map/halo/pallas_call | solution.py:724
  23.3 0.0 copy-done.2
  23.3 0.0 copy-start.3
  23.3 6.9 %first_steps.1 = (f32[5120,128]{1,0:T(8,128)S(1)}, f32[9,128,128]{2,1,0:T(8,128)S(1)}, f32[2,4]{1,0:T(2,128)S(1)}) custom-call(f32[5,5]{1,0:T(8,128)} %copy-done, s32[128]{0:T(128)} %copy-done.2, f32[5,128,128]{2,1,0:T(8,128)S(1)} %get-tuple-element.37.forcing, f32[5,128,128]{2,1,0:T(8,128)S(1)} %get-tuple-element.43.fe, ...), custom_call_target="tpu_custom_call" | custom-call | flops 1000000000 | bytes 1000000 | tf_op jit(solution)/shard_map/first_steps/pallas_call | solution.py:724
  30.2 0.2 collective-permute-start.7
  30.4 0.0 copy-done.1
  30.4 0.0 copy-done.3
  30.4 5.4 %last_step.1 = f32[40,128,128]{2,1,0:T(8,128)} custom-call(f32[5,5]{1,0:T(8,128)S(1)} %copy-done.1, s32[128]{0:T(128)S(1)} %copy-done.3, f32[5120,128]{1,0:T(8,128)S(1)} %get-tuple-element.64.refs_0_, f32[9,128,128]{2,1,0:T(8,128)S(1)} %get-tuple-element.65.refs_1_, bf16[640,256]{1,0:T(8,128)(2,1)S(1)} %get-tuple-element.66.refs_2_, ...), custom_call_target="tpu_custom_call" | custom-call | flops 1000000000 | bytes 1000000 | tf_op jit(solution)/shard_map/last_step/pallas_call | solution.py:837
  35.8 0.0 collective-permute-done.7
  35.9 1.7 %collective-permute-start.8 = (f32[2,4]{1,0:T(2,128)S(1)}, f32[2,4]{1,0:T(2,128)S(1)}, u32[]{:S(2)}, u32[]{:S(2)}) collective-permute-start(f32[2,4]{1,0:T(2,128)S(1)} %add.9), channel_id=1, source_target_pairs={{0,2},{1,3},{2,0},{3,1},{4,6},{5,7},{6,4},{7,5},{8,10},{9,11},{10,... | collective-permute-start | bytes 104 | tf_op jit(solution)/shard_map/ppermute | solution.py:689
  37.5 2.0 %collective-permute-done.8 = f32[2,4]{1,0:T(2,128)S(1)} collective-permute-done((f32[2,4]{1,0:T(2,128)S(1)}, f32[2,4]{1,0:T(2,128)S(1)}, u32[]{:S(2)}, u32[]{:S(2)}) %collective-permute-start.8) | collective-permute-done | bytes 64 | tf_op jit(solution)/shard_map/ppermute | solution.py:689
  39.5 0.6 %collective-permute-start.9 = (f32[2,4]{1,0:T(2,128)S(1)}, f32[2,4]{1,0:T(2,128)S(1)}, u32[]{:S(2)}, u32[]{:S(2)}) collective-permute-start(f32[2,4]{1,0:T(2,128)S(1)} %add.10), channel_id=1, source_target_pairs={{0,1},{1,0},{2,3},{3,2},{4,5},{5,4},{6,7},{7,6},{8,9},{9,8},{10,11... | collective-permute-start | bytes 104 | tf_op jit(solution)/shard_map/ppermute | solution.py:689
  40.1 0.8 %collective-permute-done.9 = f32[2,4]{1,0:T(2,128)S(1)} collective-permute-done((f32[2,4]{1,0:T(2,128)S(1)}, f32[2,4]{1,0:T(2,128)S(1)}, u32[]{:S(2)}, u32[]{:S(2)}) %collective-permute-start.9) | collective-permute-done | bytes 64 | tf_op jit(solution)/shard_map/ppermute | solution.py:689
  41.0 0.6 %add.11 = f32[2,4]{1,0:T(2,128)} add(f32[2,4]{1,0:T(2,128)S(1)} %add.10, f32[2,4]{1,0:T(2,128)S(1)} %collective-permute-done.9) | non-fusion elementwise | flops 8 | bytes 96 | tf_op jit(solution)/shard_map/add | solution.py:689
  (2 shorter events, 0.0 us)
Async XLA Ops:
  0.6 12.0 %collective-permute-start.4 = (bf16[5,128,128]{2,1,0:T(8,128)(2,1)}, bf16[5,128,128]{2,1,0:T(8,128)(2,1)S(1)}, u32[]{:S(2)}, u32[]{:S(2)}) collective-permute-start(bf16[5,128,128]{2,1,0:T(8,128)(2,1)} %bitcast.4), channel_id=1, source_target_pairs={{0,24},{8,0},{16,8},{24,16},{1,25},{9,1},{17,9},{25,17},{2,26},{10... | collective-permute-start | bytes 491528 | tf_op jit(solution)/shard_map/ppermute | solution.py:718
  4.6 9.4 %collective-permute-start.3 = (bf16[5,128,128]{2,1,0:T(8,128)(2,1)}, bf16[5,128,128]{2,1,0:T(8,128)(2,1)S(1)}, u32[]{:S(2)}, u32[]{:S(2)}) collective-permute-start(bf16[5,128,128]{2,1,0:T(8,128)(2,1)} %bitcast.5), channel_id=1, source_target_pairs={{0,16},{8,24},{16,0},{24,8},{1,17},{9,25},{17,1},{25,9},{2,18},{10... | collective-permute-start | bytes 491528 | tf_op jit(solution)/shard_map/ppermute | solution.py:718
  5.1 8.9 %collective-permute-start.2 = (bf16[5,128,128]{2,1,0:T(8,128)(2,1)}, bf16[5,128,128]{2,1,0:T(8,128)(2,1)S(1)}, u32[]{:S(2)}, u32[]{:S(2)}) collective-permute-start(bf16[5,128,128]{2,1,0:T(8,128)(2,1)} %bitcast.6), channel_id=1, source_target_pairs={{0,8},{8,16},{16,24},{24,0},{1,9},{9,17},{17,25},{25,1},{2,10},{10... | collective-permute-start | bytes 491528 | tf_op jit(solution)/shard_map/ppermute | solution.py:718
  8.8 5.1 %copy-start = (f32[5,5]{1,0:T(8,128)}, f32[5,5]{1,0:T(8,128)S(1)}, u32[]{:S(2)}) copy-start(f32[5,5]{1,0:T(8,128)S(1)} %get-tuple-element.35.fm) | copy-start | bytes 304
  8.9 5.1 %copy-start.4 = (s32[4]{0:T(128)}, s32[4]{0:T(128)S(1)}, u32[]{:S(2)}) copy-start(s32[4]{0:T(128)S(1)} %get-tuple-element.46.refs_0_) | copy-start | bytes 52
  8.9 14.4 %copy-start.2 = (s32[128]{0:T(128)}, s32[128]{0:T(128)S(1)}, u32[]{:S(2)}) copy-start(s32[128]{0:T(128)S(1)} %get-tuple-element.36.inv) | copy-start | bytes 1540
  8.9 10.0 %collective-permute-start = (bf16[160,128]{1,0:T(8,128)(2,1)S(1)}, bf16[160,128]{1,0:T(8,128)(2,1)S(1)}, u32[]{:S(2)}, u32[]{:S(2)}) collective-permute-start(bf16[160,128]{1,0:T(8,128)(2,1)S(1)} %get-tuple-element.39.sa), channel_id=1, source_target_pairs={{0,1},{1,0},{2,3},{3,2},{4,5},{5,4},{6,7},{7,6},{8,9},{9,8},{10,11... | collective-permute-start | bytes 122888 | tf_op jit(solution)/shard_map/ppermute | solution.py:694
  9.0 9.9 %collective-permute-start.1 = (bf16[160,128]{1,0:T(8,128)(2,1)S(1)}, bf16[160,128]{1,0:T(8,128)(2,1)S(1)}, u32[]{:S(2)}, u32[]{:S(2)}) collective-permute-start(bf16[160,128]{1,0:T(8,128)(2,1)S(1)} %get-tuple-element.40.sb), channel_id=1, source_target_pairs={{0,7},{1,2},{2,1},{3,4},{4,3},{5,6},{6,5},{7,0},{8,15},{9,10},{10,... | collective-permute-start | bytes 122888 | tf_op jit(solution)/shard_map/ppermute | solution.py:695
  15.1 15.3 %copy-start.1 = (f32[5,5]{1,0:T(8,128)S(1)}, f32[5,5]{1,0:T(8,128)}, u32[]{:S(2)}) copy-start(f32[5,5]{1,0:T(8,128)} %copy-done) | copy-start | bytes 304
  15.1 5.9 %collective-permute-start.5 = (bf16[160,128]{1,0:T(8,128)(2,1)S(1)}, bf16[160,128]{1,0:T(8,128)(2,1)S(1)}, u32[]{:S(2)}, u32[]{:S(2)}) collective-permute-start(bf16[160,128]{1,0:T(8,128)(2,1)S(1)} %get-tuple-element.49.sa), channel_id=1, source_target_pairs={{0,1},{1,0},{2,3},{3,2},{4,5},{5,4},{6,7},{7,6},{8,9},{9,8},{10,11... | collective-permute-start | bytes 122888 | tf_op jit(solution)/shard_map/ppermute | solution.py:694
  15.2 5.8 %collective-permute-start.6 = (bf16[160,128]{1,0:T(8,128)(2,1)S(1)}, bf16[160,128]{1,0:T(8,128)(2,1)S(1)}, u32[]{:S(2)}, u32[]{:S(2)}) collective-permute-start(bf16[160,128]{1,0:T(8,128)(2,1)S(1)} %get-tuple-element.50.sb), channel_id=1, source_target_pairs={{0,7},{1,2},{2,1},{3,4},{4,3},{5,6},{6,5},{7,0},{8,15},{9,10},{10,... | collective-permute-start | bytes 122888 | tf_op jit(solution)/shard_map/ppermute | solution.py:695
  23.3 7.1 %copy-start.3 = (s32[128]{0:T(128)S(1)}, s32[128]{0:T(128)}, u32[]{:S(2)}) copy-start(s32[128]{0:T(128)} %copy-done.2) | copy-start | bytes 1540
  30.2 5.6 %collective-permute-start.7 = (f32[2,4]{1,0:T(2,128)S(1)}, f32[2,4]{1,0:T(2,128)S(1)}, u32[]{:S(2)}, u32[]{:S(2)}) collective-permute-start(f32[2,4]{1,0:T(2,128)S(1)} %get-tuple-element.67), channel_id=1, source_target_pairs={{0,4},{1,5},{2,6},{3,7},{4,0},{5,1},{6,2},{7,3},{8,12},{9,13},{10,... | collective-permute-start | bytes 104 | tf_op jit(solution)/shard_map/ppermute | solution.py:689
  35.9 3.6 %collective-permute-start.8 = (f32[2,4]{1,0:T(2,128)S(1)}, f32[2,4]{1,0:T(2,128)S(1)}, u32[]{:S(2)}, u32[]{:S(2)}) collective-permute-start(f32[2,4]{1,0:T(2,128)S(1)} %add.9), channel_id=1, source_target_pairs={{0,2},{1,3},{2,0},{3,1},{4,6},{5,7},{6,4},{7,5},{8,10},{9,11},{10,... | collective-permute-start | bytes 104 | tf_op jit(solution)/shard_map/ppermute | solution.py:689
  39.5 1.5 %collective-permute-start.9 = (f32[2,4]{1,0:T(2,128)S(1)}, f32[2,4]{1,0:T(2,128)S(1)}, u32[]{:S(2)}, u32[]{:S(2)}) collective-permute-start(f32[2,4]{1,0:T(2,128)S(1)} %add.10), channel_id=1, source_target_pairs={{0,1},{1,0},{2,3},{3,2},{4,5},{5,4},{6,7},{7,6},{8,9},{9,8},{10,11... | collective-permute-start | bytes 104 | tf_op jit(solution)/shard_map/ppermute | solution.py:689

commit v4 on v3

--- a/solution.py
+++ b/solution.py
@@ -36,15 +36,14 @@
 LINK_ROW = PARTS * FW
 SEG = 16
 HALF = SEG // 2
+HALO_LANES = (2, 3, 5, 12, 13, 14)
 VMEM_LIMIT = 40 * 2**20
 SMALL_LIMIT = 16 * 2**20
-PARTS_LAST = 1
 
 VMEM = pl.BlockSpec(memory_space=pltpu.VMEM)
 SMEM = pl.BlockSpec(memory_space=pltpu.SMEM)
 HBM = pl.BlockSpec(memory_space=pltpu.HBM)
 UNIT = time_step * fourth_diff
-CENTRE = round(C0 / UNIT)
 NEAR = round(C1 / UNIT)
 F32 = jnp.float32
 BF16 = jnp.bfloat16
@@ -280,44 +279,28 @@
 
 def stencil_selects(width):
     blocks = width // SEG
-    inner = np.zeros((2, width, 2 * width), np.float32)
-    outer = np.zeros((blocks, 2, width, 2 * width), np.float32)
+    out = np.zeros((blocks, 2, width, 2 * width), np.float32)
 
     def spread(column):
-        out = []
-        for c, w in ((column + 1, 1.0), (column - 1, -1.0)):
-            if 0 <= c < width:
-                out.append((c, w))
-        for c, w in (
-            (column, CENTRE),
-            (column - 1, NEAR),
-            (column + 1, NEAR),
-            (column - 2, -1.0),
-            (column + 2, -1.0),
-        ):
-            if 0 <= c < width:
-                out.append((width + c, w))
-        return out
+        near = ((1, 1.0), (-1, -1.0))
+        far = ((-1, NEAR), (1, NEAR), (-2, -1.0), (2, -1.0))
+        pairs = [(column + d, w) for d, w in near if 0 <= column + d < width]
+        return pairs + [(width + column + d, w) for d, w in far if 0 <= column + d < width]
 
     for column in range(width):
         for lane, w in spread(column):
-            inner[:, column, lane] = w
+            out[:, :, column, lane] = w
     for j in range(blocks):
         for p, column in ((2, -2), (3, -1), (HALF + QW, width), (HALF + QW + 1, width + 1)):
-            for lane, w in spread(column):
-                outer[j, :, j * SEG + p, lane] = w
-    return (
-        inner.reshape(2 * width, 2 * width).astype(jnp.bfloat16),
-        outer.reshape(blocks, 2 * width, 2 * width)
-        .swapaxes(0, 1)
-        .reshape(2 * width, blocks * 2 * width)
-        .astype(jnp.bfloat16),
-    )
-
-
-def halves(x):
-    hi = x.astype(BF16)
-    return jnp.concatenate([hi, (x - hi.astype(F32)).astype(BF16)], axis=1)
+            for held in (p, p + 2) if column in (-1, width) else (p,):
+                out[j, 1, j * SEG + held] = 0.0
+                for to, w in spread(column):
+                    out[j, 1, j * SEG + held, to] = w
+    return out.reshape(blocks, 2 * width, 2 * width).astype(jnp.bfloat16)
+
+
+def high(x):
+    return x.astype(BF16).astype(F32)
 
 
 def gather_sources(sa, sb, ra, rb):
@@ -451,6 +434,13 @@
     for f in range(FIELDS):
         q_ref[f] = part(0, f, 1)
     kp = [kp_ref[i] for i in range(5)]
+    p = lax.broadcasted_iota(jnp.int32, (8, width), 1) & (SEG - 1)
+    holds_high = (p != 5) & (p != 14)
+
+    def both_halves(x):
+        top = high(x)
+        return jnp.where(holds_high, top, pltpu.roll(x - top, 2, 1))
+
 
     def body(r, c):
         def row(ref, index):
@@ -473,13 +463,13 @@
             )
         moved = flux(fmc, [row(q_ref, (f,)) for f in range(FIELDS)], d)
         at = pl.ds(pl.multiple_of(r * (FIELDS * 8), 8), FIELDS * 8)
-        e1_ref[at, :] = halves(jnp.concatenate(mu, axis=0))
-        e2_ref[at, :] = halves(
-            jnp.concatenate([b - m for b, m in zip(base, moved)], axis=0)
+        e1_ref[at, :] = jnp.concatenate([both_halves(x) for x in mu], axis=0)
+        e2_ref[at, :] = jnp.concatenate(
+            [both_halves(b - m) for b, m in zip(base, moved)], axis=0
         )
         return c
 
-    lax.fori_loop(0, step, body, 0, unroll=8)
+    lax.fori_loop(0, step, body, 0, unroll=16)
 
 
 def shift_edges(x, edge, lane, width):
@@ -507,23 +497,29 @@
     return [[jnp.full((8, width), fmc[f, e]) for e in range(FIELDS)] for f in range(FIELDS)]
 
 
-def stencil_products(dz, dze, source, first, count, edges, inner, outer, lanes):
-    dz[...] = mm(halves(source[first : first + count, :]), inner[...])
-    dze[...] = mm(edges[...], outer[:, lanes])
-
-
-def step_row(source, dz, dze, coef, fmv, linked, r, local, j, chunk):
+def stencil_products(dz, source, edges, products):
     width = source.shape[1]
-
-    def both(f, half):
-        own = dz[place(local, f), half * width : (half + 1) * width]
-        lanes = pl.ds(pl.multiple_of(j * (2 * width) + half * width, width), width)
-        return own + dze[chunk + f * 8 : chunk + f * 8 + 8, lanes]
-
-    d = [both(f, 0) for f in range(FIELDS)]
+    count = edges.shape[0]
+    lane = lax.broadcasted_iota(jnp.int32, (count, width), 1)
+    p = lane & (SEG - 1)
+    halo = functools.reduce(jnp.logical_or, [p == held for held in HALO_LANES])
+    for j in range(products.shape[0]):
+        x = source[j * count : (j + 1) * count, :]
+        top = x.astype(BF16)
+        rest = jnp.where(halo & (lane // SEG == j), edges[...], x - top.astype(F32))
+        dz[j * count : (j + 1) * count, :] = mm(
+            jnp.concatenate([top, rest.astype(BF16)], axis=1), products[j]
+        )
+
+
+def step_row(source, dz, coef, fmv, linked, r):
+    width = source.shape[1]
+
+    d = [dz[place(r, f), :width] for f in range(FIELDS)]
     out = []
     for e in range(FIELDS):
-        value = UNIT * both(e, 1) + CP * source[place(linked, e), :]
+        value = C0 * source[place(r, e), :] + UNIT * dz[place(r, e), width:]
+        value = value + CP * source[place(linked, e), :]
         for f in range(FIELDS):
             if f == e:
                 m = spread(coef, (e,), r)
@@ -537,9 +533,9 @@
 
 
 def first_steps_kernel(
-    cycle, fm, inv, forcing, fe, b0, v0, qe, k_ref, inner, outer, e1, q0, q1, q2,
+    cycle, fm, inv, forcing, fe, b0, v0, qe, k_ref, products, e1, q0, q1, q2,
     mu2, coef0, sens_ref,
-    bs, coef1, mu1, dz, dze, weighted, heavy, fmc,
+    bs, coef1, mu1, dz, weighted, heavy, fmc,
 ):
     rows, width = forcing.shape[1], forcing.shape[2]
     total = cycle * width
@@ -617,13 +613,13 @@
 
     acc = lax.fori_loop(0, blocks, first, (zero,) * FIELDS)
     fmv = matrix_rows(fmc, width)
-    stencil_products(dz, dze, mu1, 0, rows * FIELDS * 8, e1, inner, outer, slice(None))
+    stencil_products(dz, mu1, e1, products)
 
     def second(j, acc):
         acc = list(acc)
         for i in range(size):
             r = j * size + i
-            made = step_row(mu1, dz, dze, coef1, fmv, inv[r], r, r, j, i * FIELDS * 8)
+            made = step_row(mu1, dz, coef1, fmv, inv[r], r)
             for f, value in enumerate(made):
                 value = value + spread(forcing, (f,), r) * k[2]
                 mu2[place(r, f), :] = value
@@ -640,35 +636,23 @@
         sens_ref[group : group + 1, :] = jnp.sum(mine, axis=0, keepdims=True)[:, :AMP]
 
 
-def last_step_kernel(part, parts, fm, inv, *refs):
-    mu2, coef0, e2, inner, outer = refs[-11:-6]
-    out_hbm, dz, dze, stage, fmc, out_sems = refs[-6:]
+def last_step_kernel(fm, inv, mu2, coef0, e2, products, out_hbm, dz, stage, fmc, out_sems):
     rows, width = coef0.shape[1:]
     blocks = width // SEG
     size = rows // blocks
-    here = blocks // parts
-    begin = part * here
     scaled_matrix(fm, fmc)
     fmv = matrix_rows(fmc, width)
-    chunk = size * FIELDS * 8
-    lanes = slice(begin * 2 * width, (begin + here) * 2 * width)
-    stencil_products(dz, dze, mu2, begin * chunk, here * chunk, e2, inner, outer, lanes)
+    stencil_products(dz, mu2, e2, products)
 
     def send(j):
         at = pl.ds(pl.multiple_of(j * 8, 8), 8)
-        to = pl.ds(pl.multiple_of(begin * size + j * 8, 8), 8)
-        return pltpu.make_async_copy(stage.at[:, at, :], out_hbm.at[:, to, :], out_sems.at[j])
+        return pltpu.make_async_copy(stage.at[:, at, :], out_hbm.at[:, at, :], out_sems.at[j])
 
     def third(j, c):
         for half in range(size // 8):
-            made = []
-            for i in range(half * 8, half * 8 + 8):
-                local = j * size + i
-                r = begin * size + local
-                made.append(
-                    step_row(mu2, dz, dze, coef0, fmv, inv[r], r, local, j, i * FIELDS * 8)
-                )
-            at = pl.ds(pl.multiple_of(j * size + half * 8, 8), 8)
+            r0 = j * size + half * 8
+            made = [step_row(mu2, dz, coef0, fmv, inv[r0 + i], r0 + i) for i in range(8)]
+            at = pl.ds(pl.multiple_of(r0, 8), 8)
             for e in range(FIELDS):
                 turned = jnp.swapaxes(jnp.stack([x[e] for x in made]), 0, 1)
                 for pair in range(PAIRS):
@@ -676,8 +660,8 @@
             send(j * (size // 8) + half).start()
         return c
 
-    lax.fori_loop(0, here, third, 0)
-    for j in range(here * size // 8):
+    lax.fori_loop(0, blocks, third, 0)
+    for j in range(rows // 8):
         send(j).wait()
 
 
@@ -734,7 +718,7 @@
 
     kept = (
         forcing, row_link, forcing_select(width), slot, state_select(width),
-        *halo_selects(width), *stencil_selects(width),
+        *halo_selects(width), stencil_selects(width),
     )
     made = (
         factors, factors, field, field, strip, strip,
@@ -754,7 +738,7 @@
         (VMEM,) * 6 + (SMEM,) * 3 + (VMEM,) * len(kept),
     )
     forcing_v, link, _, slot_v, state_sel, *held = held
-    forcing_tiled, state_tiled, edge, state_edge, inner, outer = held
+    forcing_tiled, state_tiled, edge, state_edge, products = held
     f_sent = (f_a, f_b, *to_neighbours(f_a, f_b, cycle))
 
     q_a, q_b, *chosen = call(
@@ -781,38 +765,43 @@
         10**8,
         "halo_forcing",
     )
-    edge_struct = struct((step_rows * FIELDS * 8, 2 * width), BF16)
-    e1, e2, qe = call(
-        halo_kernel,
-        (edge_struct, edge_struct, field),
-        (fm_s,),
-        (),
-        (*q_sent, state_tiled, state_edge, kp, hot, y),
-        [
-            like(y),
-            pltpu.VMEM((blocks * 4 * SLOT, state_tiled.shape[1]), BF16),
-            pltpu.VMEM((FIELDS, step_rows, width), F32),
-            pltpu.SMEM((FIELDS, FIELDS), F32),
-        ],
-        SMALL_LIMIT,
-        10**8,
-        "halo",
-    )
     flat = rows * FIELDS * PAIRS
     coefficients = (2 * FIELDS - 1, rows, width)
-    outside = (flat // blocks, blocks * 2 * width)
-    mu2, coef0, sens = call(
-        functools.partial(first_steps_kernel, cycle),
-        (struct((flat, width)), struct(coefficients), struct((GRP_DEV, AMP))),
+    edges = (step_rows * FIELDS * 8, width)
+    halo_operands = (*q_sent, state_tiled, state_edge, kp, hot, y)
+    halo_scratch = [
+        pltpu.VMEM(edges, F32),
+        pltpu.VMEM((FIELDS, rows, width), F32),
+        like(y),
+        pltpu.VMEM((blocks * 4 * SLOT, state_tiled.shape[1]), BF16),
+        pltpu.VMEM((FIELDS, step_rows, width), F32),
+        pltpu.SMEM((FIELDS, FIELDS), F32),
+    ]
+
+    def halo_and_first_steps(fm, inv, *refs):
+        halo_in, refs = refs[: len(halo_operands)], refs[len(halo_operands) :]
+        forcing, fe, b0, v0, k_ref, products, q0, q1, q2 = refs[:9]
+        mu2, coef0, sens, e2, e1, qe, *work = refs[9 : 13 + len(halo_scratch)]
+        halo_kernel(fm, *halo_in, e1, e2, qe, *work)
+        first_steps_kernel(
+            cycle, fm, inv, forcing, fe, b0, v0, qe, k_ref, products, e1, q0, q1, q2,
+            mu2, coef0, sens, *refs[13 + len(halo_scratch) :],
+        )
+
+    mu2, coef0, sens, e2 = call(
+        halo_and_first_steps,
+        (
+            struct((flat, width)), struct(coefficients), struct((GRP_DEV, AMP)), struct(edges),
+        ),
         (fm_s, inv),
         (),
-        (forcing_v, fe, b0, v0, qe, k, inner, outer, e1, *chosen),
-        [
+        (*halo_operands, forcing_v, fe, b0, v0, k, products, *chosen),
+        halo_scratch
+        + [
             pltpu.VMEM((4, FIELDS, rows, width), F32),
             pltpu.VMEM(coefficients, F32),
             pltpu.VMEM((flat, width), F32),
             pltpu.VMEM((flat, 2 * width), F32),
-            pltpu.VMEM(outside, F32),
             pltpu.VMEM((FIELDS, rows, width), F32),
             pltpu.VMEM((FIELDS, rows, width), F32),
             pltpu.SMEM((FIELDS, FIELDS), F32),
@@ -827,30 +816,25 @@
     exact = 1 << len(bits) == cycle
     if not exact:
         sens = lax.psum(sens, "blk")
-    adjoint = None
-    for part in range(PARTS_LAST):
-        if part:
-            adjoint, sens = lax.optimization_barrier((adjoint, sens))
-        if exact and bits:
-            sens = round_over(sens, "blk", bits.pop(0))
-        before = () if adjoint is None else (adjoint,)
-        adjoint = pl.pallas_call(
-            functools.partial(last_step_kernel, part, PARTS_LAST),
-            out_shape=struct((pairs_fields, rows, width)),
-            in_specs=[SMEM] * 2 + [HBM] * len(before) + [VMEM] * 5,
-            out_specs=HBM,
-            scratch_shapes=[
-                pltpu.VMEM((flat // PARTS_LAST, 2 * width), F32),
-                pltpu.VMEM((flat // blocks, blocks // PARTS_LAST * 2 * width), F32),
-                pltpu.VMEM((pairs_fields, rows // PARTS_LAST, width), F32),
-                pltpu.SMEM((FIELDS, FIELDS), F32),
-                sems((rows // 8 // PARTS_LAST,)),
-            ],
-            input_output_aliases={2: 0} if before else {},
-            compiler_params=pltpu.CompilerParams(vmem_limit_bytes=SMALL_LIMIT),
-            cost_estimate=cost(10**9, 10**6),
-            name="last_step",
-        )(fm_s, inv, *before, mu2, coef0, e2, inner, outer)
+    if exact and bits:
+        sens = round_over(sens, "blk", bits.pop(0))
+    (adjoint,) = call(
+        last_step_kernel,
+        (struct((pairs_fields, rows, width)),),
+        (fm_s, inv),
+        (),
+        (mu2, coef0, e2, products),
+        [
+            pltpu.VMEM((flat, 2 * width), F32),
+            pltpu.VMEM((pairs_fields, rows, width), F32),
+            pltpu.SMEM((FIELDS, FIELDS), F32),
+            sems((rows // 8,)),
+        ],
+        VMEM_LIMIT,
+        10**9,
+        "last_step",
+        (HBM,),
+    )
     for bit in bits if exact else ():
         sens = round_over(sens, "blk", bit)
     return adjoint.reshape(GRP_DEV, AMP, FIELDS, rows, width), sens

time: 41.8 us -> 39.4 us (0.943)
  Pallas kernels: 20.9 us -> 18.6 us
    pallas_call x1 -> x0, Pallas kernels: 5.4 us -> none  [on_device(): pl.pallas_call(functools.partial(last_step_kernel, part, PARTS_LAST), out...]
    pallas_call x5, Pallas kernels: 15.5 us -> 18.6 us  [call(): pl.pallas_call(kernel, out_shape=out_shape, in_specs=[SMEM] * len(smem) +...]
where the time goes in v4:
time: 39.4 us; the launch traced here: 39.1 us
  Pallas kernels  18.6 us (47%)
  starting transfers between devices  15.1 us (38%)
  waiting for transfers between devices  4.14 us (11%)
  between operations  0.75 us (2%)
  other arithmetic  0.57 us (1%)
    pallas_call x5, Pallas kernels, call(): pl.pallas_call(kernel, out_shape=out_shape, in_specs=[SMEM] * len(smem) +...  18.6 us
    ppermute x2, starting transfers between devices, to_neighbours(): lax.ppermute(send_b, 'blk', [(i, (i + 1) % cycle if i % 2 else (i - 1) %...  7.4 us
    ppermute x3, starting transfers between devices, on_device(): lax.ppermute(slot, 'out', shift_pairs(n_out, k))  5.04 us
    ppermute x3, waiting for transfers between devices, round_over(): lax.ppermute(x, axis, [(i, i ^ bit) for i in range(lax.axis_size(axis))])  2.81 us
    ppermute x3, starting transfers between devices, round_over(): lax.ppermute(x, axis, [(i, i ^ bit) for i in range(lax.axis_size(axis))])  2.49 us
    ppermute x3, waiting for transfers between devices, on_device(): lax.ppermute(slot, 'out', shift_pairs(n_out, k))  1.32 us
  transfers between devices with their start and end apart: 10, of which 3 were waited for; matrix products, arithmetic and copies ran while one was open for 0% of the time, Pallas kernels for 28%

profile of v4, /device:TPU:0, one launch (start us, length us, event | category | flops | bytes accessed | tf_op | source)
XLA Modules:
  0.0 39.1 jit_solution(8049696551166507196)
XLA Ops:
  0.6 3.9 %collective-permute-start.2 = (bf16[5,128,128]{2,1,0:T(8,128)(2,1)}, bf16[5,128,128]{2,1,0:T(8,128)(2,1)S(1)}, u32[]{:S(2)}, u32[]{:S(2)}) collective-permute-start(bf16[5,128,128]{2,1,0:T(8,128)(2,1)} %bitcast.4), channel_id=1, source_target_pairs={{0,24},{8,0},{16,8},{24,16},{1,25},{9,1},{17,9},{25,17},{2,26},{10... | collective-permute-start | bytes 491528 | tf_op jit(solution)/shard_map/ppermute | solution.py:702
  4.6 0.5 %collective-permute-start.1 = (bf16[5,128,128]{2,1,0:T(8,128)(2,1)}, bf16[5,128,128]{2,1,0:T(8,128)(2,1)S(1)}, u32[]{:S(2)}, u32[]{:S(2)}) collective-permute-start(bf16[5,128,128]{2,1,0:T(8,128)(2,1)} %bitcast.5), channel_id=1, source_target_pairs={{0,16},{8,24},{16,0},{24,8},{1,17},{9,25},{17,1},{25,9},{2,18},{10... | collective-permute-start | bytes 491528 | tf_op jit(solution)/shard_map/ppermute | solution.py:702
  5.1 0.6 %collective-permute-start = (bf16[5,128,128]{2,1,0:T(8,128)(2,1)}, bf16[5,128,128]{2,1,0:T(8,128)(2,1)S(1)}, u32[]{:S(2)}, u32[]{:S(2)}) collective-permute-start(bf16[5,128,128]{2,1,0:T(8,128)(2,1)} %bitcast.6), channel_id=1, source_target_pairs={{0,8},{8,16},{16,24},{24,0},{1,9},{9,17},{17,25},{25,1},{2,10},{10... | collective-permute-start | bytes 491528 | tf_op jit(solution)/shard_map/ppermute | solution.py:702
  5.7 3.1 %prepare.1 = (f32[5,8,128]{2,1,0:T(8,128)S(1)}, f32[5,8,128]{2,1,0:T(8,128)S(1)}, f32[5,128,128]{2,1,0:T(8,128)S(1)}, f32[5,128,128]{2,1,0:T(8,128)S(1)}, bf16[1...) custom-call(s32[96]{0:T(128)} %blade_group.1, ...), custom_call_target="tpu_custom_call" | custom-call | flops 100000000 | bytes 1000000 | tf_op jit(solution)/shard_map/prepare/pallas_call | solution.py:708
  8.8 0.0 copy-start.2
  8.8 0.0 copy-start
  8.9 0.0 copy-start.1
  8.9 0.1 collective-permute-start.5
  8.9 3.7 %collective-permute-start.6 = (bf16[160,128]{1,0:T(8,128)(2,1)S(1)}, bf16[160,128]{1,0:T(8,128)(2,1)S(1)}, u32[]{:S(2)}, u32[]{:S(2)}) collective-permute-start(bf16[160,128]{1,0:T(8,128)(2,1)S(1)} %get-tuple-element.44.sb), channel_id=1, source_target_pairs={{0,7},{1,2},{2,1},{3,4},{4,3},{5,6},{6,5},{7,0},{8,15},{9,10},{10,... | collective-permute-start | bytes 122888 | tf_op jit(solution)/shard_map/ppermute | solution.py:679
  12.6 0.0 collective-permute-done.2.refs_4_
  12.6 1.3 %collective-permute-done.1.refs_3_ = bf16[5,128,128]{2,1,0:T(8,128)(2,1)S(1)} collective-permute-done((bf16[5,128,128]{2,1,0:T(8,128)(2,1)}, bf16[5,128,128]{2,1,0:T(8,128)(2,1)S(1)}, u32[]{:S(2)}, u32[]{:S(2)}) %collective-permute-start.1) | collective-permute-done | bytes 163872 | tf_op jit(solution)/shard_map/ppermute | solution.py:702
  14.0 0.0 collective-permute-done.refs_2_
  14.0 0.0 copy-done.2
  14.0 1.1 %strips.1 = (bf16[160,128]{1,0:T(8,128)(2,1)S(1)}, bf16[160,128]{1,0:T(8,128)(2,1)S(1)}, bf16[5,128,128]{2,1,0:T(8,128)(2,1)S(1)}, bf16[5,128,128]{2,1,0:T(8,128)(2,1)S(1)}, bf16[5,128,128]{2,1,0:T(8,128)(2,1)S(1)}) custom-call(s32[4]{0:T(128)} %copy-done.2, bf16[5,128,128]{2,1,0:T(8,128)(2,1)S(1)} %get-tuple-element.35.refs_1_, ...), custom_call_target="tpu_custom_call" | custom-call | flops 10000000 | bytes 1000000 | tf_op jit(solution)/shard_map/strips/pallas_call | solution.py:708
  15.1 0.1 collective-permute-start.3
  15.2 3.7 %collective-permute-start.4 = (bf16[160,128]{1,0:T(8,128)(2,1)S(1)}, bf16[160,128]{1,0:T(8,128)(2,1)S(1)}, u32[]{:S(2)}, u32[]{:S(2)}) collective-permute-start(bf16[160,128]{1,0:T(8,128)(2,1)S(1)} %get-tuple-element.38.refs_1_), channel_id=1, source_target_pairs={{0,7},{1,2},{2,1},{3,4},{4,3},{5,6},{6,5},{7,0},{8,15},{9,10},{10,... | collective-permute-start | bytes 122888 | tf_op jit(solution)/shard_map/ppermute | solution.py:679
  18.8 0.0 collective-permute-done.5.ra
  18.9 0.0 collective-permute-done.6.rb
  18.9 0.0 copy-done
  18.9 2.1 %halo_forcing.1 = (f32[16,5,16,128]{3,2,1,0:T(8,128)S(1)}, f32[5,128,128]{2,1,0:T(8,128)S(1)}, bf16[384,128]{1,0:T(8,128)(2,1)S(1)}) custom-call(f32[5,5]{1,0:T(8,128)} %copy-done, s32[1,128]{1,0:T(1,128)S(1)} %get-tuple-element.42.link, bf16[160,128]{1,0:T(8,128)(2,1)S(1)} %get-tuple-element.43.sa, bf16[160,128]{1,0:T(8,128)(2,1)S(1)} %get-tuple-element.44.sb, ...), custom_call_target="tpu_custom_call" | custom-call | flops 100000000 | bytes 1000000 | tf_op jit(solution)/shard_map/halo_forcing/pallas_call | solution.py:708
  21.0 0.0 collective-permute-done.3.refs_2_
  21.0 0.0 collective-permute-done.4.refs_3_
  21.0 0.0 copy-done.1
  21.0 7.5 %first_steps.1 = (f32[5120,128]{1,0:T(8,128)S(1)}, f32[9,128,128]{2,1,0:T(8,128)S(1)}, f32[2,4]{1,0:T(2,128)S(1)}, f32[640,128]{1,0:T(8,128)S(1)}) custom-call(f32[5,5]{1,0:T(8,128)} %copy-done, s32[128]{0:T(128)} %copy-done.1, bf16[160,128]{1,0:T(8,128)(2,1)S(1)} %get-tuple-element.37.refs_0_, bf16[160,128]{1,0:T(8,128)(2,1)S(1)} %get-tuple-element.38.refs_1_, ...), custom_call_target="tpu_custom_call" | custom-call | flops 1000000000 | bytes 1000000 | tf_op jit(solution)/shard_map/first_steps/pallas_call | solution.py:708
  28.5 0.2 collective-permute-start.7
  28.7 4.7 %last_step.1 = f32[40,128,128]{2,1,0:T(8,128)} custom-call(f32[5,5]{1,0:T(8,128)} %copy-done, s32[128]{0:T(128)} %copy-done.1, f32[5120,128]{1,0:T(8,128)S(1)} %get-tuple-element.58.mu2, f32[9,128,128]{2,1,0:T(8,128)S(1)} %get-tuple-element.59.coef0, f32[640,128]{1,0:T(8,128)S(1)} %get-tuple-element.60.e2, ...), custom_call_target="tpu_custom_call" | custom-call | flops 1000000000 | bytes 1000000 | tf_op jit(solution)/shard_map/last_step/pallas_call | solution.py:708
  33.5 0.0 collective-permute-done.7
  33.5 1.6 %collective-permute-start.8 = (f32[2,4]{1,0:T(2,128)S(1)}, f32[2,4]{1,0:T(2,128)S(1)}, u32[]{:S(2)}, u32[]{:S(2)}) collective-permute-start(f32[2,4]{1,0:T(2,128)S(1)} %add.9), channel_id=1, source_target_pairs={{0,2},{1,3},{2,0},{3,1},{4,6},{5,7},{6,4},{7,5},{8,10},{9,11},{10,... | collective-permute-start | bytes 104 | tf_op jit(solution)/shard_map/ppermute | solution.py:673
  35.1 2.0 %collective-permute-done.8 = f32[2,4]{1,0:T(2,128)S(1)} collective-permute-done((f32[2,4]{1,0:T(2,128)S(1)}, f32[2,4]{1,0:T(2,128)S(1)}, u32[]{:S(2)}, u32[]{:S(2)}) %collective-permute-start.8) | collective-permute-done | bytes 64 | tf_op jit(solution)/shard_map/ppermute | solution.py:673
  37.1 0.6 %collective-permute-start.9 = (f32[2,4]{1,0:T(2,128)S(1)}, f32[2,4]{1,0:T(2,128)S(1)}, u32[]{:S(2)}, u32[]{:S(2)}) collective-permute-start(f32[2,4]{1,0:T(2,128)S(1)} %add.10), channel_id=1, source_target_pairs={{0,1},{1,0},{2,3},{3,2},{4,5},{5,4},{6,7},{7,6},{8,9},{9,8},{10,11... | collective-permute-start | bytes 104 | tf_op jit(solution)/shard_map/ppermute | solution.py:673
  37.8 0.8 %collective-permute-done.9 = f32[2,4]{1,0:T(2,128)S(1)} collective-permute-done((f32[2,4]{1,0:T(2,128)S(1)}, f32[2,4]{1,0:T(2,128)S(1)}, u32[]{:S(2)}, u32[]{:S(2)}) %collective-permute-start.9) | collective-permute-done | bytes 64 | tf_op jit(solution)/shard_map/ppermute | solution.py:673
  38.6 0.6 %add.11 = f32[2,4]{1,0:T(2,128)} add(f32[2,4]{1,0:T(2,128)S(1)} %add.10, f32[2,4]{1,0:T(2,128)S(1)} %collective-permute-done.9) | non-fusion elementwise | flops 8 | bytes 96 | tf_op jit(solution)/shard_map/add | solution.py:673
  (2 shorter events, 0.0 us)
Async XLA Ops:
  0.6 12.0 %collective-permute-start.2 = (bf16[5,128,128]{2,1,0:T(8,128)(2,1)}, bf16[5,128,128]{2,1,0:T(8,128)(2,1)S(1)}, u32[]{:S(2)}, u32[]{:S(2)}) collective-permute-start(bf16[5,128,128]{2,1,0:T(8,128)(2,1)} %bitcast.4), channel_id=1, source_target_pairs={{0,24},{8,0},{16,8},{24,16},{1,25},{9,1},{17,9},{25,17},{2,26},{10... | collective-permute-start | bytes 491528 | tf_op jit(solution)/shard_map/ppermute | solution.py:702
  4.6 9.4 %collective-permute-start.1 = (bf16[5,128,128]{2,1,0:T(8,128)(2,1)}, bf16[5,128,128]{2,1,0:T(8,128)(2,1)S(1)}, u32[]{:S(2)}, u32[]{:S(2)}) collective-permute-start(bf16[5,128,128]{2,1,0:T(8,128)(2,1)} %bitcast.5), channel_id=1, source_target_pairs={{0,16},{8,24},{16,0},{24,8},{1,17},{9,25},{17,1},{25,9},{2,18},{10... | collective-permute-start | bytes 491528 | tf_op jit(solution)/shard_map/ppermute | solution.py:702
  5.1 8.9 %collective-permute-start = (bf16[5,128,128]{2,1,0:T(8,128)(2,1)}, bf16[5,128,128]{2,1,0:T(8,128)(2,1)S(1)}, u32[]{:S(2)}, u32[]{:S(2)}) collective-permute-start(bf16[5,128,128]{2,1,0:T(8,128)(2,1)} %bitcast.6), channel_id=1, source_target_pairs={{0,8},{8,16},{16,24},{24,0},{1,9},{9,17},{17,25},{25,1},{2,10},{10... | collective-permute-start | bytes 491528 | tf_op jit(solution)/shard_map/ppermute | solution.py:702
  8.8 5.1 %copy-start.2 = (s32[4]{0:T(128)}, s32[4]{0:T(128)S(1)}, u32[]{:S(2)}) copy-start(s32[4]{0:T(128)S(1)} %get-tuple-element.34.refs_0_) | copy-start | bytes 52
  8.8 10.0 %copy-start = (f32[5,5]{1,0:T(8,128)}, f32[5,5]{1,0:T(8,128)S(1)}, u32[]{:S(2)}) copy-start(f32[5,5]{1,0:T(8,128)S(1)} %get-tuple-element.32.fm) | copy-start | bytes 304
  8.9 12.2 %copy-start.1 = (s32[128]{0:T(128)}, s32[128]{0:T(128)S(1)}, u32[]{:S(2)}) copy-start(s32[128]{0:T(128)S(1)} %get-tuple-element.33.inv) | copy-start | bytes 1540
  8.9 10.0 %collective-permute-start.5 = (bf16[160,128]{1,0:T(8,128)(2,1)S(1)}, bf16[160,128]{1,0:T(8,128)(2,1)S(1)}, u32[]{:S(2)}, u32[]{:S(2)}) collective-permute-start(bf16[160,128]{1,0:T(8,128)(2,1)S(1)} %get-tuple-element.43.sa), channel_id=1, source_target_pairs={{0,1},{1,0},{2,3},{3,2},{4,5},{5,4},{6,7},{7,6},{8,9},{9,8},{10,11... | collective-permute-start | bytes 122888 | tf_op jit(solution)/shard_map/ppermute | solution.py:678
  8.9 9.9 %collective-permute-start.6 = (bf16[160,128]{1,0:T(8,128)(2,1)S(1)}, bf16[160,128]{1,0:T(8,128)(2,1)S(1)}, u32[]{:S(2)}, u32[]{:S(2)}) collective-permute-start(bf16[160,128]{1,0:T(8,128)(2,1)S(1)} %get-tuple-element.44.sb), channel_id=1, source_target_pairs={{0,7},{1,2},{2,1},{3,4},{4,3},{5,6},{6,5},{7,0},{8,15},{9,10},{10,... | collective-permute-start | bytes 122888 | tf_op jit(solution)/shard_map/ppermute | solution.py:679
  15.1 5.9 %collective-permute-start.3 = (bf16[160,128]{1,0:T(8,128)(2,1)S(1)}, bf16[160,128]{1,0:T(8,128)(2,1)S(1)}, u32[]{:S(2)}, u32[]{:S(2)}) collective-permute-start(bf16[160,128]{1,0:T(8,128)(2,1)S(1)} %get-tuple-element.37.refs_0_), channel_id=1, source_target_pairs={{0,1},{1,0},{2,3},{3,2},{4,5},{5,4},{6,7},{7,6},{8,9},{9,8},{10,11... | collective-permute-start | bytes 122888 | tf_op jit(solution)/shard_map/ppermute | solution.py:678
  15.2 5.8 %collective-permute-start.4 = (bf16[160,128]{1,0:T(8,128)(2,1)S(1)}, bf16[160,128]{1,0:T(8,128)(2,1)S(1)}, u32[]{:S(2)}, u32[]{:S(2)}) collective-permute-start(bf16[160,128]{1,0:T(8,128)(2,1)S(1)} %get-tuple-element.38.refs_1_), channel_id=1, source_target_pairs={{0,7},{1,2},{2,1},{3,4},{4,3},{5,6},{6,5},{7,0},{8,15},{9,10},{10,... | collective-permute-start | bytes 122888 | tf_op jit(solution)/shard_map/ppermute | solution.py:679
  28.5 4.9 %collective-permute-start.7 = (f32[2,4]{1,0:T(2,128)S(1)}, f32[2,4]{1,0:T(2,128)S(1)}, u32[]{:S(2)}, u32[]{:S(2)}) collective-permute-start(f32[2,4]{1,0:T(2,128)S(1)} %get-tuple-element.61), channel_id=1, source_target_pairs={{0,4},{1,5},{2,6},{3,7},{4,0},{5,1},{6,2},{7,3},{8,12},{9,13},{10,... | collective-permute-start | bytes 104 | tf_op jit(solution)/shard_map/ppermute | solution.py:673
  33.5 3.6 %collective-permute-start.8 = (f32[2,4]{1,0:T(2,128)S(1)}, f32[2,4]{1,0:T(2,128)S(1)}, u32[]{:S(2)}, u32[]{:S(2)}) collective-permute-start(f32[2,4]{1,0:T(2,128)S(1)} %add.9), channel_id=1, source_target_pairs={{0,2},{1,3},{2,0},{3,1},{4,6},{5,7},{6,4},{7,5},{8,10},{9,11},{10,... | collective-permute-start | bytes 104 | tf_op jit(solution)/shard_map/ppermute | solution.py:673
  37.1 1.5 %collective-permute-start.9 = (f32[2,4]{1,0:T(2,128)S(1)}, f32[2,4]{1,0:T(2,128)S(1)}, u32[]{:S(2)}, u32[]{:S(2)}) collective-permute-start(f32[2,4]{1,0:T(2,128)S(1)} %add.10), channel_id=1, source_target_pairs={{0,1},{1,0},{2,3},{3,2},{4,5},{5,4},{6,7},{7,6},{8,9},{9,8},{10,11... | collective-permute-start | bytes 104 | tf_op jit(solution)/shard_map/ppermute | solution.py:673

commit v5 on v4

--- a/solution.py
+++ b/solution.py
@@ -316,14 +316,18 @@
     return left, right, turned
 
 
-def in_segments(sets, tiled, big, step):
+def spread_selection(tiled, big):
     blocks = big.shape[0] // (4 * SLOT)
-    width = blocks * SEG
-    lane_block = lax.broadcasted_iota(jnp.int32, tiled.shape, 1) % width // SEG
+    lane_block = lax.broadcasted_iota(jnp.int32, tiled.shape, 1) % (blocks * SEG) // SEG
     for j in range(blocks):
         big[j * 4 * SLOT : (j + 1) * 4 * SLOT, :] = jnp.where(
             lane_block == j, tiled[...].astype(F32), 0.0
         ).astype(BF16)
+
+
+def in_segments(sets, big, step):
+    blocks = big.shape[0] // (4 * SLOT)
+    width = blocks * SEG
     pieces = []
     for x in sets:
         for f in range(FIELDS):
@@ -331,7 +335,7 @@
             pieces.append(
                 jnp.concatenate([mine[j * step : (j + 1) * step] for j in range(blocks)], axis=1)
             )
-    y = mm(jnp.concatenate(pieces, axis=0), big[...])
+    y = mm(jnp.concatenate(pieces, axis=0), big)
 
     def part(i, f, which):
         start = (i * FIELDS + f) * step
@@ -344,7 +348,10 @@
     return lax.broadcasted_iota(jnp.int32, (step, width), 1) & (SEG - 1) < HALF
 
 
-def halo_forcing_kernel(fm, link, sa, sb, ra, rb, tiled, edge, y_ref, fe_ref, hot_ref, big):
+def halo_forcing_kernel(
+    cycle, fm, link, sa, sb, ra, rb, tiled, edge, forcing, v0, q0, q1, q2,
+    y_ref, fe_ref, hot_ref, bs, coef0, coef1, weighted, heavy, z_ref, big, fmc,
+):
     rows, width = link.shape[1], edge.shape[1]
     step = rows // (width // SEG)
     left, right, turned = gather_sources(sa, sb, ra, rb)
@@ -372,12 +379,14 @@
         fe_ref[f] = fe[f * rows : (f + 1) * rows]
     g = jnp.concatenate(turned, axis=1)
     by_left, by_right, by_tile = permuted(g)
-    part = in_segments((g, by_tile, permuted(by_tile)[2], by_left, by_right), tiled, big, step)
+    spread_selection(tiled, big)
+    part = in_segments((g, by_left, by_right), big[...], step)
+    linked = in_segments((by_tile, permuted(by_tile)[2]), big[:, 2 * width : 3 * width], step)
     is_left = left_lanes(step, width)
 
     def at(linked, f, which):
         if linked:
-            return jnp.where(is_left, part(3, f, which), part(4, f, which))
+            return jnp.where(is_left, part(1, f, which), part(2, f, which))
         return part(0, f, which)
 
     for i in range(2):
@@ -388,7 +397,7 @@
             b = (
                 C2 * shifted[0][f],
                 C1 * shifted[1][f] - minus,
-                (C0 + 1.0) * shifted[2][f] + CP * part(i + 1, f, 2),
+                (C0 + 1.0) * shifted[2][f] + CP * linked(i, f, 0),
                 C1 * shifted[3][f] + plus,
                 C2 * shifted[4][f],
                 shifted[1][f],
@@ -397,6 +406,58 @@
             )
             for d, value in enumerate(b):
                 y_ref[i * 8 + d, f] = value
+
+    scaled_matrix(fm, fmc)
+    total = cycle * width
+    start = lax.axis_index("blk") * width
+    lane = lax.broadcasted_iota(jnp.int32, (8, width), 1)
+    weight = {d: column_weight(lane + (start + d), total) for d in range(-2, 3)}
+
+    def dense(i, z):
+        rs = pl.ds(pl.multiple_of(i * 16, 16), 16)
+        for q_ref, coef in ((q0, coef0), (q1, coef1)):
+            q = [q_ref[f, rs, :].astype(F32) for f in range(FIELDS)]
+            u = CU * q[1]
+            for e in range(FIELDS):
+                coef[e, rs, :] = (u if e != 1 else u + u) + fmc[e, e]
+            for j, f in enumerate((0, 2, 3, 4)):
+                coef[FIELDS + j, rs, :] = CU * q[f] + fmc[f, 1]
+        both_q = [[q[f, rs, :].astype(F32) for f in range(FIELDS)] for q in (q0, q2)]
+        for half in range(2):
+            r8 = pl.ds(pl.multiple_of(i * 16 + half * 8, 8), 8)
+            mine, last = [[x[half * 8 : half * 8 + 8] for x in q] for q in both_q]
+            near, w = [], []
+            for f in range(FIELDS):
+                x, beside = forcing[f, r8, :], fe_ref[f, r8, :]
+                near.append(
+                    (
+                        *shift_edges(x, beside, lane, width),
+                        pltpu.roll(jnp.where(lane >= width - 2, beside, x), 2, 1),
+                        pltpu.roll(jnp.where(lane < 2, beside, x), width - 2, 1),
+                    )
+                )
+                w.append(x * weight[0])
+            minus = flux(fmc, last, [a[0] for a in near])
+            plus = flux(fmc, last, [a[1] for a in near])
+            for f in range(FIELDS):
+                m1, p1, m2, p2 = near[f]
+                bs[0, f, r8, :] = C2 * m2
+                bs[1, f, r8, :] = C1 * m1 - minus[f]
+                bs[2, f, r8, :] = C1 * p1 + plus[f]
+                bs[3, f, r8, :] = C2 * p2
+                weighted[f, r8, :] = w[f]
+                z = z + w[f] * forcing[f, r8, :]
+                x = CU * (mine[1] * w[f] + mine[f] * w[1])
+                for e in range(FIELDS):
+                    x = x + fmc[f, e] * w[e]
+                before = jnp.where(lane == 0, 0.0, pltpu.roll(x, 1, 1))
+                after = jnp.where(lane == width - 1, 0.0, pltpu.roll(x, width - 1, 1))
+                turned = v0[f, r8, :] + C1 * (m1 * weight[-1] + p1 * weight[1])
+                turned = turned + C2 * (m2 * weight[-2] + p2 * weight[2])
+                heavy[f, r8, :] = w[f] + turned + (before - after)
+        return z
+
+    z_ref[...] = lax.fori_loop(0, rows // 16, dense, jnp.zeros((8, width), F32), unroll=2)
 
 
 def halo_kernel(
@@ -416,7 +477,8 @@
     for f in range(FIELDS):
         qe_ref[f] = qe[f * rows : (f + 1) * rows]
     y = mm(hot[...], g).astype(BF16)
-    part = in_segments((g, y[:rows], y[2 * rows :]), tiled, big, step)
+    spread_selection(tiled, big)
+    part = in_segments((g, y[:rows], y[2 * rows :]), big[...], step)
     is_left = left_lanes(step, width)
     for i in range(2):
         if i:
@@ -533,9 +595,9 @@
 
 
 def first_steps_kernel(
-    cycle, fm, inv, forcing, fe, b0, v0, qe, k_ref, products, e1, q0, q1, q2,
-    mu2, coef0, sens_ref,
-    bs, coef1, mu1, dz, weighted, heavy, fmc,
+    cycle, fm, inv, forcing, fe, b0, qe, k_ref, products, e1, bs, coef1, weighted, heavy_in, z_ref,
+    mu2, sens_ref,
+    mu1, dz, heavy, fmc,
 ):
     rows, width = forcing.shape[1], forcing.shape[2]
     total = cycle * width
@@ -545,58 +607,24 @@
     lane = lax.broadcasted_iota(jnp.int32, (8, width), 1)
     start = lax.axis_index("blk") * width
     norm = 1.0 / math.sqrt(FIELDS * rows * total)
-    weight = {d: column_weight(lane + (start + d), total) for d in range(-2, 3)}
     beside = column_weight(jnp.where(lane < width // 2, lane + width, lane - width) + start, total)
 
-    def dense(i, z):
-        rs = pl.ds(pl.multiple_of(i * 16, 16), 16)
-        for n, (q_ref, coef) in enumerate(((q0, coef0), (q1, coef1))):
-            q = [q_ref[f, rs, :].astype(F32) for f in range(FIELDS)]
-            u = CU * q[1]
+    def finish(i, c):
+        r8 = pl.ds(pl.multiple_of(i * 8, 8), 8)
+        w = [fe[f, r8, :] * beside for f in range(FIELDS)]
+        q = [qe[f, r8, :] for f in range(FIELDS)]
+        for f in range(FIELDS):
+            x = CU * (q[1] * w[f] + q[f] * w[1])
             for e in range(FIELDS):
-                coef[e, rs, :] = (u if e != 1 else u + u) + fmc[e, e]
-            for j, f in enumerate((0, 2, 3, 4)):
-                coef[FIELDS + j, rs, :] = CU * q[f] + fmc[f, 1]
-        both_q = [[q[f, rs, :].astype(F32) for f in range(FIELDS)] for q in (q0, q2)]
-        for half in range(2):
-            r8 = pl.ds(pl.multiple_of(i * 16 + half * 8, 8), 8)
-            mine, last = [[x[half * 8 : half * 8 + 8] for x in q] for q in both_q]
-            near, w, we = [], [], []
-            for f in range(FIELDS):
-                x, edge = forcing[f, r8, :], fe[f, r8, :]
-                near.append(
-                    (
-                        *shift_edges(x, edge, lane, width),
-                        pltpu.roll(jnp.where(lane >= width - 2, edge, x), 2, 1),
-                        pltpu.roll(jnp.where(lane < 2, edge, x), width - 2, 1),
-                    )
-                )
-                w.append(x * weight[0])
-                we.append(edge * beside)
-            minus = flux(fmc, last, [a[0] for a in near])
-            plus = flux(fmc, last, [a[1] for a in near])
-            q_edge = [qe[f, r8, :] for f in range(FIELDS)]
-            for f in range(FIELDS):
-                m1, p1, m2, p2 = near[f]
-                bs[0, f, r8, :] = C2 * m2
-                bs[1, f, r8, :] = C1 * m1 - minus[f]
-                bs[2, f, r8, :] = C1 * p1 + plus[f]
-                bs[3, f, r8, :] = C2 * p2
-                weighted[f, r8, :] = w[f]
-                z = z + w[f] * forcing[f, r8, :]
-                x = CU * (mine[1] * w[f] + mine[f] * w[1])
-                xe = CU * (q_edge[1] * we[f] + q_edge[f] * we[1])
-                for e in range(FIELDS):
-                    x = x + fmc[f, e] * w[e]
-                    xe = xe + fmc[f, e] * we[e]
-                before, after = shift_edges(x, xe, lane, width)
-                turned = v0[f, r8, :] + C1 * (m1 * weight[-1] + p1 * weight[1])
-                turned = turned + C2 * (m2 * weight[-2] + p2 * weight[2])
-                heavy[f, r8, :] = w[f] + turned + (before - after)
-        return z
+                x = x + fmc[f, e] * w[e]
+            before = jnp.where(lane == 0, pltpu.roll(x, 1, 1), 0.0)
+            after = jnp.where(lane == width - 1, pltpu.roll(x, width - 1, 1), 0.0)
+            heavy[f, r8, :] = heavy_in[f, r8, :] + (before - after)
+        return c
 
     zero = jnp.zeros((8, width), F32)
-    z = lax.fori_loop(0, rows // 16, dense, zero)
+    lax.fori_loop(0, rows // 8, finish, 0, unroll=8)
+    z = z_ref[...]
     k = [k_ref[i] for i in range(5)]
 
     def first(j, acc):
@@ -754,19 +782,26 @@
     )
     q_sent = (q_a, q_b, *to_neighbours(q_a, q_b, cycle))
 
-    y, fe, hot = call(
-        halo_forcing_kernel,
-        (struct((16, FIELDS, step_rows, width)), field, struct((3 * rows, rows), BF16)),
+    coefficients = struct((2 * FIELDS - 1, rows, width))
+    y, fe, hot, bs, coef0, coef1, weighted, heavy, z = call(
+        functools.partial(halo_forcing_kernel, cycle),
+        (
+            struct((16, FIELDS, step_rows, width)), field, struct((3 * rows, rows), BF16),
+            struct((4, FIELDS, rows, width)), coefficients, coefficients, field, field,
+            struct((PAIRS, width)),
+        ),
         (fm_s,),
         (),
-        (link, *f_sent, forcing_tiled, edge),
-        [pltpu.VMEM((blocks * 4 * SLOT, forcing_tiled.shape[1]), BF16)],
+        (link, *f_sent, forcing_tiled, edge, forcing_v, v0, *chosen),
+        [
+            pltpu.VMEM((blocks * 4 * SLOT, forcing_tiled.shape[1]), BF16),
+            pltpu.SMEM((FIELDS, FIELDS), F32),
+        ],
         SMALL_LIMIT,
         10**8,
         "halo_forcing",
     )
     flat = rows * FIELDS * PAIRS
-    coefficients = (2 * FIELDS - 1, rows, width)
     edges = (step_rows * FIELDS * 8, width)
     halo_operands = (*q_sent, state_tiled, state_edge, kp, hot, y)
     halo_scratch = [
@@ -780,29 +815,24 @@
 
     def halo_and_first_steps(fm, inv, *refs):
         halo_in, refs = refs[: len(halo_operands)], refs[len(halo_operands) :]
-        forcing, fe, b0, v0, k_ref, products, q0, q1, q2 = refs[:9]
-        mu2, coef0, sens, e2, e1, qe, *work = refs[9 : 13 + len(halo_scratch)]
+        forcing, fe, b0, k_ref, products, *ready = refs[:10]
+        mu2, sens, e2, e1, qe, *work = refs[10 : 13 + len(halo_scratch)]
         halo_kernel(fm, *halo_in, e1, e2, qe, *work)
         first_steps_kernel(
-            cycle, fm, inv, forcing, fe, b0, v0, qe, k_ref, products, e1, q0, q1, q2,
-            mu2, coef0, sens, *refs[13 + len(halo_scratch) :],
+            cycle, fm, inv, forcing, fe, b0, qe, k_ref, products, e1, *ready,
+            mu2, sens, *refs[13 + len(halo_scratch) :],
         )
 
-    mu2, coef0, sens, e2 = call(
+    mu2, sens, e2 = call(
         halo_and_first_steps,
-        (
-            struct((flat, width)), struct(coefficients), struct((GRP_DEV, AMP)), struct(edges),
-        ),
+        (struct((flat, width)), struct((GRP_DEV, AMP)), struct(edges)),
         (fm_s, inv),
         (),
-        (*halo_operands, forcing_v, fe, b0, v0, k, products, *chosen),
+        (*halo_operands, forcing_v, fe, b0, k, products, bs, coef1, weighted, heavy, z),
         halo_scratch
         + [
-            pltpu.VMEM((4, FIELDS, rows, width), F32),
-            pltpu.VMEM(coefficients, F32),
             pltpu.VMEM((flat, width), F32),
             pltpu.VMEM((flat, 2 * width), F32),
-            pltpu.VMEM((FIELDS, rows, width), F32),
             pltpu.VMEM((FIELDS, rows, width), F32),
             pltpu.SMEM((FIELDS, FIELDS), F32),
         ],

time: 39.4 us -> 39 us (0.990)
  starting transfers between devices: 15.1 us -> 13.8 us
  waiting for transfers between devices: 4.14 us -> 4.9 us
    ppermute x3, starting transfers between devices: 2.49 us -> 1.22 us  [round_over(): lax.ppermute(x, axis, [(i, i ^ bit) for i in range(lax.axis_size(axis))])]
    ppermute x3, waiting for transfers between devices: 2.81 us -> 3.57 us  [round_over(): lax.ppermute(x, axis, [(i, i ^ bit) for i in range(lax.axis_size(axis))])]
  transfers between devices with their start and end apart: 10 -> 10, of which waited for: 3 -> 3; matrix products, arithmetic and copies ran while one was open for 0% -> 0% of each run, Pallas kernels for 28% -> 31%
where the time goes in v5:
time: 39 us; the launch traced here: 38.7 us
  Pallas kernels  18.6 us (48%)
  starting transfers between devices  13.8 us (35%)
  waiting for transfers between devices  4.9 us (13%)
  between operations  0.75 us (2%)
  other arithmetic  0.57 us (1%)
    pallas_call x5, Pallas kernels, call(): pl.pallas_call(kernel, out_shape=out_shape, in_specs=[SMEM] * len(smem) +...  18.6 us
    ppermute x2, starting transfers between devices, to_neighbours(): lax.ppermute(send_b, 'blk', [(i, (i + 1) % cycle if i % 2 else (i - 1) %...  7.41 us
    ppermute x3, starting transfers between devices, on_device(): lax.ppermute(slot, 'out', shift_pairs(n_out, k))  5.04 us
    ppermute x3, waiting for transfers between devices, round_over(): lax.ppermute(x, axis, [(i, i ^ bit) for i in range(lax.axis_size(axis))])  3.57 us
    ppermute x3, waiting for transfers between devices, on_device(): lax.ppermute(slot, 'out', shift_pairs(n_out, k))  1.32 us
    ppermute x3, starting transfers between devices, round_over(): lax.ppermute(x, axis, [(i, i ^ bit) for i in range(lax.axis_size(axis))])  1.22 us
  transfers between devices with their start and end apart: 10, of which 3 were waited for; matrix products, arithmetic and copies ran while one was open for 0% of the time, Pallas kernels for 31%

profile of v5, /device:TPU:0, one launch (start us, length us, event | category | flops | bytes accessed | tf_op | source)
XLA Modules:
  0.0 38.7 jit_solution(9117201579872907623)
XLA Ops:
  0.6 3.9 %collective-permute-start.2 = (bf16[5,128,128]{2,1,0:T(8,128)(2,1)}, bf16[5,128,128]{2,1,0:T(8,128)(2,1)S(1)}, u32[]{:S(2)}, u32[]{:S(2)}) collective-permute-start(bf16[5,128,128]{2,1,0:T(8,128)(2,1)} %bitcast.4), channel_id=1, source_target_pairs={{0,24},{8,0},{16,8},{24,16},{1,25},{9,1},{17,9},{25,17},{2,26},{10... | collective-permute-start | bytes 491528 | tf_op jit(solution)/shard_map/ppermute | solution.py:730
  4.6 0.5 %collective-permute-start.1 = (bf16[5,128,128]{2,1,0:T(8,128)(2,1)}, bf16[5,128,128]{2,1,0:T(8,128)(2,1)S(1)}, u32[]{:S(2)}, u32[]{:S(2)}) collective-permute-start(bf16[5,128,128]{2,1,0:T(8,128)(2,1)} %bitcast.5), channel_id=1, source_target_pairs={{0,16},{8,24},{16,0},{24,8},{1,17},{9,25},{17,1},{25,9},{2,18},{10... | collective-permute-start | bytes 491528 | tf_op jit(solution)/shard_map/ppermute | solution.py:730
  5.1 0.6 %collective-permute-start = (bf16[5,128,128]{2,1,0:T(8,128)(2,1)}, bf16[5,128,128]{2,1,0:T(8,128)(2,1)S(1)}, u32[]{:S(2)}, u32[]{:S(2)}) collective-permute-start(bf16[5,128,128]{2,1,0:T(8,128)(2,1)} %bitcast.6), channel_id=1, source_target_pairs={{0,8},{8,16},{16,24},{24,0},{1,9},{9,17},{17,25},{25,1},{2,10},{10... | collective-permute-start | bytes 491528 | tf_op jit(solution)/shard_map/ppermute | solution.py:730
  5.7 3.1 %prepare.1 = (f32[5,8,128]{2,1,0:T(8,128)S(1)}, f32[5,8,128]{2,1,0:T(8,128)S(1)}, f32[5,128,128]{2,1,0:T(8,128)S(1)}, f32[5,128,128]{2,1,0:T(8,128)S(1)}, bf16[1...) custom-call(s32[96]{0:T(128)} %blade_group.1, ...), custom_call_target="tpu_custom_call" | custom-call | flops 100000000 | bytes 1000000 | tf_op jit(solution)/shard_map/prepare/pallas_call | solution.py:736
  8.8 0.0 copy-start.2
  8.8 0.0 copy-start.1
  8.9 0.0 copy-start
  8.9 0.1 collective-permute-start.5
  8.9 3.7 %collective-permute-start.6 = (bf16[160,128]{1,0:T(8,128)(2,1)S(1)}, bf16[160,128]{1,0:T(8,128)(2,1)S(1)}, u32[]{:S(2)}, u32[]{:S(2)}) collective-permute-start(bf16[160,128]{1,0:T(8,128)(2,1)S(1)} %get-tuple-element.49.sb), channel_id=1, source_target_pairs={{0,7},{1,2},{2,1},{3,4},{4,3},{5,6},{6,5},{7,0},{8,15},{9,10},{10,... | collective-permute-start | bytes 122888 | tf_op jit(solution)/shard_map/ppermute | solution.py:707
  12.6 0.0 collective-permute-done.2.refs_4_
  12.6 1.3 %collective-permute-done.1.refs_3_ = bf16[5,128,128]{2,1,0:T(8,128)(2,1)S(1)} collective-permute-done((bf16[5,128,128]{2,1,0:T(8,128)(2,1)}, bf16[5,128,128]{2,1,0:T(8,128)(2,1)S(1)}, u32[]{:S(2)}, u32[]{:S(2)}) %collective-permute-start.1) | collective-permute-done | bytes 163872 | tf_op jit(solution)/shard_map/ppermute | solution.py:730
  14.0 0.0 collective-permute-done.refs_2_
  14.0 0.0 copy-done.2
  14.0 1.1 %strips.1 = (bf16[160,128]{1,0:T(8,128)(2,1)S(1)}, bf16[160,128]{1,0:T(8,128)(2,1)S(1)}, bf16[5,128,128]{2,1,0:T(8,128)(2,1)S(1)}, bf16[5,128,128]{2,1,0:T(8,128)(2,1)S(1)}, bf16[5,128,128]{2,1,0:T(8,128)(2,1)S(1)}) custom-call(s32[4]{0:T(128)} %copy-done.2, bf16[5,128,128]{2,1,0:T(8,128)(2,1)S(1)} %get-tuple-element.40.refs_1_, ...), custom_call_target="tpu_custom_call" | custom-call | flops 10000000 | bytes 1000000 | tf_op jit(solution)/shard_map/strips/pallas_call | solution.py:736
  15.1 0.1 collective-permute-start.3
  15.1 3.7 %collective-permute-start.4 = (bf16[160,128]{1,0:T(8,128)(2,1)S(1)}, bf16[160,128]{1,0:T(8,128)(2,1)S(1)}, u32[]{:S(2)}, u32[]{:S(2)}) collective-permute-start(bf16[160,128]{1,0:T(8,128)(2,1)S(1)} %get-tuple-element.43.refs_1_), channel_id=1, source_target_pairs={{0,7},{1,2},{2,1},{3,4},{4,3},{5,6},{6,5},{7,0},{8,15},{9,10},{10,... | collective-permute-start | bytes 122888 | tf_op jit(solution)/shard_map/ppermute | solution.py:707
  18.9 0.0 collective-permute-done.5.ra
  18.9 0.0 collective-permute-done.6.rb
  18.9 0.0 copy-done.1
  18.9 0.0 copy-done
  18.9 3.0 %halo_forcing.1 = (f32[16,5,16,128]{3,2,1,0:T(8,128)S(1)}, f32[5,128,128]{2,1,0:T(8,128)S(1)}, bf16[384,128]{1,0:T(8,128)(2,1)S(1)}, f32[4,5,128,128]{3,2,1,0:T(...) custom-call(f32[5,5]{1,0:T(8,128)} %copy-done, ...), custom_call_target="tpu_custom_call" | custom-call | flops 100000000 | bytes 1000000 | tf_op jit(solution)/shard_map/halo_forcing/pallas_call | solution.py:736
  21.8 0.0 collective-permute-done.3.refs_2_
  21.9 0.0 collective-permute-done.4.refs_3_
  21.9 6.7 %first_steps.1 = (f32[5120,128]{1,0:T(8,128)S(1)}, f32[2,4]{1,0:T(2,128)S(1)}, f32[640,128]{1,0:T(8,128)S(1)}) custom-call(f32[5,5]{1,0:T(8,128)} %copy-done, s32[128]{0:T(128)} %copy-done.1, bf16[160,128]{1,0:T(8,128)(2,1)S(1)} %get-tuple-element.42.refs_0_, bf16[160,128]{1,0:T(8,128)(2,1)S(1)} %get-tuple-element.43.refs_1_, ...), custom_call_target="tpu_custom_call" | custom-call | flops 1000000000 | bytes 1000000 | tf_op jit(solution)/shard_map/first_steps/pallas_call | solution.py:736
  28.6 0.0 collective-permute-start.7
  28.6 4.7 %last_step.1 = f32[40,128,128]{2,1,0:T(8,128)} custom-call(f32[5,5]{1,0:T(8,128)} %copy-done, s32[128]{0:T(128)} %copy-done.1, f32[5120,128]{1,0:T(8,128)S(1)} %get-tuple-element.68.mu2, f32[9,128,128]{2,1,0:T(8,128)S(1)} %get-tuple-element.69.coef0, f32[640,128]{1,0:T(8,128)S(1)} %get-tuple-element.70.e2, ...), custom_call_target="tpu_custom_call" | custom-call | flops 1000000000 | bytes 1000000 | tf_op jit(solution)/shard_map/last_step/pallas_call | solution.py:736
  33.3 0.0 collective-permute-done.7
  33.3 1.1 %collective-permute-start.8 = (f32[2,4]{1,0:T(2,128)S(1)}, f32[2,4]{1,0:T(2,128)S(1)}, u32[]{:S(2)}, u32[]{:S(2)}) collective-permute-start(f32[2,4]{1,0:T(2,128)S(1)} %add.9), channel_id=1, source_target_pairs={{0,2},{1,3},{2,0},{3,1},{4,6},{5,7},{6,4},{7,5},{8,10},{9,11},{10,... | collective-permute-start | bytes 104 | tf_op jit(solution)/shard_map/ppermute | solution.py:701
  34.4 2.5 %collective-permute-done.8 = f32[2,4]{1,0:T(2,128)S(1)} collective-permute-done((f32[2,4]{1,0:T(2,128)S(1)}, f32[2,4]{1,0:T(2,128)S(1)}, u32[]{:S(2)}, u32[]{:S(2)}) %collective-permute-start.8) | collective-permute-done | bytes 64 | tf_op jit(solution)/shard_map/ppermute | solution.py:701
  37.0 0.1 collective-permute-start.9
  37.1 1.0 %collective-permute-done.9 = f32[2,4]{1,0:T(2,128)S(1)} collective-permute-done((f32[2,4]{1,0:T(2,128)S(1)}, f32[2,4]{1,0:T(2,128)S(1)}, u32[]{:S(2)}, u32[]{:S(2)}) %collective-permute-start.9) | collective-permute-done | bytes 64 | tf_op jit(solution)/shard_map/ppermute | solution.py:701
  38.1 0.6 %add.11 = f32[2,4]{1,0:T(2,128)} add(f32[2,4]{1,0:T(2,128)S(1)} %add.10, f32[2,4]{1,0:T(2,128)S(1)} %collective-permute-done.9) | non-fusion elementwise | flops 8 | bytes 96 | tf_op jit(solution)/shard_map/add | solution.py:701
  (2 shorter events, 0.0 us)
Async XLA Ops:
  0.6 12.0 %collective-permute-start.2 = (bf16[5,128,128]{2,1,0:T(8,128)(2,1)}, bf16[5,128,128]{2,1,0:T(8,128)(2,1)S(1)}, u32[]{:S(2)}, u32[]{:S(2)}) collective-permute-start(bf16[5,128,128]{2,1,0:T(8,128)(2,1)} %bitcast.4), channel_id=1, source_target_pairs={{0,24},{8,0},{16,8},{24,16},{1,25},{9,1},{17,9},{25,17},{2,26},{10... | collective-permute-start | bytes 491528 | tf_op jit(solution)/shard_map/ppermute | solution.py:730
  4.6 9.4 %collective-permute-start.1 = (bf16[5,128,128]{2,1,0:T(8,128)(2,1)}, bf16[5,128,128]{2,1,0:T(8,128)(2,1)S(1)}, u32[]{:S(2)}, u32[]{:S(2)}) collective-permute-start(bf16[5,128,128]{2,1,0:T(8,128)(2,1)} %bitcast.5), channel_id=1, source_target_pairs={{0,16},{8,24},{16,0},{24,8},{1,17},{9,25},{17,1},{25,9},{2,18},{10... | collective-permute-start | bytes 491528 | tf_op jit(solution)/shard_map/ppermute | solution.py:730
  5.1 8.9 %collective-permute-start = (bf16[5,128,128]{2,1,0:T(8,128)(2,1)}, bf16[5,128,128]{2,1,0:T(8,128)(2,1)S(1)}, u32[]{:S(2)}, u32[]{:S(2)}) collective-permute-start(bf16[5,128,128]{2,1,0:T(8,128)(2,1)} %bitcast.6), channel_id=1, source_target_pairs={{0,8},{8,16},{16,24},{24,0},{1,9},{9,17},{17,25},{25,1},{2,10},{10... | collective-permute-start | bytes 491528 | tf_op jit(solution)/shard_map/ppermute | solution.py:730
  8.8 5.1 %copy-start.2 = (s32[4]{0:T(128)}, s32[4]{0:T(128)S(1)}, u32[]{:S(2)}) copy-start(s32[4]{0:T(128)S(1)} %get-tuple-element.39.refs_0_) | copy-start | bytes 52
  8.8 10.0 %copy-start.1 = (s32[128]{0:T(128)}, s32[128]{0:T(128)S(1)}, u32[]{:S(2)}) copy-start(s32[128]{0:T(128)S(1)} %get-tuple-element.38.inv) | copy-start | bytes 1540
  8.9 10.0 %copy-start = (f32[5,5]{1,0:T(8,128)}, f32[5,5]{1,0:T(8,128)S(1)}, u32[]{:S(2)}) copy-start(f32[5,5]{1,0:T(8,128)S(1)} %get-tuple-element.37.fm) | copy-start | bytes 304
  8.9 10.0 %collective-permute-start.5 = (bf16[160,128]{1,0:T(8,128)(2,1)S(1)}, bf16[160,128]{1,0:T(8,128)(2,1)S(1)}, u32[]{:S(2)}, u32[]{:S(2)}) collective-permute-start(bf16[160,128]{1,0:T(8,128)(2,1)S(1)} %get-tuple-element.48.sa), channel_id=1, source_target_pairs={{0,1},{1,0},{2,3},{3,2},{4,5},{5,4},{6,7},{7,6},{8,9},{9,8},{10,11... | collective-permute-start | bytes 122888 | tf_op jit(solution)/shard_map/ppermute | solution.py:706
  8.9 9.9 %collective-permute-start.6 = (bf16[160,128]{1,0:T(8,128)(2,1)S(1)}, bf16[160,128]{1,0:T(8,128)(2,1)S(1)}, u32[]{:S(2)}, u32[]{:S(2)}) collective-permute-start(bf16[160,128]{1,0:T(8,128)(2,1)S(1)} %get-tuple-element.49.sb), channel_id=1, source_target_pairs={{0,7},{1,2},{2,1},{3,4},{4,3},{5,6},{6,5},{7,0},{8,15},{9,10},{10,... | collective-permute-start | bytes 122888 | tf_op jit(solution)/shard_map/ppermute | solution.py:707
  15.1 6.8 %collective-permute-start.3 = (bf16[160,128]{1,0:T(8,128)(2,1)S(1)}, bf16[160,128]{1,0:T(8,128)(2,1)S(1)}, u32[]{:S(2)}, u32[]{:S(2)}) collective-permute-start(bf16[160,128]{1,0:T(8,128)(2,1)S(1)} %get-tuple-element.42.refs_0_), channel_id=1, source_target_pairs={{0,1},{1,0},{2,3},{3,2},{4,5},{5,4},{6,7},{7,6},{8,9},{9,8},{10,11... | collective-permute-start | bytes 122888 | tf_op jit(solution)/shard_map/ppermute | solution.py:706
  15.1 6.7 %collective-permute-start.4 = (bf16[160,128]{1,0:T(8,128)(2,1)S(1)}, bf16[160,128]{1,0:T(8,128)(2,1)S(1)}, u32[]{:S(2)}, u32[]{:S(2)}) collective-permute-start(bf16[160,128]{1,0:T(8,128)(2,1)S(1)} %get-tuple-element.43.refs_1_), channel_id=1, source_target_pairs={{0,7},{1,2},{2,1},{3,4},{4,3},{5,6},{6,5},{7,0},{8,15},{9,10},{10,... | collective-permute-start | bytes 122888 | tf_op jit(solution)/shard_map/ppermute | solution.py:707
  28.6 4.8 %collective-permute-start.7 = (f32[2,4]{1,0:T(2,128)S(1)}, f32[2,4]{1,0:T(2,128)S(1)}, u32[]{:S(2)}, u32[]{:S(2)}) collective-permute-start(f32[2,4]{1,0:T(2,128)S(1)} %get-tuple-element.71), channel_id=1, source_target_pairs={{0,4},{1,5},{2,6},{3,7},{4,0},{5,1},{6,2},{7,3},{8,12},{9,13},{10,... | collective-permute-start | bytes 104 | tf_op jit(solution)/shard_map/ppermute | solution.py:701
  33.3 3.7 %collective-permute-start.8 = (f32[2,4]{1,0:T(2,128)S(1)}, f32[2,4]{1,0:T(2,128)S(1)}, u32[]{:S(2)}, u32[]{:S(2)}) collective-permute-start(f32[2,4]{1,0:T(2,128)S(1)} %add.9), channel_id=1, source_target_pairs={{0,2},{1,3},{2,0},{3,1},{4,6},{5,7},{6,4},{7,5},{8,10},{9,11},{10,... | collective-permute-start | bytes 104 | tf_op jit(solution)/shard_map/ppermute | solution.py:701
  37.0 1.1 %collective-permute-start.9 = (f32[2,4]{1,0:T(2,128)S(1)}, f32[2,4]{1,0:T(2,128)S(1)}, u32[]{:S(2)}, u32[]{:S(2)}) collective-permute-start(f32[2,4]{1,0:T(2,128)S(1)} %add.10), channel_id=1, source_target_pairs={{0,1},{1,0},{2,3},{3,2},{4,5},{5,4},{6,7},{7,6},{8,9},{9,8},{10,11... | collective-permute-start | bytes 104 | tf_op jit(solution)/shard_map/ppermute | solution.py:701

commit v6 on v5

--- a/solution.py
+++ b/solution.py
@@ -36,7 +36,6 @@
 LINK_ROW = PARTS * FW
 SEG = 16
 HALF = SEG // 2
-HALO_LANES = (2, 3, 5, 12, 13, 14)
 VMEM_LIMIT = 40 * 2**20
 SMALL_LIMIT = 16 * 2**20
 
@@ -279,7 +278,7 @@
 
 def stencil_selects(width):
     blocks = width // SEG
-    out = np.zeros((blocks, 2, width, 2 * width), np.float32)
+    out = np.zeros((blocks, 3, width, 2 * width), np.float32)
 
     def spread(column):
         near = ((1, 1.0), (-1, -1.0))
@@ -289,14 +288,13 @@
 
     for column in range(width):
         for lane, w in spread(column):
-            out[:, :, column, lane] = w
+            out[:, :2, column, lane] = w
     for j in range(blocks):
         for p, column in ((2, -2), (3, -1), (HALF + QW, width), (HALF + QW + 1, width + 1)):
             for held in (p, p + 2) if column in (-1, width) else (p,):
-                out[j, 1, j * SEG + held] = 0.0
                 for to, w in spread(column):
-                    out[j, 1, j * SEG + held, to] = w
-    return out.reshape(blocks, 2 * width, 2 * width).astype(jnp.bfloat16)
+                    out[j, 2, j * SEG + held, to] = w
+    return out.reshape(blocks, 3 * width, 2 * width).astype(jnp.bfloat16)
 
 
 def high(x):
@@ -560,17 +558,14 @@
 
 
 def stencil_products(dz, source, edges, products):
-    width = source.shape[1]
     count = edges.shape[0]
-    lane = lax.broadcasted_iota(jnp.int32, (count, width), 1)
-    p = lane & (SEG - 1)
-    halo = functools.reduce(jnp.logical_or, [p == held for held in HALO_LANES])
+    outside = edges[...].astype(BF16)
     for j in range(products.shape[0]):
         x = source[j * count : (j + 1) * count, :]
         top = x.astype(BF16)
-        rest = jnp.where(halo & (lane // SEG == j), edges[...], x - top.astype(F32))
+        rest = (x - top.astype(F32)).astype(BF16)
         dz[j * count : (j + 1) * count, :] = mm(
-            jnp.concatenate([top, rest.astype(BF16)], axis=1), products[j]
+            jnp.concatenate([top, rest, outside], axis=1), products[j]
         )
 
 

time: 39 us -> 40.3 us (1.033)
  Pallas kernels: 18.6 us -> 20 us
    pallas_call x5, Pallas kernels: 18.6 us -> 20 us  [call(): pl.pallas_call(kernel, out_shape=out_shape, in_specs=[SMEM] * len(smem) +...]
  transfers between devices with their start and end apart: 10 -> 10, of which waited for: 3 -> 3; matrix products, arithmetic and copies ran while one was open for 0% -> 0% of each run, Pallas kernels for 31% -> 32%
where the time goes in v6:
time: 40.3 us; the launch traced here: 40 us
  Pallas kernels  20 us (50%)
  starting transfers between devices  13.8 us (34%)
  waiting for transfers between devices  4.79 us (12%)
  between operations  0.75 us (2%)
  other arithmetic  0.57 us (1%)
    pallas_call x5, Pallas kernels, call(): pl.pallas_call(kernel, out_shape=out_shape, in_specs=[SMEM] * len(smem) +...  20 us
    ppermute x2, starting transfers between devices, to_neighbours(): lax.ppermute(send_b, 'blk', [(i, (i + 1) % cycle if i % 2 else (i - 1) %...  7.42 us
    ppermute x3, starting transfers between devices, on_device(): lax.ppermute(slot, 'out', shift_pairs(n_out, k))  5.04 us
    ppermute x3, waiting for transfers between devices, round_over(): lax.ppermute(x, axis, [(i, i ^ bit) for i in range(lax.axis_size(axis))])  3.6 us
    ppermute x3, starting transfers between devices, round_over(): lax.ppermute(x, axis, [(i, i ^ bit) for i in range(lax.axis_size(axis))])  1.19 us
    ppermute x3, waiting for transfers between devices, on_device(): lax.ppermute(slot, 'out', shift_pairs(n_out, k))  1.18 us
  transfers between devices with their start and end apart: 10, of which 3 were waited for; matrix products, arithmetic and copies ran while one was open for 0% of the time, Pallas kernels for 32%

profile of v6, /device:TPU:0, one launch (start us, length us, event | category | flops | bytes accessed | tf_op | source)
XLA Modules:
  0.0 40.0 jit_solution(8523920573618847273)
XLA Ops:
  0.6 3.9 %collective-permute-start.2 = (bf16[5,128,128]{2,1,0:T(8,128)(2,1)}, bf16[5,128,128]{2,1,0:T(8,128)(2,1)S(1)}, u32[]{:S(2)}, u32[]{:S(2)}) collective-permute-start(bf16[5,128,128]{2,1,0:T(8,128)(2,1)} %bitcast.4), channel_id=1, source_target_pairs={{0,24},{8,0},{16,8},{24,16},{1,25},{9,1},{17,9},{25,17},{2,26},{10... | collective-permute-start | bytes 491528 | tf_op jit(solution)/shard_map/ppermute | solution.py:725
  4.6 0.5 %collective-permute-start.1 = (bf16[5,128,128]{2,1,0:T(8,128)(2,1)}, bf16[5,128,128]{2,1,0:T(8,128)(2,1)S(1)}, u32[]{:S(2)}, u32[]{:S(2)}) collective-permute-start(bf16[5,128,128]{2,1,0:T(8,128)(2,1)} %bitcast.5), channel_id=1, source_target_pairs={{0,16},{8,24},{16,0},{24,8},{1,17},{9,25},{17,1},{25,9},{2,18},{10... | collective-permute-start | bytes 491528 | tf_op jit(solution)/shard_map/ppermute | solution.py:725
  5.1 0.6 %collective-permute-start = (bf16[5,128,128]{2,1,0:T(8,128)(2,1)}, bf16[5,128,128]{2,1,0:T(8,128)(2,1)S(1)}, u32[]{:S(2)}, u32[]{:S(2)}) collective-permute-start(bf16[5,128,128]{2,1,0:T(8,128)(2,1)} %bitcast.6), channel_id=1, source_target_pairs={{0,8},{8,16},{16,24},{24,0},{1,9},{9,17},{17,25},{25,1},{2,10},{10... | collective-permute-start | bytes 491528 | tf_op jit(solution)/shard_map/ppermute | solution.py:725
  5.7 3.3 %prepare.1 = (f32[5,8,128]{2,1,0:T(8,128)S(1)}, f32[5,8,128]{2,1,0:T(8,128)S(1)}, f32[5,128,128]{2,1,0:T(8,128)S(1)}, f32[5,128,128]{2,1,0:T(8,128)S(1)}, bf16[1...) custom-call(s32[96]{0:T(128)} %blade_group.1, ...), custom_call_target="tpu_custom_call" | custom-call | flops 100000000 | bytes 1000000 | tf_op jit(solution)/shard_map/prepare/pallas_call | solution.py:731
  9.0 0.0 copy-start.2
  9.0 0.0 copy-start.1
  9.0 0.0 copy-start
  9.0 0.1 collective-permute-start.5
  9.1 3.7 %collective-permute-start.6 = (bf16[160,128]{1,0:T(8,128)(2,1)S(1)}, bf16[160,128]{1,0:T(8,128)(2,1)S(1)}, u32[]{:S(2)}, u32[]{:S(2)}) collective-permute-start(bf16[160,128]{1,0:T(8,128)(2,1)S(1)} %get-tuple-element.49.sb), channel_id=1, source_target_pairs={{0,7},{1,2},{2,1},{3,4},{4,3},{5,6},{6,5},{7,0},{8,15},{9,10},{10,... | collective-permute-start | bytes 122888 | tf_op jit(solution)/shard_map/ppermute | solution.py:702
  12.8 0.0 collective-permute-done.2.refs_4_
  12.8 1.2 %collective-permute-done.1.refs_3_ = bf16[5,128,128]{2,1,0:T(8,128)(2,1)S(1)} collective-permute-done((bf16[5,128,128]{2,1,0:T(8,128)(2,1)}, bf16[5,128,128]{2,1,0:T(8,128)(2,1)S(1)}, u32[]{:S(2)}, u32[]{:S(2)}) %collective-permute-start.1) | collective-permute-done | bytes 163872 | tf_op jit(solution)/shard_map/ppermute | solution.py:725
  14.0 0.0 collective-permute-done.refs_2_
  14.0 0.0 copy-done.2
  14.0 1.1 %strips.1 = (bf16[160,128]{1,0:T(8,128)(2,1)S(1)}, bf16[160,128]{1,0:T(8,128)(2,1)S(1)}, bf16[5,128,128]{2,1,0:T(8,128)(2,1)S(1)}, bf16[5,128,128]{2,1,0:T(8,128)(2,1)S(1)}, bf16[5,128,128]{2,1,0:T(8,128)(2,1)S(1)}) custom-call(s32[4]{0:T(128)} %copy-done.2, bf16[5,128,128]{2,1,0:T(8,128)(2,1)S(1)} %get-tuple-element.40.refs_1_, ...), custom_call_target="tpu_custom_call" | custom-call | flops 10000000 | bytes 1000000 | tf_op jit(solution)/shard_map/strips/pallas_call | solution.py:731
  15.1 0.1 collective-permute-start.3
  15.1 3.7 %collective-permute-start.4 = (bf16[160,128]{1,0:T(8,128)(2,1)S(1)}, bf16[160,128]{1,0:T(8,128)(2,1)S(1)}, u32[]{:S(2)}, u32[]{:S(2)}) collective-permute-start(bf16[160,128]{1,0:T(8,128)(2,1)S(1)} %get-tuple-element.43.refs_1_), channel_id=1, source_target_pairs={{0,7},{1,2},{2,1},{3,4},{4,3},{5,6},{6,5},{7,0},{8,15},{9,10},{10,... | collective-permute-start | bytes 122888 | tf_op jit(solution)/shard_map/ppermute | solution.py:702
  18.9 0.0 collective-permute-done.5.ra
  18.9 0.0 collective-permute-done.6.rb
  18.9 0.0 copy-done.1
  18.9 0.0 copy-done
  18.9 3.0 %halo_forcing.1 = (f32[16,5,16,128]{3,2,1,0:T(8,128)S(1)}, f32[5,128,128]{2,1,0:T(8,128)S(1)}, bf16[384,128]{1,0:T(8,128)(2,1)S(1)}, f32[4,5,128,128]{3,2,1,0:T(...) custom-call(f32[5,5]{1,0:T(8,128)} %copy-done, ...), custom_call_target="tpu_custom_call" | custom-call | flops 100000000 | bytes 1000000 | tf_op jit(solution)/shard_map/halo_forcing/pallas_call | solution.py:731
  21.8 0.0 collective-permute-done.3.refs_2_
  21.9 0.0 collective-permute-done.4.refs_3_
  21.9 7.3 %first_steps.1 = (f32[5120,128]{1,0:T(8,128)S(1)}, f32[2,4]{1,0:T(2,128)S(1)}, f32[640,128]{1,0:T(8,128)S(1)}) custom-call(f32[5,5]{1,0:T(8,128)} %copy-done, s32[128]{0:T(128)} %copy-done.1, bf16[160,128]{1,0:T(8,128)(2,1)S(1)} %get-tuple-element.42.refs_0_, bf16[160,128]{1,0:T(8,128)(2,1)S(1)} %get-tuple-element.43.refs_1_, ...), custom_call_target="tpu_custom_call" | custom-call | flops 1000000000 | bytes 1000000 | tf_op jit(solution)/shard_map/first_steps/pallas_call | solution.py:731
  29.1 0.0 collective-permute-start.7
  29.1 5.4 %last_step.1 = f32[40,128,128]{2,1,0:T(8,128)} custom-call(f32[5,5]{1,0:T(8,128)} %copy-done, s32[128]{0:T(128)} %copy-done.1, f32[5120,128]{1,0:T(8,128)S(1)} %get-tuple-element.68.mu2, f32[9,128,128]{2,1,0:T(8,128)S(1)} %get-tuple-element.69.coef0, f32[640,128]{1,0:T(8,128)S(1)} %get-tuple-element.70.e2, ...), custom_call_target="tpu_custom_call" | custom-call | flops 1000000000 | bytes 1000000 | tf_op jit(solution)/shard_map/last_step/pallas_call | solution.py:731
  34.6 0.0 collective-permute-done.7
  34.6 1.1 %collective-permute-start.8 = (f32[2,4]{1,0:T(2,128)S(1)}, f32[2,4]{1,0:T(2,128)S(1)}, u32[]{:S(2)}, u32[]{:S(2)}) collective-permute-start(f32[2,4]{1,0:T(2,128)S(1)} %add.9), channel_id=1, source_target_pairs={{0,2},{1,3},{2,0},{3,1},{4,6},{5,7},{6,4},{7,5},{8,10},{9,11},{10,... | collective-permute-start | bytes 104 | tf_op jit(solution)/shard_map/ppermute | solution.py:696
  35.7 2.6 %collective-permute-done.8 = f32[2,4]{1,0:T(2,128)S(1)} collective-permute-done((f32[2,4]{1,0:T(2,128)S(1)}, f32[2,4]{1,0:T(2,128)S(1)}, u32[]{:S(2)}, u32[]{:S(2)}) %collective-permute-start.8) | collective-permute-done | bytes 64 | tf_op jit(solution)/shard_map/ppermute | solution.py:696
  38.2 0.1 collective-permute-start.9
  38.4 1.0 %collective-permute-done.9 = f32[2,4]{1,0:T(2,128)S(1)} collective-permute-done((f32[2,4]{1,0:T(2,128)S(1)}, f32[2,4]{1,0:T(2,128)S(1)}, u32[]{:S(2)}, u32[]{:S(2)}) %collective-permute-start.9) | collective-permute-done | bytes 64 | tf_op jit(solution)/shard_map/ppermute | solution.py:696
  39.4 0.6 %add.11 = f32[2,4]{1,0:T(2,128)} add(f32[2,4]{1,0:T(2,128)S(1)} %add.10, f32[2,4]{1,0:T(2,128)S(1)} %collective-permute-done.9) | non-fusion elementwise | flops 8 | bytes 96 | tf_op jit(solution)/shard_map/add | solution.py:696
  (2 shorter events, 0.0 us)
Async XLA Ops:
  0.6 12.2 %collective-permute-start.2 = (bf16[5,128,128]{2,1,0:T(8,128)(2,1)}, bf16[5,128,128]{2,1,0:T(8,128)(2,1)S(1)}, u32[]{:S(2)}, u32[]{:S(2)}) collective-permute-start(bf16[5,128,128]{2,1,0:T(8,128)(2,1)} %bitcast.4), channel_id=1, source_target_pairs={{0,24},{8,0},{16,8},{24,16},{1,25},{9,1},{17,9},{25,17},{2,26},{10... | collective-permute-start | bytes 491528 | tf_op jit(solution)/shard_map/ppermute | solution.py:725
  4.6 9.4 %collective-permute-start.1 = (bf16[5,128,128]{2,1,0:T(8,128)(2,1)}, bf16[5,128,128]{2,1,0:T(8,128)(2,1)S(1)}, u32[]{:S(2)}, u32[]{:S(2)}) collective-permute-start(bf16[5,128,128]{2,1,0:T(8,128)(2,1)} %bitcast.5), channel_id=1, source_target_pairs={{0,16},{8,24},{16,0},{24,8},{1,17},{9,25},{17,1},{25,9},{2,18},{10... | collective-permute-start | bytes 491528 | tf_op jit(solution)/shard_map/ppermute | solution.py:725
  5.1 8.9 %collective-permute-start = (bf16[5,128,128]{2,1,0:T(8,128)(2,1)}, bf16[5,128,128]{2,1,0:T(8,128)(2,1)S(1)}, u32[]{:S(2)}, u32[]{:S(2)}) collective-permute-start(bf16[5,128,128]{2,1,0:T(8,128)(2,1)} %bitcast.6), channel_id=1, source_target_pairs={{0,8},{8,16},{16,24},{24,0},{1,9},{9,17},{17,25},{25,1},{2,10},{10... | collective-permute-start | bytes 491528 | tf_op jit(solution)/shard_map/ppermute | solution.py:725
  9.0 5.0 %copy-start.2 = (s32[4]{0:T(128)}, s32[4]{0:T(128)S(1)}, u32[]{:S(2)}) copy-start(s32[4]{0:T(128)S(1)} %get-tuple-element.39.refs_0_) | copy-start | bytes 52
  9.0 9.9 %copy-start.1 = (s32[128]{0:T(128)}, s32[128]{0:T(128)S(1)}, u32[]{:S(2)}) copy-start(s32[128]{0:T(128)S(1)} %get-tuple-element.38.inv) | copy-start | bytes 1540
  9.0 9.9 %copy-start = (f32[5,5]{1,0:T(8,128)}, f32[5,5]{1,0:T(8,128)S(1)}, u32[]{:S(2)}) copy-start(f32[5,5]{1,0:T(8,128)S(1)} %get-tuple-element.37.fm) | copy-start | bytes 304
  9.0 9.9 %collective-permute-start.5 = (bf16[160,128]{1,0:T(8,128)(2,1)S(1)}, bf16[160,128]{1,0:T(8,128)(2,1)S(1)}, u32[]{:S(2)}, u32[]{:S(2)}) collective-permute-start(bf16[160,128]{1,0:T(8,128)(2,1)S(1)} %get-tuple-element.48.sa), channel_id=1, source_target_pairs={{0,1},{1,0},{2,3},{3,2},{4,5},{5,4},{6,7},{7,6},{8,9},{9,8},{10,11... | collective-permute-start | bytes 122888 | tf_op jit(solution)/shard_map/ppermute | solution.py:701
  9.1 9.8 %collective-permute-start.6 = (bf16[160,128]{1,0:T(8,128)(2,1)S(1)}, bf16[160,128]{1,0:T(8,128)(2,1)S(1)}, u32[]{:S(2)}, u32[]{:S(2)}) collective-permute-start(bf16[160,128]{1,0:T(8,128)(2,1)S(1)} %get-tuple-element.49.sb), channel_id=1, source_target_pairs={{0,7},{1,2},{2,1},{3,4},{4,3},{5,6},{6,5},{7,0},{8,15},{9,10},{10,... | collective-permute-start | bytes 122888 | tf_op jit(solution)/shard_map/ppermute | solution.py:702
  15.1 6.8 %collective-permute-start.3 = (bf16[160,128]{1,0:T(8,128)(2,1)S(1)}, bf16[160,128]{1,0:T(8,128)(2,1)S(1)}, u32[]{:S(2)}, u32[]{:S(2)}) collective-permute-start(bf16[160,128]{1,0:T(8,128)(2,1)S(1)} %get-tuple-element.42.refs_0_), channel_id=1, source_target_pairs={{0,1},{1,0},{2,3},{3,2},{4,5},{5,4},{6,7},{7,6},{8,9},{9,8},{10,11... | collective-permute-start | bytes 122888 | tf_op jit(solution)/shard_map/ppermute | solution.py:701
  15.1 6.7 %collective-permute-start.4 = (bf16[160,128]{1,0:T(8,128)(2,1)S(1)}, bf16[160,128]{1,0:T(8,128)(2,1)S(1)}, u32[]{:S(2)}, u32[]{:S(2)}) collective-permute-start(bf16[160,128]{1,0:T(8,128)(2,1)S(1)} %get-tuple-element.43.refs_1_), channel_id=1, source_target_pairs={{0,7},{1,2},{2,1},{3,4},{4,3},{5,6},{6,5},{7,0},{8,15},{9,10},{10,... | collective-permute-start | bytes 122888 | tf_op jit(solution)/shard_map/ppermute | solution.py:702
  29.1 5.4 %collective-permute-start.7 = (f32[2,4]{1,0:T(2,128)S(1)}, f32[2,4]{1,0:T(2,128)S(1)}, u32[]{:S(2)}, u32[]{:S(2)}) collective-permute-start(f32[2,4]{1,0:T(2,128)S(1)} %get-tuple-element.71), channel_id=1, source_target_pairs={{0,4},{1,5},{2,6},{3,7},{4,0},{5,1},{6,2},{7,3},{8,12},{9,13},{10,... | collective-permute-start | bytes 104 | tf_op jit(solution)/shard_map/ppermute | solution.py:696
  34.6 3.6 %collective-permute-start.8 = (f32[2,4]{1,0:T(2,128)S(1)}, f32[2,4]{1,0:T(2,128)S(1)}, u32[]{:S(2)}, u32[]{:S(2)}) collective-permute-start(f32[2,4]{1,0:T(2,128)S(1)} %add.9), channel_id=1, source_target_pairs={{0,2},{1,3},{2,0},{3,1},{4,6},{5,7},{6,4},{7,5},{8,10},{9,11},{10,... | collective-permute-start | bytes 104 | tf_op jit(solution)/shard_map/ppermute | solution.py:696
  38.2 1.1 %collective-permute-start.9 = (f32[2,4]{1,0:T(2,128)S(1)}, f32[2,4]{1,0:T(2,128)S(1)}, u32[]{:S(2)}, u32[]{:S(2)}) collective-permute-start(f32[2,4]{1,0:T(2,128)S(1)} %add.10), channel_id=1, source_target_pairs={{0,1},{1,0},{2,3},{3,2},{4,5},{5,4},{6,7},{7,6},{8,9},{9,8},{10,11... | collective-permute-start | bytes 104 | tf_op jit(solution)/shard_map/ppermute | solution.py:696

commit v7 on v6

--- a/solution.py
+++ b/solution.py
@@ -125,8 +125,11 @@
             def _():
                 target[...] = slot[...]
 
+    beside = [jnp.concatenate([q[f] for q in chosen], axis=1) for f in range(FIELDS)]
+    rows = beside[0].shape[0]
+    both = mm(sel[...], jnp.concatenate(beside, axis=0), NT)
     for f in range(FIELDS):
-        give(send_a, send_b, f, mm(sel[...], jnp.concatenate([q[f] for q in chosen], axis=1), NT))
+        give(send_a, send_b, f, both[:, f * rows : (f + 1) * rows])
 
 
 def column_factor(columns, pair, start, total, group_base, blade_group):

time: 40.3 us -> 40.2 us (level)
  no operation moved by 1% of the time
where the time goes in v7:
time: 40.2 us; the launch traced here: 39.9 us
  Pallas kernels  20 us (50%)
  starting transfers between devices  13.8 us (34%)
  waiting for transfers between devices  4.79 us (12%)
  between operations  0.76 us (2%)
  other arithmetic  0.57 us (1%)
    pallas_call x5, Pallas kernels, call(): pl.pallas_call(kernel, out_shape=out_shape, in_specs=[SMEM] * len(smem) +...  20 us
    ppermute x2, starting transfers between devices, to_neighbours(): lax.ppermute(send_b, 'blk', [(i, (i + 1) % cycle if i % 2 else (i - 1) %...  7.41 us
    ppermute x3, starting transfers between devices, on_device(): lax.ppermute(slot, 'out', shift_pairs(n_out, k))  5.04 us
    ppermute x3, waiting for transfers between devices, round_over(): lax.ppermute(x, axis, [(i, i ^ bit) for i in range(lax.axis_size(axis))])  3.6 us
    ppermute x3, starting transfers between devices, round_over(): lax.ppermute(x, axis, [(i, i ^ bit) for i in range(lax.axis_size(axis))])  1.19 us
    ppermute x3, waiting for transfers between devices, on_device(): lax.ppermute(slot, 'out', shift_pairs(n_out, k))  1.18 us
  transfers between devices with their start and end apart: 10, of which 3 were waited for; matrix products, arithmetic and copies ran while one was open for 0% of the time, Pallas kernels for 32%

profile of v7, /device:TPU:0, one launch (start us, length us, event | category | flops | bytes accessed | tf_op | source)
XLA Modules:
  0.0 39.9 jit_solution(3731294077990545530)
XLA Ops:
  0.6 3.9 %collective-permute-start.2 = (bf16[5,128,128]{2,1,0:T(8,128)(2,1)}, bf16[5,128,128]{2,1,0:T(8,128)(2,1)S(1)}, u32[]{:S(2)}, u32[]{:S(2)}) collective-permute-start(bf16[5,128,128]{2,1,0:T(8,128)(2,1)} %bitcast.4), channel_id=1, source_target_pairs={{0,24},{8,0},{16,8},{24,16},{1,25},{9,1},{17,9},{25,17},{2,26},{10... | collective-permute-start | bytes 491528 | tf_op jit(solution)/shard_map/ppermute | solution.py:728
  4.6 0.5 %collective-permute-start.1 = (bf16[5,128,128]{2,1,0:T(8,128)(2,1)}, bf16[5,128,128]{2,1,0:T(8,128)(2,1)S(1)}, u32[]{:S(2)}, u32[]{:S(2)}) collective-permute-start(bf16[5,128,128]{2,1,0:T(8,128)(2,1)} %bitcast.5), channel_id=1, source_target_pairs={{0,16},{8,24},{16,0},{24,8},{1,17},{9,25},{17,1},{25,9},{2,18},{10... | collective-permute-start | bytes 491528 | tf_op jit(solution)/shard_map/ppermute | solution.py:728
  5.1 0.6 %collective-permute-start = (bf16[5,128,128]{2,1,0:T(8,128)(2,1)}, bf16[5,128,128]{2,1,0:T(8,128)(2,1)S(1)}, u32[]{:S(2)}, u32[]{:S(2)}) collective-permute-start(bf16[5,128,128]{2,1,0:T(8,128)(2,1)} %bitcast.6), channel_id=1, source_target_pairs={{0,8},{8,16},{16,24},{24,0},{1,9},{9,17},{17,25},{25,1},{2,10},{10... | collective-permute-start | bytes 491528 | tf_op jit(solution)/shard_map/ppermute | solution.py:728
  5.7 3.3 %prepare.1 = (f32[5,8,128]{2,1,0:T(8,128)S(1)}, f32[5,8,128]{2,1,0:T(8,128)S(1)}, f32[5,128,128]{2,1,0:T(8,128)S(1)}, f32[5,128,128]{2,1,0:T(8,128)S(1)}, bf16[1...) custom-call(s32[96]{0:T(128)} %blade_group.1, ...), custom_call_target="tpu_custom_call" | custom-call | flops 100000000 | bytes 1000000 | tf_op jit(solution)/shard_map/prepare/pallas_call | solution.py:734
  9.0 0.0 copy-start.2
  9.0 0.0 copy-start.1
  9.0 0.0 copy-start
  9.0 0.1 collective-permute-start.5
  9.1 3.7 %collective-permute-start.6 = (bf16[160,128]{1,0:T(8,128)(2,1)S(1)}, bf16[160,128]{1,0:T(8,128)(2,1)S(1)}, u32[]{:S(2)}, u32[]{:S(2)}) collective-permute-start(bf16[160,128]{1,0:T(8,128)(2,1)S(1)} %get-tuple-element.49.sb), channel_id=1, source_target_pairs={{0,7},{1,2},{2,1},{3,4},{4,3},{5,6},{6,5},{7,0},{8,15},{9,10},{10,... | collective-permute-start | bytes 122888 | tf_op jit(solution)/shard_map/ppermute | solution.py:705
  12.8 0.0 collective-permute-done.2.refs_4_
  12.8 1.2 %collective-permute-done.1.refs_3_ = bf16[5,128,128]{2,1,0:T(8,128)(2,1)S(1)} collective-permute-done((bf16[5,128,128]{2,1,0:T(8,128)(2,1)}, bf16[5,128,128]{2,1,0:T(8,128)(2,1)S(1)}, u32[]{:S(2)}, u32[]{:S(2)}) %collective-permute-start.1) | collective-permute-done | bytes 163872 | tf_op jit(solution)/shard_map/ppermute | solution.py:728
  14.0 0.0 collective-permute-done.refs_2_
  14.0 0.0 copy-done.2
  14.0 1.1 %strips.1 = (bf16[160,128]{1,0:T(8,128)(2,1)S(1)}, bf16[160,128]{1,0:T(8,128)(2,1)S(1)}, bf16[5,128,128]{2,1,0:T(8,128)(2,1)S(1)}, bf16[5,128,128]{2,1,0:T(8,128)(2,1)S(1)}, bf16[5,128,128]{2,1,0:T(8,128)(2,1)S(1)}) custom-call(s32[4]{0:T(128)} %copy-done.2, bf16[5,128,128]{2,1,0:T(8,128)(2,1)S(1)} %get-tuple-element.40.refs_1_, ...), custom_call_target="tpu_custom_call" | custom-call | flops 10000000 | bytes 1000000 | tf_op jit(solution)/shard_map/strips/pallas_call | solution.py:734
  15.0 0.1 collective-permute-start.3
  15.1 3.7 %collective-permute-start.4 = (bf16[160,128]{1,0:T(8,128)(2,1)S(1)}, bf16[160,128]{1,0:T(8,128)(2,1)S(1)}, u32[]{:S(2)}, u32[]{:S(2)}) collective-permute-start(bf16[160,128]{1,0:T(8,128)(2,1)S(1)} %get-tuple-element.43.refs_1_), channel_id=1, source_target_pairs={{0,7},{1,2},{2,1},{3,4},{4,3},{5,6},{6,5},{7,0},{8,15},{9,10},{10,... | collective-permute-start | bytes 122888 | tf_op jit(solution)/shard_map/ppermute | solution.py:705
  18.8 0.0 collective-permute-done.5.ra
  18.8 0.0 collective-permute-done.6.rb
  18.8 0.0 copy-done.1
  18.8 0.0 copy-done
  18.8 3.0 %halo_forcing.1 = (f32[16,5,16,128]{3,2,1,0:T(8,128)S(1)}, f32[5,128,128]{2,1,0:T(8,128)S(1)}, bf16[384,128]{1,0:T(8,128)(2,1)S(1)}, f32[4,5,128,128]{3,2,1,0:T(...) custom-call(f32[5,5]{1,0:T(8,128)} %copy-done, ...), custom_call_target="tpu_custom_call" | custom-call | flops 100000000 | bytes 1000000 | tf_op jit(solution)/shard_map/halo_forcing/pallas_call | solution.py:734
  21.8 0.0 collective-permute-done.3.refs_2_
  21.8 0.0 collective-permute-done.4.refs_3_
  21.8 7.3 %first_steps.1 = (f32[5120,128]{1,0:T(8,128)S(1)}, f32[2,4]{1,0:T(2,128)S(1)}, f32[640,128]{1,0:T(8,128)S(1)}) custom-call(f32[5,5]{1,0:T(8,128)} %copy-done, s32[128]{0:T(128)} %copy-done.1, bf16[160,128]{1,0:T(8,128)(2,1)S(1)} %get-tuple-element.42.refs_0_, bf16[160,128]{1,0:T(8,128)(2,1)S(1)} %get-tuple-element.43.refs_1_, ...), custom_call_target="tpu_custom_call" | custom-call | flops 1000000000 | bytes 1000000 | tf_op jit(solution)/shard_map/first_steps/pallas_call | solution.py:734
  29.1 0.0 collective-permute-start.7
  29.1 5.4 %last_step.1 = f32[40,128,128]{2,1,0:T(8,128)} custom-call(f32[5,5]{1,0:T(8,128)} %copy-done, s32[128]{0:T(128)} %copy-done.1, f32[5120,128]{1,0:T(8,128)S(1)} %get-tuple-element.68.mu2, f32[9,128,128]{2,1,0:T(8,128)S(1)} %get-tuple-element.69.coef0, f32[640,128]{1,0:T(8,128)S(1)} %get-tuple-element.70.e2, ...), custom_call_target="tpu_custom_call" | custom-call | flops 1000000000 | bytes 1000000 | tf_op jit(solution)/shard_map/last_step/pallas_call | solution.py:734
  34.5 0.0 collective-permute-done.7
  34.5 1.1 %collective-permute-start.8 = (f32[2,4]{1,0:T(2,128)S(1)}, f32[2,4]{1,0:T(2,128)S(1)}, u32[]{:S(2)}, u32[]{:S(2)}) collective-permute-start(f32[2,4]{1,0:T(2,128)S(1)} %add.9), channel_id=1, source_target_pairs={{0,2},{1,3},{2,0},{3,1},{4,6},{5,7},{6,4},{7,5},{8,10},{9,11},{10,... | collective-permute-start | bytes 104 | tf_op jit(solution)/shard_map/ppermute | solution.py:699
  35.6 2.6 %collective-permute-done.8 = f32[2,4]{1,0:T(2,128)S(1)} collective-permute-done((f32[2,4]{1,0:T(2,128)S(1)}, f32[2,4]{1,0:T(2,128)S(1)}, u32[]{:S(2)}, u32[]{:S(2)}) %collective-permute-start.8) | collective-permute-done | bytes 64 | tf_op jit(solution)/shard_map/ppermute | solution.py:699
  38.2 0.1 collective-permute-start.9
  38.3 1.0 %collective-permute-done.9 = f32[2,4]{1,0:T(2,128)S(1)} collective-permute-done((f32[2,4]{1,0:T(2,128)S(1)}, f32[2,4]{1,0:T(2,128)S(1)}, u32[]{:S(2)}, u32[]{:S(2)}) %collective-permute-start.9) | collective-permute-done | bytes 64 | tf_op jit(solution)/shard_map/ppermute | solution.py:699
  39.3 0.6 %add.11 = f32[2,4]{1,0:T(2,128)} add(f32[2,4]{1,0:T(2,128)S(1)} %add.10, f32[2,4]{1,0:T(2,128)S(1)} %collective-permute-done.9) | non-fusion elementwise | flops 8 | bytes 96 | tf_op jit(solution)/shard_map/add | solution.py:699
  (2 shorter events, 0.0 us)
Async XLA Ops:
  0.6 12.2 %collective-permute-start.2 = (bf16[5,128,128]{2,1,0:T(8,128)(2,1)}, bf16[5,128,128]{2,1,0:T(8,128)(2,1)S(1)}, u32[]{:S(2)}, u32[]{:S(2)}) collective-permute-start(bf16[5,128,128]{2,1,0:T(8,128)(2,1)} %bitcast.4), channel_id=1, source_target_pairs={{0,24},{8,0},{16,8},{24,16},{1,25},{9,1},{17,9},{25,17},{2,26},{10... | collective-permute-start | bytes 491528 | tf_op jit(solution)/shard_map/ppermute | solution.py:728
  4.6 9.4 %collective-permute-start.1 = (bf16[5,128,128]{2,1,0:T(8,128)(2,1)}, bf16[5,128,128]{2,1,0:T(8,128)(2,1)S(1)}, u32[]{:S(2)}, u32[]{:S(2)}) collective-permute-start(bf16[5,128,128]{2,1,0:T(8,128)(2,1)} %bitcast.5), channel_id=1, source_target_pairs={{0,16},{8,24},{16,0},{24,8},{1,17},{9,25},{17,1},{25,9},{2,18},{10... | collective-permute-start | bytes 491528 | tf_op jit(solution)/shard_map/ppermute | solution.py:728
  5.1 8.9 %collective-permute-start = (bf16[5,128,128]{2,1,0:T(8,128)(2,1)}, bf16[5,128,128]{2,1,0:T(8,128)(2,1)S(1)}, u32[]{:S(2)}, u32[]{:S(2)}) collective-permute-start(bf16[5,128,128]{2,1,0:T(8,128)(2,1)} %bitcast.6), channel_id=1, source_target_pairs={{0,8},{8,16},{16,24},{24,0},{1,9},{9,17},{17,25},{25,1},{2,10},{10... | collective-permute-start | bytes 491528 | tf_op jit(solution)/shard_map/ppermute | solution.py:728
  9.0 5.0 %copy-start.2 = (s32[4]{0:T(128)}, s32[4]{0:T(128)S(1)}, u32[]{:S(2)}) copy-start(s32[4]{0:T(128)S(1)} %get-tuple-element.39.refs_0_) | copy-start | bytes 52
  9.0 9.8 %copy-start.1 = (s32[128]{0:T(128)}, s32[128]{0:T(128)S(1)}, u32[]{:S(2)}) copy-start(s32[128]{0:T(128)S(1)} %get-tuple-element.38.inv) | copy-start | bytes 1540
  9.0 9.8 %copy-start = (f32[5,5]{1,0:T(8,128)}, f32[5,5]{1,0:T(8,128)S(1)}, u32[]{:S(2)}) copy-start(f32[5,5]{1,0:T(8,128)S(1)} %get-tuple-element.37.fm) | copy-start | bytes 304
  9.0 9.8 %collective-permute-start.5 = (bf16[160,128]{1,0:T(8,128)(2,1)S(1)}, bf16[160,128]{1,0:T(8,128)(2,1)S(1)}, u32[]{:S(2)}, u32[]{:S(2)}) collective-permute-start(bf16[160,128]{1,0:T(8,128)(2,1)S(1)} %get-tuple-element.48.sa), channel_id=1, source_target_pairs={{0,1},{1,0},{2,3},{3,2},{4,5},{5,4},{6,7},{7,6},{8,9},{9,8},{10,11... | collective-permute-start | bytes 122888 | tf_op jit(solution)/shard_map/ppermute | solution.py:704
  9.1 9.7 %collective-permute-start.6 = (bf16[160,128]{1,0:T(8,128)(2,1)S(1)}, bf16[160,128]{1,0:T(8,128)(2,1)S(1)}, u32[]{:S(2)}, u32[]{:S(2)}) collective-permute-start(bf16[160,128]{1,0:T(8,128)(2,1)S(1)} %get-tuple-element.49.sb), channel_id=1, source_target_pairs={{0,7},{1,2},{2,1},{3,4},{4,3},{5,6},{6,5},{7,0},{8,15},{9,10},{10,... | collective-permute-start | bytes 122888 | tf_op jit(solution)/shard_map/ppermute | solution.py:705
  15.0 6.8 %collective-permute-start.3 = (bf16[160,128]{1,0:T(8,128)(2,1)S(1)}, bf16[160,128]{1,0:T(8,128)(2,1)S(1)}, u32[]{:S(2)}, u32[]{:S(2)}) collective-permute-start(bf16[160,128]{1,0:T(8,128)(2,1)S(1)} %get-tuple-element.42.refs_0_), channel_id=1, source_target_pairs={{0,1},{1,0},{2,3},{3,2},{4,5},{5,4},{6,7},{7,6},{8,9},{9,8},{10,11... | collective-permute-start | bytes 122888 | tf_op jit(solution)/shard_map/ppermute | solution.py:704
  15.1 6.7 %collective-permute-start.4 = (bf16[160,128]{1,0:T(8,128)(2,1)S(1)}, bf16[160,128]{1,0:T(8,128)(2,1)S(1)}, u32[]{:S(2)}, u32[]{:S(2)}) collective-permute-start(bf16[160,128]{1,0:T(8,128)(2,1)S(1)} %get-tuple-element.43.refs_1_), channel_id=1, source_target_pairs={{0,7},{1,2},{2,1},{3,4},{4,3},{5,6},{6,5},{7,0},{8,15},{9,10},{10,... | collective-permute-start | bytes 122888 | tf_op jit(solution)/shard_map/ppermute | solution.py:705
  29.1 5.4 %collective-permute-start.7 = (f32[2,4]{1,0:T(2,128)S(1)}, f32[2,4]{1,0:T(2,128)S(1)}, u32[]{:S(2)}, u32[]{:S(2)}) collective-permute-start(f32[2,4]{1,0:T(2,128)S(1)} %get-tuple-element.71), channel_id=1, source_target_pairs={{0,4},{1,5},{2,6},{3,7},{4,0},{5,1},{6,2},{7,3},{8,12},{9,13},{10,... | collective-permute-start | bytes 104 | tf_op jit(solution)/shard_map/ppermute | solution.py:699
  34.5 3.6 %collective-permute-start.8 = (f32[2,4]{1,0:T(2,128)S(1)}, f32[2,4]{1,0:T(2,128)S(1)}, u32[]{:S(2)}, u32[]{:S(2)}) collective-permute-start(f32[2,4]{1,0:T(2,128)S(1)} %add.9), channel_id=1, source_target_pairs={{0,2},{1,3},{2,0},{3,1},{4,6},{5,7},{6,4},{7,5},{8,10},{9,11},{10,... | collective-permute-start | bytes 104 | tf_op jit(solution)/shard_map/ppermute | solution.py:699
  38.2 1.1 %collective-permute-start.9 = (f32[2,4]{1,0:T(2,128)S(1)}, f32[2,4]{1,0:T(2,128)S(1)}, u32[]{:S(2)}, u32[]{:S(2)}) collective-permute-start(f32[2,4]{1,0:T(2,128)S(1)} %add.10), channel_id=1, source_target_pairs={{0,1},{1,0},{2,3},{3,2},{4,5},{5,4},{6,7},{7,6},{8,9},{9,8},{10,11... | collective-permute-start | bytes 104 | tf_op jit(solution)/shard_map/ppermute | solution.py:699
